TPU v7x, 32 devices: a whole 2x2x4 slice. The times are simulated.
32 devices in a mesh: section: 2 (over x), wide: 16 (over z, y, core).
Axes of the slice: x: 2, y: 2, z: 4, core: 2. Of those that a mesh axis runs over, the one named last changes fastest.
Arguments:
- tokens: bfloat16 [4, 4096, 768], P(None, 'wide'), may hold values from -6 to 6
- cotangent: bfloat16 [4, 4096, 768], P(None, 'wide'), may hold values from -6 to 6
- seg_lengths: int32 [4, 1, 17], replicated, may hold values from 1 to 257, 4096 in all within a row
- w_query: bfloat16 [2, 768, 768], P('section'), may hold values from -0.21875 to 0.21875
- w_key: bfloat16 [2, 768, 768], P('section'), may hold values from -0.21875 to 0.21875
- w_value: bfloat16 [2, 768, 768], P('section'), may hold values from -0.21875 to 0.21875
- w_output: bfloat16 [2, 768, 768], P('section'), may hold values from -0.875 to 0.875
- w_gate: bfloat16 [2, 768, 2048], P('section'), may hold values from -0.21875 to 0.21875
- w_up: bfloat16 [2, 768, 2048], P('section'), may hold values from -0.21875 to 0.21875
- w_down: bfloat16 [2, 2048, 768], P('section'), may hold values from -0.1875 to 0.1875
- gain_attn: float32 [2, 768], P('section'), may hold values from 0.25 to 1.75
- gain_mlp: float32 [2, 768], P('section'), may hold values from 0.25 to 1.75
Outputs:
- block_outputs: bfloat16 [2, 4, 4096, 768], P('section', None, 'wide')
- input_grads: bfloat16 [2, 4, 4096, 768], P('section', None, 'wide')
- grad_query: float32 [2, 768, 768], P('section', 'wide')
- grad_key: float32 [2, 768, 768], P('section', 'wide')
- grad_value: float32 [2, 768, 768], P('section', 'wide')
- grad_output: float32 [2, 768, 768], P('section', 'wide')
- grad_gate: float32 [2, 768, 2048], P('section', 'wide')
- grad_up: float32 [2, 768, 2048], P('section', 'wide')
- grad_down: float32 [2, 2048, 768], P('section', 'wide')
- grad_gain_attn: float32 [2, 768], P('section', 'wide')
- grad_gain_mlp: float32 [2, 768], P('section', 'wide')
Inputs may be any that keep to these rules, and one draw needn't show every extreme that they name: `seg_lengths`: each row's 17 lengths sum to 4096, and the longest is exactly 257.
All inputs are finite; a program needn't handle non-finite values.
Results may differ from a plain program's by a relative error of at most 0.02.
Values may be sent and summed in bfloat16 or wider, within the bound.
A program may use at most 320 MiB of HBM per device.

v0:
```python
import jax
import jax.numpy as jnp
from jax import lax
from jax.sharding import PartitionSpec as P

HEADS = 12


EPS = 1e-05
THETA = 10000.0


def shifted(array, axis, by):
    size = lax.axis_size(axis)
    pairs = [(i, i + by) for i in range(size) if 0 <= i + by < size]
    return lax.ppermute(array, axis, pairs)


def matmul(left, right):
    return jnp.dot(left, right, preferred_element_type=jnp.float32)


def matmul_back(left, right):
    return lax.dot_general(
        left, right, (((1,), (1,)), ((), ())), preferred_element_type=jnp.float32
    )


def outer_sum(left, right):
    return lax.dot_general(
        left, right, (((0,), (0,)), ((), ())), preferred_element_type=jnp.float32
    )


def rms_parts(hidden):
    inverse = lax.rsqrt(jnp.mean(hidden * hidden, axis=1, keepdims=True) + EPS)
    return (hidden * inverse, inverse)


def rms_back(upstream, scaled, inverse):
    return inverse * (upstream - scaled * jnp.mean(upstream * scaled, axis=1, keepdims=True))


def rotate(field, offsets, direction):
    head_dim = field.shape[1] // HEADS
    half_dim = head_dim // 2
    freqs = THETA ** (-jnp.arange(half_dim, dtype=jnp.float32) * 2.0 / head_dim)
    angles = offsets[:, None] * freqs[None, :]
    cosine = jnp.cos(angles)[:, None, :]
    sine_part = direction * jnp.sin(angles)[:, None, :]
    shaped = field.reshape(field.shape[0], HEADS, 2, half_dim)
    first = shaped[:, :, 0, :]
    second = shaped[:, :, 1, :]
    turned = jnp.stack(
        [first * cosine - second * sine_part, second * cosine + first * sine_part], axis=2
    )
    return turned.reshape(field.shape)


def seg_info(lengths_batch, positions, row_len):
    starts = jnp.cumsum(lengths_batch, axis=1) - lengths_batch
    rows_count = lengths_batch.shape[0]
    row_index = jnp.clip(positions // row_len, 0, rows_count - 1)
    within = positions - row_index * row_len
    start_table = jnp.take(starts, row_index, axis=0)
    counted = jnp.sum((start_table <= within[:, None]).astype(jnp.int32), axis=1) - 1
    picked = jnp.sum(
        jnp.where(jnp.arange(start_table.shape[1])[None, :] == counted[:, None], start_table, 0),
        axis=1,
    )
    seg_ids = jnp.where(positions >= 0, row_index * start_table.shape[1] + counted, -1)
    return (seg_ids, (within - picked).astype(jnp.float32))


def store(buffer, batch_index, value, live_tick):
    previous = lax.dynamic_index_in_dim(buffer, batch_index, 0, False)
    return lax.dynamic_update_index_in_dim(
        buffer, jnp.where(live_tick, value, previous), batch_index, 0
    )


def neighbour_rows(key_b, value_b):
    return shifted(jnp.stack([key_b, value_b]), "wide", 1)


def attend(queries, key_rows, value_rows, allowed):
    rows_n = queries.shape[0]
    query_heads = queries.reshape(rows_n, HEADS, -1)
    key_heads = key_rows.reshape(key_rows.shape[0], HEADS, -1)
    value_heads = value_rows.reshape(value_rows.shape[0], HEADS, -1)
    score_scale = query_heads.shape[2] ** (-0.5)
    scores = (
        jnp.einsum("qhd,khd->hqk", query_heads, key_heads, preferred_element_type=jnp.float32)
        * score_scale
    )
    masked = jnp.where(allowed[None], scores, -1e30)
    row_peak = jnp.max(masked, axis=2, keepdims=True)
    raw_weights = jnp.exp(masked - row_peak)
    probs = raw_weights / jnp.sum(raw_weights, axis=2, keepdims=True)
    probs_b = probs.astype(jnp.bfloat16)
    attended = jnp.einsum("hqk,khd->qhd", probs_b, value_heads, preferred_element_type=jnp.float32)
    return (attended.reshape(rows_n, -1), probs, probs_b)


def forward_layer(inputs_b, params, offsets, allowed, fetch):
    w_query, w_key, w_value, w_output, w_gate, w_up, w_down, gain_attn, gain_mlp = params
    hidden = inputs_b.astype(jnp.float32)
    rms_one, inv_one = rms_parts(hidden)
    normed = (rms_one * gain_attn).astype(jnp.bfloat16)
    queries = rotate(matmul(normed, w_query), offsets, 1.0).astype(jnp.bfloat16)
    key_b = rotate(matmul(normed, w_key), offsets, 1.0).astype(jnp.bfloat16)
    value_b = matmul(normed, w_value).astype(jnp.bfloat16)
    halo_pair = fetch(key_b, value_b)
    key_rows = jnp.concatenate([halo_pair[0], key_b], axis=0)
    value_rows = jnp.concatenate([halo_pair[1], value_b], axis=0)
    attended, probs, probs_b = attend(queries, key_rows, value_rows, allowed)
    attended_b = attended.astype(jnp.bfloat16)
    mixed = hidden + matmul(attended_b, w_output)
    rms_two, inv_two = rms_parts(mixed)
    normed_two = (rms_two * gain_mlp).astype(jnp.bfloat16)
    gate = matmul(normed_two, w_gate)
    up_part = matmul(normed_two, w_up)
    product = (jax.nn.silu(gate) * up_part).astype(jnp.bfloat16)
    output = mixed + matmul(product, w_down)
    saved = (
        rms_one,
        inv_one,
        normed,
        queries,
        key_rows,
        value_rows,
        probs,
        probs_b,
        attended_b,
        rms_two,
        inv_two,
        normed_two,
        gate,
        up_part,
        product,
        halo_pair,
    )
    return (output, saved)


def backward_layer(grad_b, saved, params, offsets, allowed):
    w_query, w_key, w_value, w_output, w_gate, w_up, w_down, gain_attn, gain_mlp = params
    (
        rms_one,
        inv_one,
        normed,
        queries,
        key_rows,
        value_rows,
        probs,
        probs_b,
        attended_b,
        rms_two,
        inv_two,
        normed_two,
        gate,
        up_part,
        product,
        halo_pair,
    ) = saved
    grad_f = grad_b.astype(jnp.float32)
    grad_down_w = outer_sum(product, grad_b)
    d_product = matmul_back(grad_b, w_down)
    sigma = jax.nn.sigmoid(gate)
    d_gate_b = (d_product * up_part * (sigma * (1.0 + gate * (1.0 - sigma)))).astype(jnp.bfloat16)
    d_up_b = (d_product * (gate * sigma)).astype(jnp.bfloat16)
    grad_gate_w = outer_sum(normed_two, d_gate_b)
    grad_up_w = outer_sum(normed_two, d_up_b)
    d_normed_two = matmul_back(d_gate_b, w_gate) + matmul_back(d_up_b, w_up)
    grad_gain_two = jnp.sum(d_normed_two * rms_two, axis=0)
    d_mixed = grad_f + rms_back(d_normed_two * gain_mlp, rms_two, inv_two)
    d_branch = d_mixed.astype(jnp.bfloat16)
    grad_output_w = outer_sum(attended_b, d_branch)
    d_attended = matmul_back(d_branch, w_output).astype(jnp.bfloat16)
    rows_n = queries.shape[0]
    query_heads = queries.reshape(rows_n, HEADS, -1)
    key_heads = key_rows.reshape(2 * rows_n, HEADS, -1)
    value_heads = value_rows.reshape(2 * rows_n, HEADS, -1)
    attended_heads = d_attended.reshape(rows_n, HEADS, -1)
    score_scale = query_heads.shape[2] ** (-0.5)
    d_probs = jnp.einsum(
        "qhd,khd->hqk", attended_heads, value_heads, preferred_element_type=jnp.float32
    )
    centre = jnp.sum(probs * d_probs, axis=2, keepdims=True)
    d_scores = jnp.where(allowed[None], probs * (d_probs - centre), 0.0).astype(jnp.bfloat16)
    d_queries = score_scale * jnp.einsum(
        "hqk,khd->qhd", d_scores, key_heads, preferred_element_type=jnp.float32
    )
    d_keys = score_scale * jnp.einsum(
        "hqk,qhd->khd", d_scores, query_heads, preferred_element_type=jnp.float32
    )
    d_values = jnp.einsum(
        "hqk,qhd->khd", probs_b, attended_heads, preferred_element_type=jnp.float32
    )
    d_keys = d_keys.reshape(2 * rows_n, -1)
    d_values = d_values.reshape(2 * rows_n, -1)
    returned = shifted(
        jnp.stack([d_keys[:rows_n], d_values[:rows_n]]).astype(jnp.bfloat16), "wide", -1
    ).astype(jnp.float32)
    d_key_own = d_keys[rows_n:] + returned[0]
    d_value_own = d_values[rows_n:] + returned[1]
    d_query_b = rotate(d_queries.reshape(rows_n, -1), offsets, -1.0).astype(jnp.bfloat16)
    d_key_b = rotate(d_key_own, offsets, -1.0).astype(jnp.bfloat16)
    d_value_b = d_value_own.astype(jnp.bfloat16)
    grad_query_w = outer_sum(normed, d_query_b)
    grad_key_w = outer_sum(normed, d_key_b)
    grad_value_w = outer_sum(normed, d_value_b)
    d_normed = (
        matmul_back(d_query_b, w_query)
        + matmul_back(d_key_b, w_key)
        + matmul_back(d_value_b, w_value)
    )
    grad_gain_one = jnp.sum(d_normed * rms_one, axis=0)
    d_hidden = d_mixed + rms_back(d_normed * gain_attn, rms_one, inv_one)
    grads = (
        grad_query_w,
        grad_key_w,
        grad_value_w,
        grad_output_w,
        grad_gate_w,
        grad_up_w,
        grad_down_w,
        grad_gain_one,
        grad_gain_two,
    )
    return (d_hidden, grads)


def per_device(
    tokens,
    cotangent,
    seg_lengths,
    w_query,
    w_key,
    w_value,
    w_output,
    w_gate,
    w_up,
    w_down,
    gain_attn,
    gain_mlp,
):
    params = tuple(
        (
            w[0]
            for w in (w_query, w_key, w_value, w_output, w_gate, w_up, w_down, gain_attn, gain_mlp)
        )
    )
    sections = lax.axis_size("section")
    section_id = lax.axis_index("section")
    batch_count = tokens.shape[0]
    tok_rows = tokens.shape[1]
    model_width = tokens.shape[2]
    row_len = tok_rows * lax.axis_size("wide") // seg_lengths.shape[1]
    start_row = lax.axis_index("wide") * tok_rows
    own_pos = start_row + jnp.arange(tok_rows, dtype=jnp.int32)
    halo_pos = own_pos - tok_rows
    key_pos = jnp.concatenate([halo_pos, own_pos])
    tick_count = batch_count + sections - 1

    def context(batch_index):
        lengths_batch = lax.dynamic_index_in_dim(seg_lengths, batch_index, 0, False)
        own_ids, own_offsets = seg_info(lengths_batch, own_pos, row_len)
        halo_ids, halo_offsets = seg_info(lengths_batch, halo_pos, row_len)
        key_ids = jnp.concatenate([halo_ids, own_ids])
        allowed = (
            (key_ids[None, :] == own_ids[:, None])
            & (key_pos[None, :] <= own_pos[:, None])
            & (key_ids[None, :] >= 0)
        )
        return (own_offsets, allowed)

    empty_rows = jnp.zeros((tok_rows, model_width), jnp.bfloat16)
    received = empty_rows
    kept_inputs = jnp.zeros_like(tokens)
    block_out = jnp.zeros_like(tokens)
    for tick in range(tick_count):
        batch_raw = tick - section_id
        live_tick = (batch_raw >= 0) & (batch_raw < batch_count)
        batch_index = jnp.clip(batch_raw, 0, batch_count - 1)
        inputs_b = jnp.where(
            section_id == 0, lax.dynamic_index_in_dim(tokens, batch_index, 0, False), received
        )
        offsets, allowed = context(batch_index)
        output, saved = forward_layer(inputs_b, params, offsets, allowed, neighbour_rows)
        output_b = output.astype(jnp.bfloat16)
        kept_inputs = store(kept_inputs, batch_index, inputs_b, live_tick)
        block_out = store(block_out, batch_index, output_b, live_tick)
        received = shifted(output_b, "section", 1)
    grad_received = empty_rows
    input_grads = jnp.zeros_like(tokens)
    totals = tuple((jnp.zeros(p.shape, jnp.float32) for p in params))
    shares = None
    for tick in range(tick_count):
        batch_raw = tick - (sections - 1 - section_id)
        live_tick = (batch_raw >= 0) & (batch_raw < batch_count)
        batch_index = jnp.clip(batch_raw, 0, batch_count - 1)
        grad_b = jnp.where(
            section_id == sections - 1,
            lax.dynamic_index_in_dim(cotangent, batch_index, 0, False),
            grad_received,
        )
        inputs_b = lax.dynamic_index_in_dim(kept_inputs, batch_index, 0, False)
        offsets, allowed = context(batch_index)
        output, saved = forward_layer(inputs_b, params, offsets, allowed, neighbour_rows)
        d_hidden, grads = backward_layer(grad_b, saved, params, offsets, allowed)
        d_hidden_b = d_hidden.astype(jnp.bfloat16)
        input_grads = store(input_grads, batch_index, d_hidden_b, live_tick)
        live_scale = live_tick.astype(jnp.float32)
        grads = tuple((g * live_scale for g in grads))
        totals = tuple((left_sum + right_sum for left_sum, right_sum in zip(totals, grads)))
        grad_received = shifted(d_hidden_b, "section", -1)
    shares = (
        lax.psum_scatter(totals[0][None], "wide", scatter_dimension=1, tiled=True),
        lax.psum_scatter(totals[1][None], "wide", scatter_dimension=1, tiled=True),
        lax.psum_scatter(totals[2][None], "wide", scatter_dimension=1, tiled=True),
        lax.psum_scatter(totals[3][None], "wide", scatter_dimension=1, tiled=True),
        lax.psum_scatter(totals[4][None], "wide", scatter_dimension=1, tiled=True),
        lax.psum_scatter(totals[5][None], "wide", scatter_dimension=1, tiled=True),
        lax.psum_scatter(totals[6][None], "wide", scatter_dimension=1, tiled=True),
        lax.psum_scatter(totals[7][None], "wide", scatter_dimension=1, tiled=True),
        lax.psum_scatter(totals[8][None], "wide", scatter_dimension=1, tiled=True),
    )
    return (
        block_out[None],
        input_grads[None],
        shares[0],
        shares[1],
        shares[2],
        shares[3],
        shares[4],
        shares[5],
        shares[6],
        shares[7],
        shares[8],
    )


def solution(mesh):
    in_specs = (
        P(None, "wide", None),
        P(None, "wide", None),
        P(),
        P("section", None, None),
        P("section", None, None),
        P("section", None, None),
        P("section", None, None),
        P("section", None, None),
        P("section", None, None),
        P("section", None, None),
        P("section", None),
        P("section", None),
    )
    out_specs = (
        P("section", None, "wide", None),
        P("section", None, "wide", None),
        P("section", "wide", None),
        P("section", "wide", None),
        P("section", "wide", None),
        P("section", "wide", None),
        P("section", "wide", None),
        P("section", "wide", None),
        P("section", "wide", None),
        P("section", "wide"),
        P("section", "wide"),
    )
    return jax.shard_map(
        per_device, mesh=mesh, in_specs=in_specs, out_specs=out_specs, check_vma=False
    )
```

profile of v0, /device:TPU:0, one launch (start us, length us, event | category | flops | bytes accessed | tf_op | source)
XLA Modules:
  0.0 1575.7 jit_solution(16284539118089237124)
XLA Ops:
  76.0 6.0 bitcast_dynamic-update-slice_fusion.11
  82.0 5.2 collective-permute-start.1
  92.0 4.2 collective-permute-done.1
  133.6 6.0 bitcast_dynamic-update-slice_fusion.10
  139.6 5.3 collective-permute-start.3
  148.4 5.1 collective-permute-done.3
  191.0 6.0 bitcast_dynamic-update-slice_fusion.9
  197.0 5.3 collective-permute-start.5
  219.6 4.1 collective-permute-start.6
  248.7 6.0 bitcast_dynamic-update-slice_fusion.8
  254.7 4.2 collective-permute-start.7
  276.6 5.7 collective-permute-start.9
  294.5 6.7 fusion.886
  301.2 4.1 fusion.325
  322.8 4.9 fusion.563
  327.7 4.8 fusion.240
  332.4 26.6 %multiply_bitcast_fusion.4 = f32[512,12,64]{0,2,1:T(8,128)} fusion(bf16[256,12,64]{0,2,1:T(8,128)(2,1)S(1)} %bitcast.1286, f32[12,256,512]{2,1,0:T(8,128)} %fusion.563, pred[256,512]{1,0:T(8,128)(4,1)} %get-tuple-element.210, f32[12,256,512]{2,1,0:T(8,128)} %get-tuple-element.322, f32[12,256]{1,0:T(8,128)} %get-tuple-element.321), kind=kOutput, calls=%fused_computation.267 | convolution fusion | flops 212733440 | bytes 14692352 | tf_op jit(solution)/shard_map/hqk,qhd->khd/dot_general | solution.py:194
  364.0 22.5 %fusion.265 = f32[12,64,256]{2,1,0:T(8,128)} fusion(f32[12,256,512]{2,1,0:T(8,128)} %fusion.563, pred[256,512]{1,0:T(8,128)(4,1)} %get-tuple-element.210, bf16[256,12,64]{0,2,1:T(8,128)(2,1)S(1)} %bitcast.1226, bf16[256,12,64]{0,2,1:T(8,128)(2,1)} %bitcast.1284, f32[12,256,512]{2,1,0:T(8,128)} %get-tuple-element.322, f32[12,256]{1,0:T(8,128)} %get-tuple-element.321), kind=kOutput, calls=%fused_computation.297 | convolution fusion | flops 214109696 | bytes 14299136 | tf_op jit(solution)/shard_map/hqk,khd->qhd/dot_general | solution.py:191
  430.9 8.9 collective-permute-start.12
  445.1 4.4 collective-permute-start.21
  462.4 4.3 collective-permute-start.18
  494.7 6.8 fusion.888
  501.5 4.9 fusion.328
  506.4 6.7 fusion.887
  513.1 4.1 fusion.337
  526.9 6.8 fusion.889
  533.6 4.2 fusion.331
  546.2 6.9 fusion.890
  553.1 4.1 fusion.334
  574.7 5.1 fusion.562
  579.8 4.7 fusion.243
  584.5 23.3 %multiply_bitcast_fusion.3 = f32[512,12,64]{0,2,1:T(8,128)} fusion(bf16[256,12,64]{0,2,1:T(8,128)(2,1)} %bitcast.1279, f32[12,256,512]{2,1,0:T(8,128)} %fusion.562, pred[256,512]{1,0:T(8,128)(4,1)} %get-tuple-element.209, f32[12,256,512]{2,1,0:T(8,128)} %get-tuple-element.333, f32[12,256]{1,0:T(8,128)} %get-tuple-element.332), kind=kOutput, calls=%fused_computation.262 | convolution fusion | flops 212733440 | bytes 14692352 | tf_op jit(solution)/shard_map/hqk,qhd->khd/dot_general | solution.py:194
  614.2 22.6 %fusion.268 = f32[12,64,256]{2,1,0:T(8,128)} fusion(f32[12,256,512]{2,1,0:T(8,128)} %fusion.562, pred[256,512]{1,0:T(8,128)(4,1)} %get-tuple-element.209, bf16[256,12,64]{0,2,1:T(8,128)(2,1)} %bitcast.1223, bf16[256,12,64]{0,2,1:T(8,128)(2,1)} %bitcast.1281, f32[12,256,512]{2,1,0:T(8,128)} %get-tuple-element.333, f32[12,256]{1,0:T(8,128)} %get-tuple-element.332), kind=kOutput, calls=%fused_computation.298 | convolution fusion | flops 214109696 | bytes 14299136 | tf_op jit(solution)/shard_map/hqk,khd->qhd/dot_general | solution.py:191
  651.0 9.7 collective-permute-done.14
  672.5 4.9 fusion.561
  677.4 4.7 fusion.246
  682.2 23.3 %multiply_bitcast_fusion.2 = f32[512,12,64]{0,2,1:T(8,128)} fusion(bf16[256,12,64]{0,2,1:T(8,128)(2,1)} %bitcast.1275, f32[12,256,512]{2,1,0:T(8,128)} %fusion.561, pred[256,512]{1,0:T(8,128)(4,1)} %get-tuple-element.208, f32[12,256,512]{2,1,0:T(8,128)} %get-tuple-element.337, f32[12,256]{1,0:T(8,128)} %get-tuple-element.336), kind=kOutput, calls=%fused_computation.257 | convolution fusion | flops 212733440 | bytes 14692352 | tf_op jit(solution)/shard_map/hqk,qhd->khd/dot_general | solution.py:194
  715.5 22.6 %fusion.271 = f32[12,64,256]{2,1,0:T(8,128)} fusion(f32[12,256,512]{2,1,0:T(8,128)} %fusion.561, pred[256,512]{1,0:T(8,128)(4,1)} %get-tuple-element.208, bf16[256,12,64]{0,2,1:T(8,128)(2,1)} %bitcast.1220, bf16[256,12,64]{0,2,1:T(8,128)(2,1)} %bitcast.1277, f32[12,256,512]{2,1,0:T(8,128)} %get-tuple-element.337, f32[12,256]{1,0:T(8,128)} %get-tuple-element.336), kind=kOutput, calls=%fused_computation.299 | convolution fusion | flops 214109696 | bytes 14299136 | tf_op jit(solution)/shard_map/hqk,khd->qhd/dot_general | solution.py:191
  752.1 9.4 collective-permute-done.17
  773.4 4.9 fusion.560
  778.2 4.7 fusion.249
  783.0 23.3 %multiply_bitcast_fusion.1 = f32[512,12,64]{0,2,1:T(8,128)} fusion(bf16[256,12,64]{0,2,1:T(8,128)(2,1)} %bitcast.1271, f32[12,256,512]{2,1,0:T(8,128)} %fusion.560, pred[256,512]{1,0:T(8,128)(4,1)} %get-tuple-element.207, f32[12,256,512]{2,1,0:T(8,128)} %get-tuple-element.341, f32[12,256]{1,0:T(8,128)} %get-tuple-element.340), kind=kOutput, calls=%fused_computation.252 | convolution fusion | flops 212733440 | bytes 14692352 | tf_op jit(solution)/shard_map/hqk,qhd->khd/dot_general | solution.py:194
  818.9 22.6 %fusion.274 = f32[12,64,256]{2,1,0:T(8,128)} fusion(f32[12,256,512]{2,1,0:T(8,128)} %fusion.560, pred[256,512]{1,0:T(8,128)(4,1)} %get-tuple-element.207, bf16[256,12,64]{0,2,1:T(8,128)(2,1)} %bitcast.1217, bf16[256,12,64]{0,2,1:T(8,128)(2,1)} %bitcast.1273, f32[12,256,512]{2,1,0:T(8,128)} %get-tuple-element.341, f32[12,256]{1,0:T(8,128)} %get-tuple-element.340), kind=kOutput, calls=%fused_computation.300 | convolution fusion | flops 214109696 | bytes 14299136 | tf_op jit(solution)/shard_map/hqk,khd->qhd/dot_general | solution.py:191
  856.7 8.4 collective-permute-done.20
  878.0 5.0 fusion.559
  883.0 4.7 fusion.252
  887.7 23.3 %multiply_bitcast_fusion = f32[512,12,64]{0,2,1:T(8,128)} fusion(bf16[256,12,64]{0,2,1:T(8,128)(2,1)} %bitcast.1267, f32[12,256,512]{2,1,0:T(8,128)} %fusion.559, pred[256,512]{1,0:T(8,128)(4,1)} %get-tuple-element.206, f32[12,256,512]{2,1,0:T(8,128)} %get-tuple-element.329, f32[12,256]{1,0:T(8,128)} %get-tuple-element.328), kind=kOutput, calls=%fused_computation.247 | convolution fusion | flops 212733440 | bytes 14692352 | tf_op jit(solution)/shard_map/hqk,qhd->khd/dot_general | solution.py:194
  919.2 22.6 %fusion.277 = f32[12,64,256]{2,1,0:T(8,128)} fusion(f32[12,256,512]{2,1,0:T(8,128)} %fusion.559, pred[256,512]{1,0:T(8,128)(4,1)} %get-tuple-element.206, bf16[256,12,64]{0,2,1:T(8,128)(2,1)} %bitcast.1214, bf16[256,12,64]{0,2,1:T(8,128)(2,1)} %bitcast.1269, f32[12,256,512]{2,1,0:T(8,128)} %get-tuple-element.329, f32[12,256]{1,0:T(8,128)} %get-tuple-element.328), kind=kOutput, calls=%fused_computation.301 | convolution fusion | flops 214109696 | bytes 14299136 | tf_op jit(solution)/shard_map/hqk,khd->qhd/dot_general | solution.py:191
  951.1 6.4 add_bitcast_fusion.3
  997.8 6.5 add_bitcast_fusion.2
  1013.4 6.6 add_bitcast_fusion.1
  1020.1 3.9 fusion.399
  1024.1 4.0 fusion.400
  1028.1 4.1 fusion.401
  1032.3 4.0 fusion.402
  1036.4 10.9 add_bitcast_fusion
  1056.9 4.2 collective-permute-start.8
  1084.3 5.8 fusion.396
  1101.6 66.7 %reduce-scatter.14.cloned.1.call-done = f32[1,48,768]{2,1,0:T(8,128)} async-done(((f32[1,768,768]{2,1,0:T(8,128)}), f32[1,48,768]{2,1,0:T(8,128)}) %reduce-scatter.14.cloned.1.call-update) | async-done | bytes 147472 | tf_op jit(solution)/shard_map/reduce_scatter | solution.py:319
  1168.3 66.2 %reduce-scatter.16.cloned.1.call-done = f32[1,48,768]{2,1,0:T(8,128)} async-done(((f32[1,768,768]{2,1,0:T(8,128)}), f32[1,48,768]{2,1,0:T(8,128)}) %reduce-scatter.16.cloned.1.call-update) | async-done | bytes 147472 | tf_op jit(solution)/shard_map/reduce_scatter | solution.py:320
  1234.5 66.7 %reduce-scatter.18.cloned.1.call-done = f32[1,48,768]{2,1,0:T(8,128)} async-done(((f32[1,768,768]{2,1,0:T(8,128)}), f32[1,48,768]{2,1,0:T(8,128)}) %reduce-scatter.18.cloned.1.call-update) | async-done | bytes 147472 | tf_op jit(solution)/shard_map/reduce_scatter | solution.py:321
  1301.2 88.8 %reduce-scatter.22.cloned.1.call-done = f32[1,48,2048]{2,1,0:T(8,128)} async-done(((f32[1,768,2048]{2,1,0:T(8,128)}), f32[1,48,2048]{2,1,0:T(8,128)}) %reduce-scatter.22.cloned.1.call-update) | async-done | bytes 393232 | tf_op jit(solution)/shard_map/reduce_scatter | solution.py:323
  1390.0 89.6 %reduce-scatter.24.cloned.1.call-done = f32[1,48,2048]{2,1,0:T(8,128)} async-done(((f32[1,768,2048]{2,1,0:T(8,128)}), f32[1,48,2048]{2,1,0:T(8,128)}) %reduce-scatter.24.cloned.1.call-update) | async-done | bytes 393232 | tf_op jit(solution)/shard_map/reduce_scatter | solution.py:324
  1479.6 89.1 %reduce-scatter.26.cloned.1.call-done = f32[1,128,768]{2,1,0:T(8,128)} async-done(((f32[1,2048,768]{2,1,0:T(8,128)}), f32[1,128,768]{2,1,0:T(8,128)}) %reduce-scatter.26.cloned.1.call-update) | async-done | bytes 393232 | tf_op jit(solution)/shard_map/reduce_scatter | solution.py:325
  (1116 shorter events, 589.3 us)
Async XLA Ops:
  7.2 68.8 %copy-start = (bf16[1,2048,768]{2,1,0:T(8,128)(2,1)S(1)}, bf16[1,2048,768]{2,1,0:T(8,128)(2,1)}, u32[]{:S(2)}) copy-start(bf16[1,2048,768]{2,1,0:T(8,128)(2,1)} %param.23) | copy-start | bytes 9437188
  7.2 11.9 copy-start.301
  7.2 1085.5 %reduce-scatter.30.cloned.1.call-start = ((), (), s32[]{:S(2)}) async-start(), calls=%async_computation.17 | async-start | bytes 417792
  8.6 12.6 copy-start.302
  12.2 191.3 %copy-start.287 = (s32[256]{0:T(256)}, s32[256]{0:T(256)S(1)}, u32[]{:S(2)}) copy-start(s32[256]{0:T(256)S(1)} %get-tuple-element.255) | copy-start | bytes 3076
  13.4 23.1 %copy-start.288 = (s32[256]{0:T(256)}, s32[256]{0:T(256)S(1)}, u32[]{:S(2)}) copy-start(s32[256]{0:T(256)S(1)} %get-tuple-element.261) | copy-start | bytes 3076
  29.3 28.2 %collective-permute-start = (bf16[2,256,768]{2,1,0:T(8,128)(2,1)}, bf16[2,256,768]{2,1,0:T(8,128)(2,1)}, u32[]{:S(2)}, u32[]{:S(2)}) collective-permute-start(bf16[2,256,768]{2,1,0:T(8,128)(2,1)} %pad_maximum_fusion), channel_id=1, source_target_pairs={{0,1},{1,2},{2,3},{3,4},{4,5},{5,6},{6,7},{7,8},{8,9},{9,10},{10,1... | collective-permute-start | bytes 2359304 | tf_op jit(solution)/shard_map/ppermute | solution.py:16
  82.0 9.4 copy-start.295
  82.0 14.1 collective-permute-start.1
  105.5 10.9 collective-permute-start.2
  139.6 14.0 collective-permute-start.3
  146.1 9.5 copy-start.25
  162.9 10.8 collective-permute-start.4
  197.0 13.3 collective-permute-start.5
  203.6 8.8 copy-start.26
  214.7 9.0 copy-start.289
  219.6 11.8 collective-permute-start.6
  254.7 11.6 collective-permute-start.7
  269.6 154.6 %copy-start.273 = (f32[256]{0:T(256)}, f32[256]{0:T(256)S(1)}, u32[]{:S(2)}) copy-start(f32[256]{0:T(256)S(1)} %add_rsqrt_fusion.9) | copy-start | bytes 3076
  273.6 8.7 copy-start.167
  276.6 12.0 collective-permute-start.9
  362.5 24.0 %collective-permute-start.10 = (bf16[2,256,768]{1,2,0:T(8,128)(2,1)}, bf16[2,256,768]{1,2,0:T(8,128)(2,1)}, u32[]{:S(2)}, u32[]{:S(2)}) collective-permute-start(bf16[2,256,768]{1,2,0:T(8,128)(2,1)} %pad_maximum_fusion.8), channel_id=1, source_target_pairs={{1,0},{2,1},{3,2},{4,3},{5,4},{6,5},{7,6},{8,7},{9,8},{10,9},{11,1... | collective-permute-start | bytes 2359304 | tf_op jit(solution)/shard_map/ppermute | solution.py:16
  426.4 54.6 %collective-permute-start.11 = (bf16[256,768]{1,0:T(8,128)(2,1)}, bf16[256,768]{1,0:T(8,128)(2,1)}, u32[]{:S(2)}, u32[]{:S(2)}) collective-permute-start(bf16[256,768]{1,0:T(8,128)(2,1)} %get-tuple-element.83), channel_id=1, source_target_pairs={{16,0},{17,1},{18,2},{19,3},{20,4},{21,5},{22,6},{23,7},{24,8},{25... | collective-permute-start | bytes 1179656 | tf_op jit(solution)/shard_map/ppermute | solution.py:16
  427.9 14.1 copy-start.166
  428.8 13.1 copy-start.101
  428.8 13.1 copy-start.205
  428.8 13.1 copy-start.236
  430.9 52.0 %collective-permute-start.12 = (bf16[2,256,768]{2,1,0:T(8,128)(2,1)}, bf16[2,256,768]{2,1,0:T(8,128)(2,1)}, u32[]{:S(2)}, u32[]{:S(2)}) collective-permute-start(bf16[2,256,768]{2,1,0:T(8,128)(2,1)} %pad_maximum_fusion.9), channel_id=1, source_target_pairs={{0,1},{1,2},{2,3},{3,4},{4,5},{5,6},{6,7},{7,8},{8,9},{9,10},{10,1... | collective-permute-start | bytes 2359304 | tf_op jit(solution)/shard_map/ppermute | solution.py:16
  442.0 9.6 copy-start.159
  443.0 8.5 copy-start.100
  443.0 8.5 copy-start.209
  443.0 8.5 copy-start.235
  445.1 43.7 %collective-permute-start.21 = (bf16[2,256,768]{2,1,0:T(8,128)(2,1)}, bf16[2,256,768]{2,1,0:T(8,128)(2,1)}, u32[]{:S(2)}, u32[]{:S(2)}) collective-permute-start(bf16[2,256,768]{2,1,0:T(8,128)(2,1)} %pad_maximum_fusion.21), channel_id=1, source_target_pairs={{0,1},{1,2},{2,3},{3,4},{4,5},{5,6},{6,7},{7,8},{8,9},{9,10},{10,1... | collective-permute-start | bytes 2359304 | tf_op jit(solution)/shard_map/ppermute | solution.py:16
  454.7 67.4 %collective-permute-start.15 = (bf16[2,256,768]{2,1,0:T(8,128)(2,1)}, bf16[2,256,768]{2,1,0:T(8,128)(2,1)}, u32[]{:S(2)}, u32[]{:S(2)}) collective-permute-start(bf16[2,256,768]{2,1,0:T(8,128)(2,1)} %pad_maximum_fusion.13), channel_id=1, source_target_pairs={{0,1},{1,2},{2,3},{3,4},{4,5},{5,6},{6,7},{7,8},{8,9},{9,10},{10,1... | collective-permute-start | bytes 2359304 | tf_op jit(solution)/shard_map/ppermute | solution.py:16
  459.3 11.0 copy-start.162
  460.2 8.5 copy-start.195
  460.2 8.5 copy-start.196
  460.2 9.3 copy-start.197
  460.3 9.3 copy-start.198
  462.4 79.0 %collective-permute-start.18 = (bf16[2,256,768]{2,1,0:T(8,128)(2,1)}, bf16[2,256,768]{2,1,0:T(8,128)(2,1)}, u32[]{:S(2)}, u32[]{:S(2)}) collective-permute-start(bf16[2,256,768]{2,1,0:T(8,128)(2,1)} %pad_maximum_fusion.17), channel_id=1, source_target_pairs={{0,1},{1,2},{2,3},{3,4},{4,5},{5,6},{6,7},{7,8},{8,9},{9,10},{10,1... | collective-permute-start | bytes 2359304 | tf_op jit(solution)/shard_map/ppermute | solution.py:16
  473.4 39.7 %copy-start.148 = (bf16[256,768]{0,1:T(8,128)(2,1)}, bf16[256,768]{0,1:T(8,128)(2,1)S(1)}, u32[]{:S(2)}) copy-start(bf16[256,768]{0,1:T(8,128)(2,1)S(1)} %copy.231) | copy-start | bytes 1179652
  538.5 20.5 %copy-start.274 = (f32[256]{0:T(256)}, f32[256]{0:T(256)S(1)}, u32[]{:S(2)}) copy-start(f32[256]{0:T(256)S(1)} %add_rsqrt_fusion) | copy-start | bytes 3076
  611.1 25.7 %collective-permute-start.13 = (bf16[2,256,768]{1,2,0:T(8,128)(2,1)}, bf16[2,256,768]{1,2,0:T(8,128)(2,1)}, u32[]{:S(2)}, u32[]{:S(2)}) collective-permute-start(bf16[2,256,768]{1,2,0:T(8,128)(2,1)} %pad_maximum_fusion.12), channel_id=1, source_target_pairs={{1,0},{2,1},{3,2},{4,3},{5,4},{6,5},{7,6},{8,7},{9,8},{10,9},{11,1... | collective-permute-start | bytes 2359304 | tf_op jit(solution)/shard_map/ppermute | solution.py:16
  646.5 14.1 collective-permute-start.14
  650.0 11.7 copy-start.140
  651.0 12.2 copy-start.142
  708.8 29.2 %collective-permute-start.16 = (bf16[2,256,768]{1,2,0:T(8,128)(2,1)}, bf16[2,256,768]{1,2,0:T(8,128)(2,1)}, u32[]{:S(2)}, u32[]{:S(2)}) collective-permute-start(bf16[2,256,768]{1,2,0:T(8,128)(2,1)} %pad_maximum_fusion.16), channel_id=1, source_target_pairs={{1,0},{2,1},{3,2},{4,3},{5,4},{6,5},{7,6},{8,7},{9,8},{10,9},{11,1... | collective-permute-start | bytes 2359304 | tf_op jit(solution)/shard_map/ppermute | solution.py:16
  747.8 13.7 collective-permute-start.17
  751.1 11.4 copy-start.144
  752.1 11.9 copy-start.146
  809.7 31.8 %collective-permute-start.19 = (bf16[2,256,768]{1,2,0:T(8,128)(2,1)}, bf16[2,256,768]{1,2,0:T(8,128)(2,1)}, u32[]{:S(2)}, u32[]{:S(2)}) collective-permute-start(bf16[2,256,768]{1,2,0:T(8,128)(2,1)} %pad_maximum_fusion.20), channel_id=1, source_target_pairs={{1,0},{2,1},{3,2},{4,3},{5,4},{6,5},{7,6},{8,7},{9,8},{10,9},{11,1... | collective-permute-start | bytes 2359304 | tf_op jit(solution)/shard_map/ppermute | solution.py:16
  851.2 13.9 collective-permute-start.20
  854.8 11.3 copy-start.87
  854.8 11.4 copy-start.89
  914.5 27.4 %collective-permute-start.22 = (bf16[2,256,768]{1,2,0:T(8,128)(2,1)}, bf16[2,256,768]{1,2,0:T(8,128)(2,1)}, u32[]{:S(2)}, u32[]{:S(2)}) collective-permute-start(bf16[2,256,768]{1,2,0:T(8,128)(2,1)} %pad_maximum_fusion.24), channel_id=1, source_target_pairs={{1,0},{2,1},{3,2},{4,3},{5,4},{6,5},{7,6},{8,7},{9,8},{10,9},{11,1... | collective-permute-start | bytes 2359304 | tf_op jit(solution)/shard_map/ppermute | solution.py:16
  918.7 178.0 %reduce-scatter.28.cloned.1.call-start = ((), (), s32[]{:S(2)}) async-start(), calls=%async_computation.16 | async-start | bytes 417792
  951.0 150.6 %reduce-scatter.20.cloned.1.call-start = ((), (), s32[]{:S(2)}) async-start(), calls=%async_computation.12 | async-start | bytes 2506752 | tf_op jit(solution)/shard_map/reduce_scatter | solution.py:322
  957.5 210.8 %reduce-scatter.14.cloned.1.call-start = ((), (), s32[]{:S(2)}) async-start(), calls=%async_computation.9 | async-start | bytes 2506752 | tf_op jit(solution)/shard_map/reduce_scatter | solution.py:319
  968.0 266.5 %reduce-scatter.16.cloned.1.call-start = ((), (), s32[]{:S(2)}) async-start(), calls=%async_computation.10 | async-start | bytes 2506752 | tf_op jit(solution)/shard_map/reduce_scatter | solution.py:320
  978.6 322.6 %reduce-scatter.18.cloned.1.call-start = ((), (), s32[]{:S(2)}) async-start(), calls=%async_computation.11 | async-start | bytes 2506752 | tf_op jit(solution)/shard_map/reduce_scatter | solution.py:321
  989.0 400.9 %reduce-scatter.22.cloned.1.call-start = ((), (), s32[]{:S(2)}) async-start(), calls=%async_computation.13 | async-start | bytes 6684672 | tf_op jit(solution)/shard_map/reduce_scatter | solution.py:323
  1004.4 475.2 %reduce-scatter.24.cloned.1.call-start = ((), (), s32[]{:S(2)}) async-start(), calls=%async_computation.14 | async-start | bytes 6684672 | tf_op jit(solution)/shard_map/reduce_scatter | solution.py:324
  1020.0 548.7 %reduce-scatter.26.cloned.1.call-start = ((), (), s32[]{:S(2)}) async-start(), calls=%async_computation.15 | async-start | bytes 6684672 | tf_op jit(solution)/shard_map/reduce_scatter | solution.py:325
  1056.9 10.2 collective-permute-start.8
  (281 other events, 750.0 us)
Sparse Core Ops, SparseCore 0:
  918.8 53.7 reduce-scatter.29
  976.6 54.6 reduce-scatter.27
  1035.6 66.0 reduce-scatter.19
  1106.3 61.9 reduce-scatter.13
  1172.5 61.9 reduce-scatter.15
  1239.1 62.0 reduce-scatter.17
  1305.7 84.2 reduce-scatter.21
  1395.0 84.5 reduce-scatter.23
  1484.1 84.5 reduce-scatter.25
where the time goes:
time: 1590 us; the launch traced here: 1580 us
  matrix products  642 us (40%)
  waiting for transfers between devices  514 us (32%)
  local copies, waits for them, and re-layouts  181 us (11%)
  other arithmetic  143 us (9%)
  starting transfers between devices  77.9 us (5%)
  between operations  18.5 us (1%)
    dot_general x60, matrix products, matmul(): return jnp.dot(left, right, preferred_element_type=jnp.float32)  134 us
    dot_general x5, matrix products, backward_layer(): jnp.einsum('hqk,qhd->khd', d_scores, query_heads, preferred_element_type=...  120 us
    dot_general x5, matrix products, backward_layer(): jnp.einsum('hqk,khd->qhd', d_scores, key_heads, preferred_element_type=jn...  113 us
    dot_general x35, matrix products, outer_sum(): lax.dot_general(left, right, (((0,), (0,)), ((), ())), preferred_element_...  102 us
    reduce_scatter x1, waiting for transfers between devices, per_device(): lax.psum_scatter(totals[5][None], 'wide', scatter_dimension=1, tiled=True)  89.6 us
    reduce_scatter x1, waiting for transfers between devices, per_device(): lax.psum_scatter(totals[6][None], 'wide', scatter_dimension=1, tiled=True)  89.1 us
    reduce_scatter x1, waiting for transfers between devices, per_device(): lax.psum_scatter(totals[4][None], 'wide', scatter_dimension=1, tiled=True)  88.8 us
    ppermute x23, starting transfers between devices, shifted(): return lax.ppermute(array, axis, pairs)  76.7 us
  transfers between devices with their start and end apart: 32, of which 14 were waited for; matrix products, arithmetic and copies ran while one was open for 28% of the time, Pallas kernels for 0%

commit v1 on v0

v1 whole, which is shorter than its diff:
```python
import functools

import jax
import jax.numpy as jnp
from jax import lax
from jax.experimental import pallas as pl
from jax.experimental.pallas import tpu as pltpu
from jax.sharding import PartitionSpec as P

HEADS = 12
EPS = 1e-05
THETA = 10000.0

F32 = jnp.float32
BF16 = jnp.bfloat16
MESH = pl.DeviceIdType.MESH
LANES = 128
VMEM_BYTES = 60 * 1024 * 1024


def dot(left, right):
    return jnp.dot(left, right, preferred_element_type=F32)


def dot_nt(left, right):
    return lax.dot_general(
        left, right, (((1,), (1,)), ((), ())), preferred_element_type=F32
    )


def rms_parts(hidden):
    inverse = lax.rsqrt(jnp.mean(hidden * hidden, axis=1, keepdims=True) + EPS)
    return (hidden * inverse, inverse)


def rms_back(upstream, scaled, inverse):
    return inverse * (upstream - scaled * jnp.mean(upstream * scaled, axis=1, keepdims=True))


def low_half(rows):
    lane = lax.broadcasted_iota(jnp.int32, (rows, LANES), 1)
    return lane % 64 < 32


def rope(field, cosine, sine, direction):
    partner = jnp.where(
        low_half(field.shape[0]),
        pltpu.roll(field, 96, 1),
        pltpu.roll(field, 32, 1),
    )
    if direction > 0:
        return field * cosine + partner * sine
    return field * cosine - partner * sine


def split_heads(block):
    lane = lax.broadcasted_iota(jnp.int32, block.shape, 1)
    zero = jnp.zeros_like(block)
    return jnp.concatenate(
        [jnp.where(lane < 64, block, zero), jnp.where(lane >= 64, block, zero)], axis=0
    )


def join_heads(turned):
    count = turned.shape[1] // 2
    row = lax.broadcasted_iota(jnp.int32, (LANES, count), 0)
    return jnp.where(row < 64, turned[:, :count], turned[:, count:]).T


def meet(partners):
    barrier = pltpu.get_barrier_semaphore()
    total = 0
    for condition, device in partners:

        @pl.when(condition)
        def _(device=device):
            pl.semaphore_signal(barrier, inc=1, device_id=device, device_id_type=MESH)

        total = total + condition.astype(jnp.int32)
    pl.semaphore_wait(barrier, total)


def forward_kernel(
    tokens, w_query, w_key, w_value, w_output, w_gate, w_up, w_down,
    gain_attn, gain_mlp, cosine, sine, first_key,
    block_out, x_out, normed_out, q_out, k_out, v_out, probs_out, att_out, mixed_out,
    n2_out, slope_out, silu_out, prod_out,
    wq, wk, wv, wo, wg, wu, wd,
    xs, normed, qs, ks, vs, probs, att, mixed, n2, slope, silu, prod, ys, bias,
    weight_sem, token_sem, save_sem, out_sem, halo_send, halo_recv, hand_send, hand_recv,
):
    section, wide = lax.axis_index("section"), lax.axis_index("wide")
    last_section, last_wide = lax.axis_size("section") - 1, lax.axis_size("wide") - 1
    batches, rows, width = tokens.shape
    hidden_width = wg.shape[1]
    half = rows // 2
    pairs = width // LANES
    own = pl.ds(rows, rows)
    has_left, has_right = wide > 0, wide < last_wide
    has_before, has_after = section > 0, section < last_section
    is_first = jnp.logical_not(has_before)

    meet([
        (has_left, {"wide": wide - 1}), (has_right, {"wide": wide + 1}),
        (has_before, {"section": section - 1}), (has_after, {"section": section + 1}),
    ])

    weights = ((w_query, wq), (w_key, wk), (w_value, wv), (w_output, wo),
               (w_gate, wg), (w_up, wu), (w_down, wd))
    def weight_copy(index):
        source, target = weights[index]
        return pltpu.make_async_copy(source.at[0], target, weight_sem.at[index])

    def token_copy(mb):
        return pltpu.make_async_copy(tokens.at[mb], xs.at[mb, own], token_sem.at[mb])

    def halo_copy(mb, source):
        return pltpu.make_async_remote_copy(
            source, xs.at[mb, pl.ds(0, rows)], halo_send.at[mb], halo_recv.at[mb],
            device_id={"wide": wide + 1}, device_id_type=MESH)

    def hand_copy(mb):
        return pltpu.make_async_remote_copy(
            ys.at[mb], xs.at[mb, own], hand_send.at[mb], hand_recv.at[mb],
            device_id={"section": section + 1}, device_id_type=MESH)

    @pl.when(is_first)
    def _():
        for mb in range(batches):
            token_copy(mb).start()

    @pl.when(is_first & has_right)
    def _():
        for mb in range(batches):
            halo_copy(mb, tokens.at[mb]).start()

    for index in range(7):
        weight_copy(index).start()

    @pl.when(jnp.logical_not(has_left))
    def _():
        xs[:, pl.ds(0, rows), :] = jnp.zeros((batches, rows, width), BF16)

    def saves(mb, slot):
        listed = (
            (xs.at[mb, own], x_out), (normed.at[slot], normed_out), (qs.at[slot], q_out),
            (ks.at[slot], k_out), (vs.at[slot], v_out), (probs.at[slot], probs_out),
            (att.at[slot], att_out), (mixed.at[slot], mixed_out), (n2.at[slot], n2_out),
            (slope.at[slot], slope_out), (silu.at[slot], silu_out), (prod.at[slot], prod_out),
        )
        return [
            pltpu.make_async_copy(source, target.at[mb], save_sem.at[index, slot])
            for index, (source, target) in enumerate(listed)
        ]

    def out_copy(mb):
        return pltpu.make_async_copy(ys.at[mb], block_out.at[mb], out_sem.at[mb])

    def first_use(mb, *indices):
        @pl.when(mb == 0)
        def _():
            for index in indices:
                weight_copy(index).wait()

    def keys_values(mb, slot, part):
        at = pl.ds(part * rows, rows)
        cos_rows, sin_rows = cosine[mb, at, :], sine[mb, at, :]
        rows_n = normed[slot, at, :]
        for start in range(0, width, 256):
            keys = dot(rows_n, wk[:, start:start + 256])
            for inner in range(0, 256, LANES):
                ks[slot, at, start + inner:start + inner + LANES] = rope(
                    keys[:, inner:inner + LANES], cos_rows, sin_rows, 1).astype(BF16)
            vs[slot, at, start:start + 256] = dot(rows_n, wv[:, start:start + 256]).astype(BF16)

    def normalise(mb, slot, part):
        at = pl.ds(part * rows, rows)
        scaled, _ = rms_parts(xs[mb, at, :].astype(F32))
        normed[slot, at, :] = (scaled * gain_attn[...]).astype(BF16)

    def step(mb, carry):
        slot = lax.rem(mb, 2)

        @pl.when(is_first)
        def _():
            token_copy(mb).wait()

        @pl.when(has_before)
        def _():
            hand_copy(mb).wait_recv()

        @pl.when(has_before & has_right)
        def _():
            halo_copy(mb, xs.at[mb, own]).start()

        @pl.when(mb >= 2)
        def _():
            for copy in saves(mb - 2, slot):
                copy.wait()

        for block in range(2):
            key_at = lax.broadcasted_iota(jnp.int32, (3 * half, half), 0) + (block * half - rows)
            query_at = lax.broadcasted_iota(jnp.int32, (3 * half, half), 1) + block * half
            first = first_key[mb, :, block * half:(block + 1) * half]
            seen = (key_at >= first) & (key_at <= query_at)
            bias[block] = jnp.where(seen, 0.0, -1e30)

        normalise(mb, slot, 1)
        first_use(mb, 0, 1, 2)
        cos_rows, sin_rows = cosine[mb, own, :], sine[mb, own, :]
        rows_n = normed[slot, own, :]
        for start in range(0, width, 256):
            queries = dot(rows_n, wq[:, start:start + 256])
            for inner in range(0, 256, LANES):
                turned = rope(queries[:, inner:inner + LANES], cos_rows, sin_rows, 1)
                qs[slot, :, start + inner:start + inner + LANES] = (
                    turned.astype(BF16) * jnp.asarray(0.125, BF16))
        keys_values(mb, slot, 1)

        @pl.when(has_left)
        def _():
            halo_copy(mb, xs.at[mb, own]).wait_recv()

        normalise(mb, slot, 0)
        keys_values(mb, slot, 0)

        def attend(pair, carry):
            lanes = pl.ds(pl.multiple_of(pair * LANES, LANES), LANES)
            key_pair = ks[slot, :, lanes]
            value_turned = vs[slot, :, lanes].T
            for block in range(2):
                queries = split_heads(qs[slot, block * half:(block + 1) * half, lanes])
                low = block * half
                scores = dot_nt(key_pair[low:low + 3 * half, :], queries)
                hidden = bias[block]
                scores = scores + jnp.concatenate([hidden, hidden], axis=1)
                peak = jnp.max(scores, axis=0, keepdims=True)
                raw = jnp.exp(scores - peak)
                scale = 1.0 / jnp.sum(raw, axis=0, keepdims=True)
                probs_b = (raw * scale).astype(BF16)
                probs[slot, pair, block] = probs_b
                turned = dot(value_turned[:, low:low + 3 * half], probs_b)
                att[slot, block * half:(block + 1) * half, lanes] = join_heads(turned).astype(BF16)
            return carry

        lax.fori_loop(0, pairs, attend, 0)

        first_use(mb, 3)
        rows_a = att[slot]
        for start in range(0, width, 256):
            at = slice(start, start + 256)
            mixed[slot, :, at] = xs[mb, own, at].astype(F32) + dot(rows_a, wo[:, at])
        scaled, _ = rms_parts(mixed[slot])
        n2[slot] = (scaled * gain_mlp[...]).astype(BF16)
        first_use(mb, 4, 5)
        rows_n = n2[slot]
        for start in range(0, hidden_width, 256):
            at = slice(start, start + 256)
            gate = dot(rows_n, wg[:, at])
            up = dot(rows_n, wu[:, at])
            sigma = jax.nn.sigmoid(gate)
            gated = gate * sigma
            prod[slot, :, at] = (gated * up).astype(BF16)
            silu[slot, :, at] = gated.astype(BF16)
            slope[slot, :, at] = (up * (sigma * (1.0 + gate * (1.0 - sigma)))).astype(BF16)
        first_use(mb, 6)
        rows_p = prod[slot]
        for start in range(0, width, 256):
            at = slice(start, start + 256)
            ys[mb, :, at] = (mixed[slot, :, at] + dot(rows_p, wd[:, at])).astype(BF16)

        @pl.when(has_after)
        def _():
            hand_copy(mb).start()

        out_copy(mb).start()
        for copy in saves(mb, slot):
            copy.start()
        return carry

    lax.fori_loop(0, batches, step, 0)

    for mb in range(batches):
        if mb >= batches - 2:
            for copy in saves(mb, mb % 2):
                copy.wait()
        out_copy(mb).wait()

    @pl.when(has_after)
    def _():
        for mb in range(batches):
            hand_copy(mb).wait_send()

    @pl.when(has_right)
    def _():
        for mb in range(batches):
            halo_copy(mb, xs.at[mb, own]).wait_send()


def any_spec():
    return pl.BlockSpec(memory_space=pl.ANY)


def vmem_spec():
    return pl.BlockSpec(memory_space=pltpu.VMEM)


def run_forward(tokens, weights, gain_attn, gain_mlp, cosine, sine, first_key):
    batches, rows, width = tokens.shape
    hidden_width = weights[4].shape[2]
    pairs = width // LANES
    both = 2 * rows
    one = (batches, rows, width)
    two = (batches, both, width)
    wide = (batches, rows, hidden_width)
    prob = (batches, pairs, 2, 3 * rows // 2, rows)
    saved = [(one, BF16), (one, BF16), (two, BF16), (one, BF16), (two, BF16), (two, BF16), (prob, BF16),
             (one, BF16), (one, F32), (one, BF16), (wide, BF16), (wide, BF16), (wide, BF16)]
    slots = [pltpu.VMEM((2,) + shape[1:], dtype) for shape, dtype in saved[2:]]
    return pl.pallas_call(
        forward_kernel,
        out_shape=[jax.ShapeDtypeStruct(shape, dtype) for shape, dtype in saved],
        in_specs=[any_spec()] * 8 + [vmem_spec()] * 5,
        out_specs=[any_spec()] * len(saved),
        scratch_shapes=[pltpu.VMEM(w.shape[1:], BF16) for w in weights]
        + [pltpu.VMEM(two, BF16)]
        + slots
        + [
            pltpu.VMEM(one, BF16),
            pltpu.VMEM((2, 3 * rows // 2, rows // 2), F32),
            pltpu.SemaphoreType.DMA((7,)),
            pltpu.SemaphoreType.DMA((batches,)),
            pltpu.SemaphoreType.DMA((12, 2)),
            pltpu.SemaphoreType.DMA((batches,)),
            pltpu.SemaphoreType.DMA((batches,)),
            pltpu.SemaphoreType.DMA((batches,)),
            pltpu.SemaphoreType.DMA((batches,)),
            pltpu.SemaphoreType.DMA((batches,)),
        ],
        compiler_params=pltpu.CompilerParams(
            collective_id=1, has_side_effects=True, vmem_limit_bytes=VMEM_BYTES),
        name="forward",
    )(tokens, *weights, gain_attn, gain_mlp, cosine, sine, first_key)


def backward_kernel(
    cotangent, x_in, q_in, k_in, v_in, probs_in, mixed_in, slope_in, silu_in,
    w_query, w_key, w_value, w_output, w_gate, w_up, w_down,
    gain_attn, gain_mlp, cosine, sine,
    grad_out, g_out, db_out, dg_out, du_out, dq_out, dk_out, dv_out, gains_out,
    wq, wk, wv, wo, wg, wu, wd,
    gs, xs, qs, ks, vs, probs, mixed, slope, silu, branch, d_att, d_mixed, d_norm,
    halo_out, halo_in, dxs,
    weight_sem, load_sem, probs_sem, save_sem, grad_sem, cot_sem, halo_send, halo_recv, hand_send, hand_recv,
):
    section, wide = lax.axis_index("section"), lax.axis_index("wide")
    last_section, last_wide = lax.axis_size("section") - 1, lax.axis_size("wide") - 1
    batches, rows, width = cotangent.shape
    hidden_width = wg.shape[1]
    half = rows // 2
    pairs = width // LANES
    own = pl.ds(rows, rows)
    has_left, has_right = wide > 0, wide < last_wide
    has_before, has_after = section > 0, section < last_section
    is_last = jnp.logical_not(has_after)

    meet([
        (has_left, {"wide": wide - 1}), (has_right, {"wide": wide + 1}),
        (has_before, {"section": section - 1}), (has_after, {"section": section + 1}),
    ])

    weights = ((w_query, wq), (w_key, wk), (w_value, wv), (w_output, wo),
               (w_gate, wg), (w_up, wu), (w_down, wd))
    order = (6, 4, 5, 3, 0, 1, 2)

    def weight_copy(index):
        source, target = weights[index]
        return pltpu.make_async_copy(source.at[0], target, weight_sem.at[index])

    def cot_copy(mb):
        return pltpu.make_async_copy(cotangent.at[mb], gs.at[mb], cot_sem.at[mb])

    loaded = ((slope_in, slope), (silu_in, silu), (mixed_in, mixed), (q_in, qs), (k_in, ks), (v_in, vs), (x_in, xs))

    def load_copy(index, mb):
        source, target = loaded[index]
        return pltpu.make_async_copy(source.at[mb], target.at[mb], load_sem.at[index, mb])

    def probs_copy(mb):
        slot = lax.rem(mb, 2)
        return pltpu.make_async_copy(probs_in.at[mb], probs.at[slot], probs_sem.at[slot])

    def halo_copy(mb):
        return pltpu.make_async_remote_copy(
            halo_out.at[mb], halo_in.at[mb], halo_send.at[mb], halo_recv.at[mb],
            device_id={"wide": wide - 1}, device_id_type=MESH)

    def hand_copy(mb):
        return pltpu.make_async_remote_copy(
            dxs.at[mb], gs.at[mb], hand_send.at[mb], hand_recv.at[mb],
            device_id={"section": section - 1}, device_id_type=MESH)

    def saves(mb):
        listed = ((gs, g_out), (branch, db_out), (slope, dg_out), (silu, du_out), (qs, dq_out), (ks, dk_out), (vs, dv_out))
        return [
            pltpu.make_async_copy(source.at[mb], target.at[mb], save_sem.at[index, mb])
            for index, (source, target) in enumerate(listed)
        ]

    def grad_copy(mb):
        return pltpu.make_async_copy(dxs.at[mb], grad_out.at[mb], grad_sem.at[mb])

    @pl.when(is_last)
    def _():
        for mb in range(batches):
            cot_copy(mb).start()

    weight_copy(6).start()
    load_copy(0, 0).start()
    load_copy(1, 0).start()
    for index in order[1:4]:
        weight_copy(index).start()
    probs_copy(0).start()
    for index in range(2, 7):
        load_copy(index, 0).start()
    for index in order[4:]:
        weight_copy(index).start()
    for mb in range(1, batches):
        for index in range(7):
            load_copy(index, mb).start()

    gains_out[...] = jnp.zeros(gains_out.shape, F32)

    def first_use(mb, *indices):
        @pl.when(mb == 0)
        def _():
            for index in indices:
                weight_copy(index).wait()

    def add_gain(which, product):
        folded = jnp.sum(product.reshape(rows // 8, 8, width), axis=0)
        at = pl.ds(8 * which, 8)
        gains_out[at, :] = gains_out[at, :] + folded

    def step(mb, carry):
        slot = lax.rem(mb, 2)

        @pl.when(mb + 1 < batches)
        def _():
            probs_copy(mb + 1).start()

        @pl.when(is_last)
        def _():
            cot_copy(mb).wait()

        @pl.when(has_after)
        def _():
            hand_copy(mb).wait_recv()

        first_use(mb, 6)
        load_copy(0, mb).wait()
        load_copy(1, mb).wait()
        rows_g = gs[mb]
        for start in range(0, hidden_width, 256):
            at = slice(start, start + 256)
            d_product = dot_nt(rows_g, wd[at, :])
            slope[mb, :, at] = (d_product * slope[mb, :, at].astype(F32)).astype(BF16)
            silu[mb, :, at] = (d_product * silu[mb, :, at].astype(F32)).astype(BF16)
        first_use(mb, 4, 5)
        d_gate, d_up = slope[mb], silu[mb]
        for start in range(0, width, 256):
            at = slice(start, start + 256)
            d_norm[:, at] = dot_nt(d_gate, wg[at, :]) + dot_nt(d_up, wu[at, :])
        load_copy(2, mb).wait()
        scaled, inverse = rms_parts(mixed[mb])
        d_normed = d_norm[...]
        add_gain(1, d_normed * scaled)
        back = rms_back(d_normed * gain_mlp[...], scaled, inverse)
        d_mixed[...] = rows_g.astype(F32) + back
        branch[mb] = d_mixed[...].astype(BF16)
        first_use(mb, 3)
        rows_b = branch[mb]
        for start in range(0, width, 256):
            at = slice(start, start + 256)
            d_att[:, at] = dot_nt(rows_b, wo[at, :]).astype(BF16)

        probs_copy(mb).wait()
        for index in range(3, 7):
            load_copy(index, mb).wait()

        def attend(pair, carry):
            lanes = pl.ds(pl.multiple_of(pair * LANES, LANES), LANES)
            key_pair, value_pair = ks[mb, :, lanes], vs[mb, :, lanes]
            key_turned = key_pair.T
            d_keys, d_values = [], []
            for block in range(2):
                low = block * half
                here = slice(low, low + half)
                band = slice(low, low + 3 * half)
                queries = split_heads(qs[mb, here, lanes])
                d_out = split_heads(d_att[here, lanes])
                probs_b = probs[slot, pair, block]
                weights_f = probs_b.astype(F32)
                d_probs = dot_nt(value_pair[band, :], d_out)
                moved = weights_f * d_probs
                centre = jnp.sum(moved, axis=0, keepdims=True)
                d_scores = (moved - weights_f * centre).astype(BF16)
                d_keys.append(dot(d_scores, queries))
                d_values.append(dot(probs_b, d_out))
                turned = dot(key_turned[:, band], d_scores)
                at = pl.ds(rows + low, half)
                d_query = rope(join_heads(turned) * 0.125, cosine[mb, at, :], sine[mb, at, :], -1)
                qs[mb, here, lanes] = d_query.astype(BF16)

            def overlap(first, second):
                return jnp.concatenate(
                    [first[:half], first[half:] + second[:2 * half], second[2 * half:]], axis=0)

            d_key = rope(overlap(*d_keys), cosine[mb], sine[mb], -1)
            ks[mb, :, lanes] = d_key.astype(BF16)
            vs[mb, :, lanes] = overlap(*d_values).astype(BF16)
            return carry

        lax.fori_loop(0, pairs, attend, 0)

        first_use(mb, 0, 1, 2)
        halo = pl.ds(0, rows)
        d_key, d_value = ks[mb, halo, :], vs[mb, halo, :]
        for start in range(0, width, 256):
            at = slice(start, start + 256)
            part = dot_nt(d_key, wk[at, :]) + dot_nt(d_value, wv[at, :])
            halo_out[mb, :, at] = part.astype(BF16)

        @pl.when(has_left)
        def _():
            halo_copy(mb).start()

        d_query, d_key, d_value = qs[mb], ks[mb, own, :], vs[mb, own, :]
        for start in range(0, width, 256):
            at = slice(start, start + 256)
            d_norm[:, at] = (
                dot_nt(d_query, wq[at, :]) + dot_nt(d_key, wk[at, :]) + dot_nt(d_value, wv[at, :]))
        for copy in saves(mb):
            copy.start()

        @pl.when(has_right)
        def _():
            halo_copy(mb).wait_recv()
            d_norm[...] = d_norm[...] + halo_in[mb].astype(F32)

        scaled, inverse = rms_parts(xs[mb].astype(F32))
        d_normed = d_norm[...]
        add_gain(0, d_normed * scaled)
        back = rms_back(d_normed * gain_attn[...], scaled, inverse)
        dxs[mb] = (d_mixed[...] + back).astype(BF16)

        @pl.when(has_before)
        def _():
            hand_copy(mb).start()

        grad_copy(mb).start()
        return carry

    lax.fori_loop(0, batches, step, 0)

    for mb in range(batches):
        for copy in saves(mb):
            copy.wait()
        grad_copy(mb).wait()

    @pl.when(has_left)
    def _():
        for mb in range(batches):
            halo_copy(mb).wait_send()

    @pl.when(has_before)
    def _():
        for mb in range(batches):
            hand_copy(mb).wait_send()


def run_backward(cotangent, x, q, k, v, probs, mixed, slope, silu, weights, gain_attn, gain_mlp, cosine, sine):
    batches, rows, width = cotangent.shape
    hidden_width = weights[4].shape[2]
    one = (batches, rows, width)
    two = (batches, 2 * rows, width)
    wide = (batches, rows, hidden_width)
    outs = [(one, BF16), (one, BF16), (one, BF16), (wide, BF16), (wide, BF16), (one, BF16), (two, BF16), (two, BF16),
            ((16, width), F32)]
    scratch = [pltpu.VMEM(w.shape[1:], BF16) for w in weights] + [
        pltpu.VMEM(one, BF16),
        pltpu.VMEM(one, BF16),
        pltpu.VMEM(one, BF16),
        pltpu.VMEM(two, BF16),
        pltpu.VMEM(two, BF16),
        pltpu.VMEM((2,) + probs.shape[1:], BF16),
        pltpu.VMEM(one, F32),
        pltpu.VMEM(wide, BF16),
        pltpu.VMEM(wide, BF16),
        pltpu.VMEM(one, BF16),
        pltpu.VMEM(one[1:], BF16),
        pltpu.VMEM(one[1:], F32),
        pltpu.VMEM(one[1:], F32),
        pltpu.VMEM(one, BF16),
        pltpu.VMEM(one, BF16),
        pltpu.VMEM(one, BF16),
        pltpu.SemaphoreType.DMA((7,)),
        pltpu.SemaphoreType.DMA((7, batches)),
        pltpu.SemaphoreType.DMA((2,)),
        pltpu.SemaphoreType.DMA((7, batches)),
    ] + [pltpu.SemaphoreType.DMA((batches,))] * 6
    return pl.pallas_call(
        backward_kernel,
        out_shape=[jax.ShapeDtypeStruct(shape, dtype) for shape, dtype in outs],
        in_specs=[any_spec()] * 16 + [vmem_spec()] * 4,
        out_specs=[any_spec()] * 8 + [vmem_spec()],
        scratch_shapes=scratch,
        compiler_params=pltpu.CompilerParams(
            collective_id=2, has_side_effects=True, vmem_limit_bytes=VMEM_BYTES),
        name="backward",
    )(cotangent, x, q, k, v, probs, mixed, slope, silu, *weights, gain_attn, gain_mlp, cosine, sine)


LAG = 2
SENDS = 4
CHUNK = 256


class Ladder:
    def __init__(self, refs, sems, outer):
        self.dw, self.a_out, self.a_in, self.b_out, self.b_own, self.b_in, self.c_out, self.c_own, self.c_in, self.result = refs
        self.a_send, self.a_recv, self.b_send, self.b_recv, self.c_send, self.c_recv = sems
        wide = lax.axis_index("wide")
        self.outer = outer
        self.core, self.side, self.depth = lax.rem(wide, 2), lax.rem(wide // 2, 2), wide // 4
        self.core_mate = {"wide": wide + 1 - 2 * self.core}
        self.side_mate = {"wide": wide + 2 - 4 * self.side}
        self.column = lax.rem(wide, 4)

    def a_copy(self, j):
        slot = lax.rem(j, SENDS)
        return pltpu.make_async_remote_copy(
            self.a_out.at[slot], self.a_in.at[j], self.a_send.at[slot], self.a_recv.at[j],
            device_id=self.core_mate, device_id_type=MESH)

    def b_copy(self, j):
        slot = lax.rem(j, SENDS)
        return pltpu.make_async_remote_copy(
            self.b_out.at[slot], self.b_in.at[j], self.b_send.at[slot], self.b_recv.at[j],
            device_id=self.side_mate, device_id_type=MESH)

    def c_copy(self, j, step, arriving):
        slot = lax.rem(j, SENDS)
        peer = lax.rem(self.depth + step, self.outer)
        sender = peer if arriving else self.depth
        return pltpu.make_async_remote_copy(
            self.c_out.at[slot, peer], self.c_in.at[j, sender], self.c_send.at[slot, step], self.c_recv.at[j, sender],
            device_id={"wide": peer * 4 + self.column}, device_id_type=MESH)

    def stage_a(self, j):
        slot, held = lax.rem(j, SENDS), lax.rem(j, LAG + 1)

        @pl.when(j >= SENDS)
        def _():
            self.a_copy(j - SENDS).wait_send()

        for index in range(2 * self.outer):
            self.a_out[slot, index] = self.dw[held, 2 * index + 1 - self.core].astype(BF16)
        self.a_copy(j).start()

    def stage_b(self, j):
        slot, held = lax.rem(j, SENDS), lax.rem(j, LAG + 1)

        @pl.when(j >= SENDS)
        def _():
            self.b_copy(j - SENDS).wait_send()

        self.a_copy(j).wait_recv()
        for index in range(self.outer):
            far, near = 2 * index + 1 - self.side, 2 * index + self.side
            self.b_out[slot, index] = (
                self.dw[held, 2 * far + self.core] + self.a_in[j, far].astype(F32)).astype(BF16)
            self.b_own[held, index] = self.dw[held, 2 * near + self.core] + self.a_in[j, near].astype(F32)
        self.b_copy(j).start()

    def stage_c(self, j):
        slot, held = lax.rem(j, SENDS), lax.rem(j, LAG + 1)

        @pl.when(j >= SENDS)
        def _():
            for step in range(1, self.outer):
                self.c_copy(j - SENDS, step, False).wait_send()

        self.b_copy(j).wait_recv()
        for index in range(self.outer):
            self.c_out[slot, index] = (self.b_own[held, index] + self.b_in[j, index].astype(F32)).astype(BF16)
        for step in range(1, self.outer):
            self.c_copy(j, step, False).start()
        self.c_own[held] = self.b_own[held, self.depth] + self.b_in[j, self.depth].astype(F32)

    def stage_d(self, j):
        held = lax.rem(j, LAG + 1)
        total = self.c_own[held]
        for step in range(1, self.outer):
            self.c_copy(j, step, True).wait_recv()
        for step in range(1, self.outer):
            total = total + self.c_in[j, lax.rem(self.depth + step, self.outer)].astype(F32)
        self.result[j] = total

    def drain(self, count):
        for j in range(max(0, count - SENDS), count):
            self.a_copy(j).wait_send()
            self.b_copy(j).wait_send()
            for step in range(1, self.outer):
                self.c_copy(j, step, False).wait_send()


def weight_kernel(
    normed_in, att_in, n2_in, prod_in, g_in, db_in, dg_in, du_in, dq_in, dk_in, dv_in, gains,
    out_m, out_d,
    normed, att, n2, prod, g, turned, turned_halo, turned_prod, dy, *rest,
):
    m_refs, d_refs = rest[:9], rest[9:18]
    m_sems, d_sems = rest[18:24], rest[24:30]
    x_sem, dy_sem = rest[30], rest[31]
    wide, count = lax.axis_index("wide"), lax.axis_size("wide")
    batches, rows, width = g_in.shape
    hidden_width = prod_in.shape[2]
    outer = count // 4
    own = pl.ds(rows, rows)
    m_count, d_count = out_m.shape[0], out_d.shape[0]
    per_wide, per_narrow = hidden_width // CHUNK, width // CHUNK
    ladder_m = Ladder(m_refs + (out_m,), m_sems, outer)
    ladder_d = Ladder(d_refs + (out_d,), d_sems, outer)
    true = wide >= 0
    meet([(true, ladder_m.core_mate), (true, ladder_m.side_mate)] + [
        (true, {"wide": lax.rem(ladder_m.depth + step, outer) * 4 + ladder_m.column}) for step in range(1, outer)])

    loads = ((n2_in, n2), (att_in, att), (normed_in, normed), (prod_in, prod), (g_in, g))

    def x_copy(index):
        source, target = loads[index]
        return pltpu.make_async_copy(source, target, x_sem.at[index])

    kinds = ((dg_in, per_wide), (du_in, per_wide), (db_in, per_narrow), (dq_in, per_narrow), (dk_in, per_narrow), (dv_in, per_narrow))

    def each_load(j, act):
        slot = lax.rem(j, 2)
        base = 0
        for index, (source, parts) in enumerate(kinds):
            @pl.when((j >= base) & (j < base + parts))
            def _(source=source, base=base, index=index):
                lanes = pl.ds(pl.multiple_of((j - base) * CHUNK, CHUNK), CHUNK)
                target = dy.at[slot] if index >= 4 else dy.at[slot, :, own]
                act(pltpu.make_async_copy(source.at[:, :, lanes], target, dy_sem.at[slot]))
            base += parts
        return base

    x_copy(0).start()
    each_load(jnp.int32(0), lambda copy: copy.start())
    for index in range(1, 5):
        x_copy(index).start()

    def turn(source, target, halo):
        for mb in range(batches):
            block = source[mb, :rows] if halo is None else source[mb, halo * rows:(halo + 1) * rows]
            target[:, mb * rows:(mb + 1) * rows] = block.T

    x_copy(0).wait()
    turn(n2, turned.at[0], None)

    kv_first = 2 * per_wide + 2 * per_narrow
    kv_last = kv_first + 2 * per_narrow
    narrow_first = 2 * per_wide

    def compute_m(j):
        slot, held = lax.rem(j, 2), lax.rem(j, LAG + 1)

        @pl.when(j + 1 < kv_last)
        def _():
            each_load(j + 1, lambda copy: copy.start())

        @pl.when(j < kv_last)
        def _():
            each_load(j, lambda copy: copy.wait())
            which = jnp.where(j < narrow_first, 0, jnp.where(j < narrow_first + per_narrow, 1, 2))
            right = dy[slot, :, rows:, :].reshape(batches * rows, CHUNK)
            product = dot(turned[which], right)
            ladder_m.dw[held] = product.reshape(ladder_m.dw.shape[1:])

        @pl.when((j >= kv_first) & (j < kv_last))
        def _():
            right = dy[slot, :, :rows, :].reshape(batches * rows, CHUNK)
            product = dot(turned_halo[...], right)
            ladder_m.dw[held] = ladder_m.dw[held] + product.reshape(ladder_m.dw.shape[1:])

        @pl.when(j == kv_last)
        def _():
            first = jnp.sum(gains[0:8, :], axis=0, keepdims=True)
            second = jnp.sum(gains[8:16, :], axis=0, keepdims=True)
            row = lax.broadcasted_iota(jnp.int32, (LANES, width), 0)
            placed = jnp.where(row == 0, first, jnp.where(row == 1, second, 0.0))
            columns = placed.T
            ladder_m.dw[held] = jnp.concatenate([columns, columns], axis=1).reshape(ladder_m.dw.shape[1:])

    def compute_d(j):
        held = lax.rem(j, LAG + 1)
        lanes = pl.ds(pl.multiple_of(j * LANES, LANES), LANES)
        product = dot(turned_prod[...], g[:, :, lanes].reshape(batches * rows, LANES))
        ladder_d.dw[held] = product.reshape(ladder_d.dw.shape[1:])

    def on_chunk(s, act_m, act_d):
        @pl.when((s >= 0) & (s < narrow_first))
        def _():
            act_m(s)

        @pl.when((s >= narrow_first) & (s < narrow_first + d_count))
        def _():
            act_d(s - narrow_first)

        @pl.when((s >= narrow_first + d_count) & (s < m_count + d_count))
        def _():
            act_m(s - d_count)

    def both(s, name):
        on_chunk(s, getattr(ladder_m, name), getattr(ladder_d, name))

    def step(s, carry):
        @pl.when(s == 4)
        def _():
            x_copy(1).wait()
            turn(att, turned.at[1], None)

        @pl.when(s == 6)
        def _():
            x_copy(2).wait()
            turn(normed, turned.at[2], 1)

        @pl.when(s == 8)
        def _():
            turn(normed, turned_halo, 0)

        @pl.when(s == 10)
        def _():
            x_copy(3).wait()
            x_copy(4).wait()

        for part in range(batches):
            @pl.when(s == 10 + part)
            def _(part=part):
                turned_prod[:, part * rows:(part + 1) * rows] = prod[part].T

        on_chunk(s, compute_m, compute_d)
        both(s, "stage_a")
        both(s - LAG, "stage_b")
        both(s - 2 * LAG, "stage_c")
        both(s - 3 * LAG, "stage_d")
        return carry

    lax.fori_loop(0, m_count + d_count + 3 * LAG, step, 0)
    ladder_m.drain(m_count)
    ladder_d.drain(d_count)


def run_weights(normed, att, n2, prod, g, db, dg, du, dq, dk, dv, gains, count):
    batches, rows, width = g.shape
    hidden_width = prod.shape[2]
    outer = count // 4
    m_count = 2 * (hidden_width // CHUNK) + 4 * (width // CHUNK) + 1
    d_count = width // LANES

    def ladder(chunks, block):
        refs = [
            pltpu.VMEM((LAG + 1, count) + block, F32),
            pltpu.VMEM((SENDS, count // 2) + block, BF16),
            pltpu.VMEM((chunks, count // 2) + block, BF16),
            pltpu.VMEM((SENDS, outer) + block, BF16),
            pltpu.VMEM((LAG + 1, outer) + block, F32),
            pltpu.VMEM((chunks, outer) + block, BF16),
            pltpu.VMEM((SENDS, outer) + block, BF16),
            pltpu.VMEM((LAG + 1,) + block, F32),
            pltpu.VMEM((chunks, outer) + block, BF16),
        ]
        sems = [
            pltpu.SemaphoreType.DMA((SENDS,)),
            pltpu.SemaphoreType.DMA((chunks,)),
            pltpu.SemaphoreType.DMA((SENDS,)),
            pltpu.SemaphoreType.DMA((chunks,)),
            pltpu.SemaphoreType.DMA((SENDS, outer)),
            pltpu.SemaphoreType.DMA((chunks, outer)),
        ]
        return refs, sems

    block_m, block_d = (width // count, CHUNK), (hidden_width // count, LANES)
    m_refs, m_sems = ladder(m_count, block_m)
    d_refs, d_sems = ladder(d_count, block_d)
    tokens = batches * rows
    return pl.pallas_call(
        weight_kernel,
        out_shape=[
            jax.ShapeDtypeStruct((m_count,) + block_m, F32),
            jax.ShapeDtypeStruct((d_count,) + block_d, F32),
        ],
        in_specs=[any_spec()] * 11 + [vmem_spec()],
        out_specs=[vmem_spec()] * 2,
        scratch_shapes=[
            pltpu.VMEM(normed.shape, BF16),
            pltpu.VMEM(att.shape, BF16),
            pltpu.VMEM(n2.shape, BF16),
            pltpu.VMEM(prod.shape, BF16),
            pltpu.VMEM(g.shape, BF16),
            pltpu.VMEM((3, width, tokens), BF16),
            pltpu.VMEM((width, tokens), BF16),
            pltpu.VMEM((hidden_width, tokens), BF16),
            pltpu.VMEM((2, batches, 2 * rows, CHUNK), BF16),
        ] + m_refs + d_refs + m_sems + d_sems + [
            pltpu.SemaphoreType.DMA((5,)),
            pltpu.SemaphoreType.DMA((2,)),
        ],
        compiler_params=pltpu.CompilerParams(
            collective_id=3, has_side_effects=True, vmem_limit_bytes=VMEM_BYTES),
        name="weights",
    )(normed, att, n2, prod, g, db, dg, du, dq, dk, dv, gains)


def summed_weights(normed, att, n2, prod, g, db, dg, du, dq, dk, dv, gains):
    def outer_sum(left, right):
        total = lax.dot_general(
            left, right, (((0, 1), (0, 1)), ((), ())), preferred_element_type=F32)
        return lax.psum_scatter(total[None], "wide", scatter_dimension=1, tiled=True)

    rows = g.shape[1]
    normed_own = normed[:, rows:]
    gain_rows = gains.reshape(2, 8, -1).sum(axis=1)
    gain_parts = [
        lax.psum_scatter(gain_rows[i:i + 1], "wide", scatter_dimension=1, tiled=True) for i in range(2)]
    return (
        outer_sum(normed_own, dq), outer_sum(normed, dk), outer_sum(normed, dv), outer_sum(att, db),
        outer_sum(n2, dg), outer_sum(n2, du), outer_sum(prod, g), *gain_parts,
    )


def weight_grads(normed, att, n2, prod, g, db, dg, du, dq, dk, dv, gains):
    count = lax.axis_size("wide")
    width, hidden_width = g.shape[2], prod.shape[2]
    if count % 4 or width % (16 * count) or hidden_width % (16 * count):
        return summed_weights(normed, att, n2, prod, g, db, dg, du, dq, dk, dv, gains)
    out_m, out_d = run_weights(normed, att, n2, prod, g, db, dg, du, dq, dk, dv, gains, count)

    def spread(chunks):
        return chunks.transpose(1, 0, 2).reshape(1, chunks.shape[1], -1)

    sizes = [hidden_width // CHUNK] * 2 + [width // CHUNK] * 4
    parts, base = [], 0
    for size in sizes:
        parts.append(spread(out_m[base:base + size]))
        base += size
    gate, up, output, query, key, value = parts
    return (
        query, key, value, output, gate, up, spread(out_d),
        out_m[base, :, 0][None], out_m[base, :, 1][None],
    )


def per_device(
    tokens, cotangent, seg_lengths, w_query, w_key, w_value, w_output, w_gate, w_up, w_down, gain_attn, gain_mlp,
):
    weights = (w_query, w_key, w_value, w_output, w_gate, w_up, w_down)
    batches, rows, width = tokens.shape
    start_row = lax.axis_index("wide") * rows
    lengths = seg_lengths.reshape(batches, -1)
    starts = jnp.cumsum(lengths, axis=1) - lengths
    positions = start_row - rows + jnp.arange(2 * rows, dtype=jnp.int32)
    first = jnp.max(
        jnp.where(starts[:, None, :] <= positions[None, :, None], starts[:, None, :], 0), axis=2)
    first_key = (first[:, None, rows:] - start_row).astype(jnp.int32)
    offsets = (positions[None] - first).astype(F32)
    head_dim = width // HEADS
    half_dim = head_dim // 2
    freqs = THETA ** (-jnp.arange(half_dim, dtype=F32) * 2.0 / head_dim)
    angles = offsets[:, :, None] * jnp.tile(freqs, LANES // half_dim)[None, None, :]
    sign = jnp.tile(jnp.repeat(jnp.array([-1.0, 1.0], F32), half_dim), LANES // head_dim)
    cosine, sine = jnp.cos(angles), jnp.sin(angles) * sign

    (block_out, x, normed, q, k, v, probs, att, mixed, n2, slope, silu, prod) = run_forward(
        tokens, weights, gain_attn, gain_mlp, cosine, sine, first_key)
    input_grads, g, db, dg, du, dq, dk, dv, gains = run_backward(
        cotangent, x, q, k, v, probs, mixed, slope, silu, weights, gain_attn, gain_mlp, cosine, sine)
    grads = weight_grads(normed, att, n2, prod, g, db, dg, du, dq, dk, dv, gains)
    return (block_out[None], input_grads[None], *grads)


def solution(mesh):
    in_specs = (
        P(None, "wide", None),
        P(None, "wide", None),
        P(),
        *[P("section", None, None)] * 7,
        *[P("section", None)] * 2,
    )
    out_specs = (
        *[P("section", None, "wide", None)] * 2,
        *[P("section", "wide", None)] * 7,
        *[P("section", "wide")] * 2,
    )
    return jax.shard_map(
        per_device, mesh=mesh, in_specs=in_specs, out_specs=out_specs, check_vma=False
    )
```

time: 1590 us -> 329 us (0.21)
  matrix products: 642 us -> 0 us
  waiting for transfers between devices: 514 us -> 0 us
  Pallas kernels: 0 us -> 307 us
  local copies, waits for them, and re-layouts: 181 us -> 13.3 us
  other arithmetic: 143 us -> 8.2 us
  starting transfers between devices: 77.9 us -> 0 us
  between operations: 18.5 us -> 0.76 us
    dot_general x165 -> x0, matrix products: 608 us -> none  [the longest x60 134 us: matmul(): return jnp.dot(left, right, preferred_element_type=jnp.float32)]
    reduce_scatter x7 -> x0, waiting for transfers between devices: 471 us -> none  [the longest x1 89.6 us: per_device(): lax.psum_scatter(totals[5][None], 'wide', scatter_dimension=1, tiled=True)]
    pallas_call x0 -> x3, Pallas kernels: none -> 307 us  [the longest x1 136 us: run_backward(): pl.pallas_call(backward_kernel, out_shape=[jax.ShapeDtypeStruct(shape, dt...]
    ppermute x23 -> x0, starting transfers between devices: 76.7 us -> none  [shifted(): return lax.ppermute(array, axis, pairs)]
    slice x55 -> x1, local copies, waits for them, and re-layouts: 75.5 us -> 0.7 us  [weight_grads(): out_m[base, :, 1][None]]
    another operation x60 -> x1, other arithmetic: 47.8 us -> 1.86 us  [per_device(): starts = jnp.cumsum(lengths, axis=1) - lengths]
    ppermute x23 -> x0, waiting for transfers between devices: 42.7 us -> none  [shifted(): return lax.ppermute(array, axis, pairs)]
    unnamed x624 -> x9, local copies, waits for them, and re-layouts: 45.4 us -> 4.04 us
  transfers between devices with their start and end apart: 32 -> 0, of which waited for: 14 -> 0; matrix products, arithmetic and copies ran while one was open for 28% -> 0% of each run, Pallas kernels for 0% -> 0%
where the time goes in v1:
time: 329 us
  Pallas kernels  307 us (93%)
  local copies, waits for them, and re-layouts  13.3 us (4%)
  other arithmetic  8.2 us (2%)
    pallas_call x1, Pallas kernels, run_backward(): pl.pallas_call(backward_kernel, out_shape=[jax.ShapeDtypeStruct(shape, dt...  136 us
    pallas_call x1, Pallas kernels, run_weights(): pl.pallas_call(weight_kernel, out_shape=[jax.ShapeDtypeStruct((m_count,)...  103 us
    pallas_call x1, Pallas kernels, run_forward(): pl.pallas_call(forward_kernel, out_shape=[jax.ShapeDtypeStruct(shape, dty...  68.3 us

profile of v1, /device:TPU:0, one launch (start us, length us, event | category | flops | bytes accessed | tf_op | source)
XLA Modules:
  0.0 328.9 jit_solution(6623892587278056229)
XLA Ops:
  0.7 0.7 broadcast_in_dim.26
  1.4 0.1 tile.14
  1.5 0.1 mul.36
  1.6 0.1 mul.33
  1.7 1.9 reduce_window_sum.11
  3.5 0.7 sub.29
  4.2 0.1 copy.32
  4.3 0.1 select_reduce_fusion
  4.5 0.6 sub.33.first_key
  5.1 5.5 %fusion = (f32[4,512,128]{2,1,0:T(8,128)}, f32[4,512,128]{2,1,0:T(8,128)}) fusion(f32[128]{0:T(128)S(1)} %mul.36, f32[128]{0:T(128)S(1)} %mul.33, f32[4,512]{1,0:T(4,128)S(1)} %subtract_convert_fusion), kind=kLoop, calls=%fused_computation.2 | loop fusion | flops 524288 | bytes 2106368 | tf_op jit(solution)/shard_map/mul | solution.py:983
  10.6 68.3 %forward.1 = (bf16[4,256,768]{2,1,0:T(8,128)(2,1)}, bf16[4,256,768]{2,1,0:T(8,128)(2,1)}, bf16[4,512,768]{2,1,0:T(8,128)(2,1)}, bf16[4,256,768]{2,1,0:T(8,128)(2...) custom-call(bf16[4,256,768]{2,1,0:T(8,128)(2,1)} %tokens.1, ...), custom_call_target="tpu_custom_call" | custom-call | tf_op jit(solution)/shard_map/forward/pallas_call | solution.py:320
  78.9 135.7 %backward.1 = (bf16[4,256,768]{2,1,0:T(8,128)(2,1)}, bf16[4,256,768]{2,1,0:T(8,128)(2,1)}, bf16[4,256,768]{2,1,0:T(8,128)(2,1)}, bf16[4,256,2048]{2,1,0:T(8,128)...) custom-call(bf16[4,256,768]{2,1,0:T(8,128)(2,1)} %cotangent.1, ...), custom_call_target="tpu_custom_call" | custom-call | tf_op jit(solution)/shard_map/backward/pallas_call | solution.py:612
  214.6 102.5 %weights.1 = (f32[29,48,256]{2,1,0:T(8,128)}, f32[6,128,128]{2,1,0:T(8,128)}) custom-call(bf16[4,512,768]{2,1,0:T(8,128)(2,1)} %get-tuple-element.45.normed_in, bf16[4,256,768]{2,1,0:T(8,128)(2,1)} %get-tuple-element.46.att_in, bf16[4,256,768]{2,1,0:T(8,128)(2,1)} %get-tuple-element.47.n2_in, bf16[4,256,2048]{2,1,0:T(8,128)(2,1)} %get-tuple-element.48.prod_in, ...), custom_call_target="tpu_custom_call" | custom-call | tf_op jit(solution)/shard_map/weights/pallas_call | solution.py:898
  317.2 0.0 copy-start.2
  317.2 1.3 copy.39
  318.4 0.9 copy.40
  319.4 0.0 copy-done.2
  319.4 0.7 slice_reduce_fusion
  320.1 0.1 slice_bitcast_fusion
  320.2 0.2 copy.38
  320.4 0.8 reshape.86
  321.2 0.1 copy.36
  321.3 0.8 reshape.84
  322.1 0.1 copy.35
  322.2 0.0 copy-start
  322.2 0.8 reshape.83
  323.0 0.1 copy.34
  323.1 0.8 reshape.82
  323.8 0.1 copy.33
  323.9 0.8 reshape.81
  324.7 0.2 copy.37
  324.9 0.8 reshape.85
  325.7 0.0 copy-done
  325.7 0.0 copy-start.1
  325.7 1.1 copy.43
  326.9 0.8 copy-done.1
  327.7 1.1 copy.44
  (7 shorter events, 0.1 us)
Async XLA Ops:
  317.2 2.2 copy-start.2
  322.2 3.6 %copy-start = (bf16[4,256,768]{2,1,0:T(8,128)(2,1)S(1)}, bf16[4,256,768]{2,1,0:T(8,128)(2,1)}, u32[]{:S(2)}) copy-start(bf16[4,256,768]{2,1,0:T(8,128)(2,1)} %get-tuple-element.35) | copy-start | bytes 4718596
  325.7 2.0 copy-start.1

commit v2 on v1

v2 whole, which is shorter than its diff:
```python
import functools

import jax
import jax.numpy as jnp
import ml_dtypes
import numpy as np
from jax import lax
from jax.experimental import pallas as pl
from jax.experimental.pallas import tpu as pltpu
from jax.sharding import PartitionSpec as P

HEADS = 12
EPS = 1e-05
THETA = 10000.0

F32 = jnp.float32
BF16 = jnp.bfloat16
MESH = pl.DeviceIdType.MESH
LANES = 128
BLOCK = 64
VMEM_BYTES = 63 * 1024 * 1024


def dot(left, right):
    return jnp.dot(left, right, preferred_element_type=F32)


def dot_nt(left, right):
    return lax.dot_general(
        left, right, (((1,), (1,)), ((), ())), preferred_element_type=F32
    )


def rms_parts(hidden):
    inverse = lax.rsqrt(jnp.mean(hidden * hidden, axis=1, keepdims=True) + EPS)
    return (hidden * inverse, inverse)


def rms_back(upstream, scaled, inverse):
    return inverse * (upstream - scaled * jnp.mean(upstream * scaled, axis=1, keepdims=True))


def low_half(rows):
    lane = lax.broadcasted_iota(jnp.int32, (rows, LANES), 1)
    return lane % 64 < 32


def rope(field, cosine, sine, direction):
    partner = jnp.where(
        low_half(field.shape[0]),
        pltpu.roll(field, 96, 1),
        pltpu.roll(field, 32, 1),
    )
    if direction > 0:
        return field * cosine + partner * sine
    return field * cosine - partner * sine


def split_heads(block):
    lane = lax.broadcasted_iota(jnp.int32, block.shape, 1)
    zero = jnp.zeros_like(block)
    return jnp.concatenate(
        [jnp.where(lane < 64, block, zero), jnp.where(lane >= 64, block, zero)], axis=0
    )


def join_heads(turned):
    count = turned.shape[1] // 2
    row = lax.broadcasted_iota(jnp.int32, (LANES, count), 0)
    return jnp.where(row < 64, turned[:, :count], turned[:, count:]).T


def meet(partners):
    barrier = pltpu.get_barrier_semaphore()
    total = 0
    for condition, device in partners:

        @pl.when(condition)
        def _(device=device):
            pl.semaphore_signal(barrier, inc=1, device_id=device, device_id_type=MESH)

        total = total + condition.astype(jnp.int32)
    pl.semaphore_wait(barrier, total)


def layers_kernel(
    tokens, cotangent, lengths,
    w_query, w_key, w_value, w_output, w_gate, w_up, w_down,
    gain_attn, gain_mlp, trig,
    block_out, grad_out, normed_out, att_out, n2_out, prod_out,
    g_out, db_out, dg_out, du_out, dq_out, dk_out, dv_out, gains_out,
    wq, wk, wv, wo, wg, wu, wd,
    xs, qs, ks, vs, probs, slope, silu, mixed, normed, att, n2, prod, outs, gs,
    halo_in, halo_out, branch, d_att, d_norm, d_own, cosine, sine, first_key, bias, scale,
    wide_f, left_b, right_b, key_f, value_f,
    weight_sem, trig_sem, token_sem, cot_sem, save_sem, out_sem,
    halo_send, halo_recv, hand_send, hand_recv, back_send, back_recv, turn_send, turn_recv,
):
    section, wide = lax.axis_index("section"), lax.axis_index("wide")
    last_section, last_wide = lax.axis_size("section") - 1, lax.axis_size("wide") - 1
    batches, rows, width = tokens.shape
    hidden_width = wg.shape[1]
    half = rows // 2
    band = rows + half
    pairs = width // LANES
    own, halo = pl.ds(rows, rows), pl.ds(0, rows)
    has_left, has_right = wide > 0, wide < last_wide
    has_before, has_after = section > 0, section < last_section
    is_first, is_last = jnp.logical_not(has_before), jnp.logical_not(has_after)

    weights = ((w_query, wq), (w_key, wk), (w_value, wv), (w_output, wo),
               (w_gate, wg), (w_up, wu), (w_down, wd))

    def weight_copy(index):
        source, target = weights[index]
        return pltpu.make_async_copy(source.at[0], target, weight_sem.at[index])

    def token_copy(mb):
        return pltpu.make_async_copy(tokens.at[mb], xs.at[mb, own], token_sem.at[mb])

    def cot_copy(mb):
        return pltpu.make_async_copy(cotangent.at[mb], gs.at[mb], cot_sem.at[mb])

    def halo_copy(mb, source):
        return pltpu.make_async_remote_copy(
            source, xs.at[mb, halo], halo_send.at[mb], halo_recv.at[mb],
            device_id={"wide": wide + 1}, device_id_type=MESH)

    def hand_copy(mb):
        return pltpu.make_async_remote_copy(
            outs.at[mb], xs.at[mb, own], hand_send.at[mb], hand_recv.at[mb],
            device_id={"section": section + 1}, device_id_type=MESH)

    def back_copy(mb):
        return pltpu.make_async_remote_copy(
            halo_out, halo_in.at[mb], back_send.at[mb], back_recv.at[mb],
            device_id={"wide": wide - 1}, device_id_type=MESH)

    def turn_copy(mb):
        return pltpu.make_async_remote_copy(
            outs.at[mb], gs.at[mb], turn_send.at[mb], turn_recv.at[mb],
            device_id={"section": section - 1}, device_id_type=MESH)

    def out_copy(mb, target):
        return pltpu.make_async_copy(outs.at[mb], target.at[mb], out_sem.at[mb])

    def save(name, mb):
        source, target, index = {
            "normed": (normed, normed_out, 0), "att": (att, att_out, 1), "n2": (n2, n2_out, 2),
            "prod": (prod, prod_out, 3), "branch": (branch.at[lax.rem(mb, 2)], db_out, 4),
            "g": (gs.at[mb], g_out, 5), "dg": (slope.at[mb], dg_out, 6), "du": (silu.at[mb], du_out, 7),
            "dq": (qs.at[mb], dq_out, 8), "dk": (ks.at[mb], dk_out, 9), "dv": (vs.at[mb], dv_out, 10),
        }[name]
        return pltpu.make_async_copy(source, target.at[mb], save_sem.at[index, mb])

    def saved_before(name, mb):
        @pl.when(mb > 0)
        def _():
            save(name, mb - 1).wait()

    @pl.when(is_first)
    def _():
        token_copy(0).start()

    trig_copy = pltpu.make_async_copy(trig, left_b, trig_sem.at[0])
    trig_copy.start()
    for index in range(3):
        weight_copy(index).start()

    meet([
        (has_left, {"wide": wide - 1}), (has_right, {"wide": wide + 1}),
        (has_before, {"section": section - 1}), (has_after, {"section": section + 1}),
    ])

    @pl.when(is_first & has_right)
    def _():
        halo_copy(0, tokens.at[0]).start()

    @pl.when(is_first)
    def _():
        for mb in range(1, batches):
            token_copy(mb).start()

    @pl.when(is_last)
    def _():
        for mb in range(batches):
            cot_copy(mb).start()

    @pl.when(jnp.logical_not(has_left))
    def _():
        xs[:, halo, :] = jnp.zeros((batches, rows, width), BF16)

    gains_out[...] = jnp.zeros(gains_out.shape, F32)

    start_row = wide * rows

    def tables(mb, carry):
        positions = lax.broadcasted_iota(jnp.int32, (2 * rows, LANES), 0) + (start_row - rows)
        query_at = lax.broadcasted_iota(jnp.int32, (8, rows), 1) + start_row

        def later(image, state):
            start, first, first_row = state
            first = jnp.where(positions >= start, start, first)
            first_row = jnp.where(query_at >= start, start, first_row)
            return (start + lengths[mb, image], first, first_row)

        _, first, first_row = lax.fori_loop(
            0, lengths.shape[1], later,
            (jnp.int32(0), jnp.zeros((2 * rows, LANES), jnp.int32), jnp.zeros((8, rows), jnp.int32)))
        offsets = positions - first
        lane = lax.broadcasted_iota(jnp.int32, (2 * rows, LANES), 1)
        one_hot = jnp.concatenate(
            [jnp.where(offsets == lane + base, 1.0, 0.0).astype(BF16) for base in range(0, band, LANES)],
            axis=1)
        for which, table in enumerate((cosine, sine)):
            parts = dot(one_hot, left_b[which])
            table[mb] = parts[:, :LANES] + parts[:, LANES:]
        first_key[mb] = first_row - start_row
        return carry

    trig_copy.wait()
    lax.fori_loop(0, batches, tables, 0)

    items = [(pair, block) for pair in range(pairs) for block in range(2)]

    def place(index):
        pair, block = items[index]
        lanes = slice(pair * LANES, (pair + 1) * LANES)
        low = block * half
        return lanes, slice(low, low + half), slice(low, low + band)

    def pipelined(first, second, third):
        first(0)
        for index in range(len(items)):
            if index + 1 < len(items):
                first(index + 1)
            second(index)
            if index:
                third(index - 1)
        third(len(items) - 1)


    def normalise(mb, part):
        for low in range(part.start, part.start + rows, BLOCK):
            at = slice(low, low + BLOCK)
            scaled, _ = rms_parts(xs[mb, at, :].astype(F32))
            normed[at, :] = (scaled * gain_attn[...]).astype(BF16)

    def keys_values(mb, part):
        cos_rows, sin_rows = cosine[mb, part, :], sine[mb, part, :]
        for start in range(0, width, 256):
            rows_n = normed[part, :]
            keys = dot(rows_n, wk[:, start:start + 256])
            for inner in range(0, 256, LANES):
                ks[mb, part, start + inner:start + inner + LANES] = rope(
                    keys[:, inner:inner + LANES], cos_rows, sin_rows, 1).astype(BF16)
            vs[mb, part, start:start + 256] = dot(rows_n, wv[:, start:start + 256]).astype(BF16)

    def attention(mb):
        def scores(index):
            lanes, here, near = place(index)
            wide_f[index % 2] = dot_nt(ks[mb, near, lanes], split_heads(qs[mb, here, lanes]))

        def soften(index):
            pair, block = items[index]
            for head in range(2):
                at = slice(head * LANES, (head + 1) * LANES)
                masked = wide_f[index % 2, :, at] + bias[block]
                raw = jnp.exp(masked - jnp.max(masked, axis=0, keepdims=True))
                probs[mb, pair, block, :, at] = raw.astype(BF16)

        def collect(index):
            pair, block = items[index]
            lanes, here, near = place(index)
            left = jnp.concatenate([vs[mb, near, lanes].T, jnp.ones((16, band), BF16)], axis=0)
            turned = dot(left, probs[mb, pair, block])
            inverse = 1.0 / turned[LANES:LANES + 1]
            scale[mb, index] = inverse
            att[here, lanes] = join_heads(turned[:LANES] * inverse).astype(BF16)

        pipelined(scores, soften, collect)

    def forward(mb, carry):
        @pl.when(is_first)
        def _():
            token_copy(mb).wait()

            @pl.when(has_right & (mb + 1 < batches))
            def _():
                halo_copy(mb + 1, tokens.at[mb + 1]).start()

        @pl.when(has_before & (mb == 0))
        def _():
            hand_copy(mb).wait_recv()

            @pl.when(has_right)
            def _():
                halo_copy(mb, xs.at[mb, own]).start()

        saved_before("normed", mb)
        normalise(mb, own)

        @pl.when(mb == 0)
        def _():
            for index in range(3):
                weight_copy(index).wait()
            for index in range(3, 7):
                weight_copy(index).start()

        cos_rows, sin_rows = cosine[mb, own, :], sine[mb, own, :]
        for start in range(0, width, 256):
            queries = dot(normed[own, :], wq[:, start:start + 256])
            for inner in range(0, 256, LANES):
                turned = rope(queries[:, inner:inner + LANES], cos_rows, sin_rows, 1)
                qs[mb, :, start + inner:start + inner + LANES] = (turned * 0.125).astype(BF16)
        keys_values(mb, own)
        for block in range(2):
            key_at = lax.broadcasted_iota(jnp.int32, (band, half), 0) + (block * half - rows)
            query_at = lax.broadcasted_iota(jnp.int32, (band, half), 1) + block * half
            first = first_key[mb, 0:1, block * half:(block + 1) * half]
            bias[block] = jnp.where((key_at >= first) & (key_at <= query_at), 0.0, -1e30)

        @pl.when(has_left)
        def _():
            halo_copy(mb, xs.at[mb, own]).wait_recv()

        normalise(mb, halo)
        keys_values(mb, halo)
        save("normed", mb).start()
        saved_before("att", mb)
        attention(mb)
        save("att", mb).start()

        @pl.when(mb == 0)
        def _():
            for index in range(3, 7):
                weight_copy(index).wait()

        saved_before("n2", mb)
        for start in range(0, width, 256):
            at = slice(start, start + 256)
            d_norm[:, at] = xs[mb, own, at].astype(F32) + dot(att[...], wo[:, at])
        for low in range(0, rows, BLOCK):
            at = slice(low, low + BLOCK)
            total = d_norm[at, :]
            scaled, _ = rms_parts(total)
            mixed[mb, at, :] = total.astype(BF16)
            n2[at, :] = (scaled * gain_mlp[...]).astype(BF16)
        save("n2", mb).start()

        @pl.when(has_before & (mb + 1 < batches))
        def _():
            hand_copy(mb + 1).wait_recv()

            @pl.when(has_right)
            def _():
                halo_copy(mb + 1, xs.at[mb + 1, own]).start()

        saved_before("prod", mb)
        for start in range(0, hidden_width, 256):
            at = slice(start, start + 256)
            gate = dot(n2[...], wg[:, at])
            up = dot(n2[...], wu[:, at])
            sigma = jax.nn.sigmoid(gate)
            gated = gate * sigma
            prod[:, at] = (gated * up).astype(BF16)
            silu[mb, :, at] = gated.astype(BF16)
            slope[mb, :, at] = (up * (sigma * (1.0 + gate * (1.0 - sigma)))).astype(BF16)
        save("prod", mb).start()
        for start in range(0, width, 256):
            at = slice(start, start + 256)
            outs[mb, :, at] = (d_norm[:, at] + dot(prod[...], wd[:, at])).astype(BF16)

        @pl.when(has_after)
        def _():
            hand_copy(mb).start()

        out_copy(mb, block_out).start()
        return carry

    lax.fori_loop(0, batches, forward, 0)

    for name in ("normed", "att", "n2", "prod"):
        save(name, batches - 1).wait()
    for mb in range(batches):
        out_copy(mb, block_out).wait()

    @pl.when(has_after)
    def _():
        for mb in range(batches):
            hand_copy(mb).wait_send()


    def add_gain(which, product):
        folded = jnp.sum(product.reshape(product.shape[0] // 8, 8, width), axis=0)
        at = pl.ds(8 * which, 8)
        gains_out[at, :] = gains_out[at, :] + folded

    def attention_back(mb):
        def d_weights(index):
            lanes, here, near = place(index)
            wide_f[index % 2] = dot_nt(vs[mb, near, lanes], split_heads(d_att[here, lanes]))

        def d_soften(index):
            pair, block = items[index]
            for head in range(2):
                at = slice(head * LANES, (head + 1) * LANES)
                weight = probs[mb, pair, block, :, at].astype(F32) * scale[mb, index, :, at]
                moved = weight * wide_f[index % 2, :, at]
                centre = jnp.sum(moved, axis=0, keepdims=True)
                left_b[index % 2, :, at] = (moved - weight * centre).astype(BF16)
                right_b[index % 2, :, at] = weight.astype(BF16)

        def collect(index):
            pair, block = items[index]
            lanes, here, near = place(index)
            d_scores = left_b[index % 2]
            d_keys = dot(d_scores, split_heads(qs[mb, here, lanes]))
            d_values = dot(right_b[index % 2], split_heads(d_att[here, lanes]))
            turned = lax.dot_general(
                ks[mb, near, lanes], d_scores, (((0,), (0,)), ((), ())), preferred_element_type=F32)
            at = pl.ds(rows + block * half, half)
            qs[mb, here, lanes] = rope(
                join_heads(turned) * 0.125, cosine[mb, at, :], sine[mb, at, :], -1).astype(BF16)
            slot = pair % 2
            if block == 0:
                key_f[slot], value_f[slot] = d_keys, d_values
                return
            earlier_k, earlier_v = key_f[slot], value_f[slot]
            pieces = (
                (0, half, earlier_k[:half], earlier_v[:half]),
                (half, band, earlier_k[half:] + d_keys[:rows], earlier_v[half:] + d_values[:rows]),
                (band, 2 * rows, d_keys[rows:], d_values[rows:]),
            )
            for low, high, piece_k, piece_v in pieces:
                ks[mb, low:high, lanes] = rope(
                    piece_k, cosine[mb, low:high, :], sine[mb, low:high, :], -1).astype(BF16)
                vs[mb, low:high, lanes] = piece_v.astype(BF16)

        pipelined(d_weights, d_soften, collect)

    def finish(mb):
        @pl.when(has_right)
        def _():
            back_copy(mb).wait_recv()
            d_own[...] = d_own[...] + halo_in[mb].astype(F32)

        for low in range(0, rows, BLOCK):
            at = slice(low, low + BLOCK)
            scaled, inverse = rms_parts(xs[mb, rows + low:rows + low + BLOCK, :].astype(F32))
            d_normed = d_own[at, :]
            add_gain(0, d_normed * scaled)
            back = rms_back(d_normed * gain_attn[...], scaled, inverse)
            outs[mb, at, :] = (branch[lax.rem(mb, 2), at, :].astype(F32) + back).astype(BF16)

        @pl.when(has_before)
        def _():
            turn_copy(mb).start()

        out_copy(mb, grad_out).start()

    def backward(mb, carry):
        @pl.when(is_last)
        def _():
            cot_copy(mb).wait()

        @pl.when(has_after)
        def _():
            turn_copy(mb).wait_recv()

        save("g", mb).start()
        for start in range(0, hidden_width, 256):
            at = slice(start, start + 256)
            d_product = dot_nt(gs[mb], wd[at, :])
            slope[mb, :, at] = (d_product * slope[mb, :, at].astype(F32)).astype(BF16)
            silu[mb, :, at] = (d_product * silu[mb, :, at].astype(F32)).astype(BF16)
        save("dg", mb).start()
        save("du", mb).start()
        for start in range(0, width, 256):
            at = slice(start, start + 256)
            d_norm[:, at] = dot_nt(slope[mb], wg[at, :]) + dot_nt(silu[mb], wu[at, :])
        slot = lax.rem(mb, 2)

        @pl.when(mb >= 2)
        def _():
            save("branch", mb - 2).wait()

        for low in range(0, rows, BLOCK):
            at = slice(low, low + BLOCK)
            scaled, inverse = rms_parts(mixed[mb, at, :].astype(F32))
            d_normed = d_norm[at, :]
            add_gain(1, d_normed * scaled)
            total = gs[mb, at, :].astype(F32) + rms_back(d_normed * gain_mlp[...], scaled, inverse)
            branch[slot, at, :] = total.astype(BF16)
        save("branch", mb).start()
        for start in range(0, width, 256):
            at = slice(start, start + 256)
            d_att[:, at] = dot_nt(branch[slot], wo[at, :]).astype(BF16)

        @pl.when(mb > 0)
        def _():
            finish(mb - 1)

        attention_back(mb)
        save("dq", mb).start()
        save("dk", mb).start()
        save("dv", mb).start()

        @pl.when(has_left & (mb > 0))
        def _():
            back_copy(mb - 1).wait_send()

        for start in range(0, width, 256):
            at = slice(start, start + 256)
            halo_out[:, at] = (
                dot_nt(ks[mb, halo, :], wk[at, :]) + dot_nt(vs[mb, halo, :], wv[at, :])).astype(BF16)

        @pl.when(has_left)
        def _():
            back_copy(mb).start()

        for start in range(0, width, 256):
            at = slice(start, start + 256)
            d_own[:, at] = (
                dot_nt(qs[mb], wq[at, :]) + dot_nt(ks[mb, own, :], wk[at, :])
                + dot_nt(vs[mb, own, :], wv[at, :]))
        return carry

    lax.fori_loop(0, batches, backward, 0)
    finish(batches - 1)

    for mb in range(batches - 2, batches):
        save("branch", mb).wait()
    for mb in range(batches):
        for name in ("g", "dg", "du", "dq", "dk", "dv"):
            save(name, mb).wait()
        out_copy(mb, grad_out).wait()

    @pl.when(has_left)
    def _():
        back_copy(batches - 1).wait_send()

    @pl.when(has_before)
    def _():
        for mb in range(batches):
            turn_copy(mb).wait_send()

    @pl.when(has_right)
    def _():
        for mb in range(batches):
            halo_copy(mb, xs.at[mb, own]).wait_send()


def any_spec():
    return pl.BlockSpec(memory_space=pl.ANY)


def vmem_spec():
    return pl.BlockSpec(memory_space=pltpu.VMEM)


def trig_table(head_dim, reach):
    half_dim = head_dim // 2
    freqs = np.float32(THETA) ** (-np.arange(half_dim, dtype=np.float32) * np.float32(2.0) / np.float32(head_dim))
    angles = np.arange(reach, dtype=np.float32)[:, None] * np.tile(freqs, LANES // half_dim)[None, :]
    sign = np.tile(np.repeat(np.array([-1.0, 1.0], np.float32), half_dim), LANES // head_dim)
    parts = []
    for table in (np.cos(angles), np.sin(angles) * sign):
        high = table.astype(ml_dtypes.bfloat16)
        low = (table - high.astype(np.float32)).astype(ml_dtypes.bfloat16)
        parts.append(np.concatenate([high, low], axis=1))
    return jnp.asarray(np.stack(parts))


def run_layers(tokens, cotangent, lengths, weights, gain_attn, gain_mlp):
    batches, rows, width = tokens.shape
    hidden_width = weights[4].shape[2]
    pairs = width // LANES
    band = rows + rows // 2
    one = (batches, rows, width)
    two = (batches, 2 * rows, width)
    wide = (batches, rows, hidden_width)
    outs = [(one, BF16), (one, BF16), (two, BF16), (one, BF16), (one, BF16), (wide, BF16),
            (one, BF16), (one, BF16), (wide, BF16), (wide, BF16), (one, BF16), (two, BF16), (two, BF16),
            ((16, width), F32)]
    dma = pltpu.SemaphoreType.DMA
    scratch = [pltpu.VMEM(w.shape[1:], BF16) for w in weights] + [
        pltpu.VMEM(two, BF16),
        pltpu.VMEM(one, BF16),
        pltpu.VMEM(two, BF16),
        pltpu.VMEM(two, BF16),
        pltpu.VMEM((batches, pairs, 2, band, rows), BF16),
        pltpu.VMEM(wide, BF16),
        pltpu.VMEM(wide, BF16),
        pltpu.VMEM(one, BF16),
        pltpu.VMEM(two[1:], BF16),
        pltpu.VMEM(one[1:], BF16),
        pltpu.VMEM(one[1:], BF16),
        pltpu.VMEM(wide[1:], BF16),
        pltpu.VMEM(one, BF16),
        pltpu.VMEM(one, BF16),
        pltpu.VMEM(one, BF16),
        pltpu.VMEM(one[1:], BF16),
        pltpu.VMEM((2,) + one[1:], BF16),
        pltpu.VMEM(one[1:], BF16),
        pltpu.VMEM(one[1:], F32),
        pltpu.VMEM(one[1:], F32),
        pltpu.VMEM((batches, 2 * rows, LANES), F32),
        pltpu.VMEM((batches, 2 * rows, LANES), F32),
        pltpu.VMEM((batches, 8, rows), jnp.int32),
        pltpu.VMEM((2, band, rows // 2), F32),
        pltpu.VMEM((batches, 2 * pairs, 1, rows), F32),
        pltpu.VMEM((2, band, rows), F32),
        pltpu.VMEM((2, band, rows), BF16),
        pltpu.VMEM((2, band, rows), BF16),
        pltpu.VMEM((2, band, LANES), F32),
        pltpu.VMEM((2, band, LANES), F32),
        dma((7,)), dma((1,)), dma((batches,)), dma((batches,)), dma((11, batches)),
    ] + [dma((batches,))] * 9
    trig = trig_table(width // HEADS, band)
    return pl.pallas_call(
        layers_kernel,
        out_shape=[jax.ShapeDtypeStruct(shape, dtype) for shape, dtype in outs],
        in_specs=[any_spec()] * 2 + [pl.BlockSpec(memory_space=pltpu.SMEM)] + [any_spec()] * 7 + [vmem_spec()] * 2 + [any_spec()],
        out_specs=[any_spec()] * 13 + [vmem_spec()],
        scratch_shapes=scratch,
        compiler_params=pltpu.CompilerParams(
            collective_id=1, has_side_effects=True, vmem_limit_bytes=VMEM_BYTES),
        name="layers",
    )(tokens, cotangent, lengths, *weights, gain_attn, gain_mlp, trig)


LAG = 2
SENDS = 4
CHUNK = 256


def dot_tn(left, right):
    return lax.dot_general(
        left, right, (((0,), (0,)), ((), ())), preferred_element_type=F32
    )


class Ladder:
    def __init__(self, refs, sems, outer):
        self.dw, self.a_out, self.a_in, self.b_out, self.b_own, self.b_in, self.c_out, self.c_own, self.c_in, self.result = refs
        self.a_send, self.a_recv, self.b_send, self.b_recv, self.c_send, self.c_recv = sems
        wide = lax.axis_index("wide")
        self.outer = outer
        self.core, self.side, self.depth = lax.rem(wide, 2), lax.rem(wide // 2, 2), wide // 4
        self.core_mate = {"wide": wide + 1 - 2 * self.core}
        self.side_mate = {"wide": wide + 2 - 4 * self.side}
        self.column = lax.rem(wide, 4)

    def a_copy(self, j):
        slot = lax.rem(j, SENDS)
        return pltpu.make_async_remote_copy(
            self.a_out.at[slot], self.a_in.at[j], self.a_send.at[slot], self.a_recv.at[j],
            device_id=self.core_mate, device_id_type=MESH)

    def b_copy(self, j):
        slot = lax.rem(j, SENDS)
        return pltpu.make_async_remote_copy(
            self.b_out.at[slot], self.b_in.at[j], self.b_send.at[slot], self.b_recv.at[j],
            device_id=self.side_mate, device_id_type=MESH)

    def c_copy(self, j, step, arriving):
        slot = lax.rem(j, SENDS)
        peer = lax.rem(self.depth + step, self.outer)
        sender = peer if arriving else self.depth
        return pltpu.make_async_remote_copy(
            self.c_out.at[slot, peer], self.c_in.at[j, sender], self.c_send.at[slot, step], self.c_recv.at[j, sender],
            device_id={"wide": peer * 4 + self.column}, device_id_type=MESH)

    def stage_a(self, j):
        slot, held = lax.rem(j, SENDS), lax.rem(j, LAG + 1)

        @pl.when(j >= SENDS)
        def _():
            self.a_copy(j - SENDS).wait_send()

        for index in range(2 * self.outer):
            self.a_out[slot, index] = self.dw[held, 2 * index + 1 - self.core].astype(BF16)
        self.a_copy(j).start()

    def stage_b(self, j):
        slot, held = lax.rem(j, SENDS), lax.rem(j, LAG + 1)

        @pl.when(j >= SENDS)
        def _():
            self.b_copy(j - SENDS).wait_send()

        self.a_copy(j).wait_recv()
        for index in range(self.outer):
            far, near = 2 * index + 1 - self.side, 2 * index + self.side
            self.b_out[slot, index] = (
                self.dw[held, 2 * far + self.core] + self.a_in[j, far].astype(F32)).astype(BF16)
            self.b_own[held, index] = self.dw[held, 2 * near + self.core] + self.a_in[j, near].astype(F32)
        self.b_copy(j).start()

    def stage_c(self, j):
        slot, held = lax.rem(j, SENDS), lax.rem(j, LAG + 1)

        @pl.when(j >= SENDS)
        def _():
            for step in range(1, self.outer):
                self.c_copy(j - SENDS, step, False).wait_send()

        self.b_copy(j).wait_recv()
        for index in range(self.outer):
            self.c_out[slot, index] = (self.b_own[held, index] + self.b_in[j, index].astype(F32)).astype(BF16)
        for step in range(1, self.outer):
            self.c_copy(j, step, False).start()
        self.c_own[held] = self.b_own[held, self.depth] + self.b_in[j, self.depth].astype(F32)

    def stage_d(self, j):
        held = lax.rem(j, LAG + 1)
        total = self.c_own[held]
        for step in range(1, self.outer):
            self.c_copy(j, step, True).wait_recv()
        for step in range(1, self.outer):
            total = total + self.c_in[j, lax.rem(self.depth + step, self.outer)].astype(F32)
        self.result[j] = total

    def drain(self, count):
        for j in range(max(0, count - SENDS), count):
            self.a_copy(j).wait_send()
            self.b_copy(j).wait_send()
            for step in range(1, self.outer):
                self.c_copy(j, step, False).wait_send()


def weight_kernel(
    normed_in, att_in, n2_in, prod_in, g_in, db_in, dg_in, du_in, dq_in, dk_in, dv_in, gains,
    out_m, out_d,
    normed, att, n2, prod, g, dy, *rest,
):
    m_refs, d_refs = rest[:9], rest[9:18]
    m_sems, d_sems = rest[18:24], rest[24:30]
    x_sem, dy_sem = rest[30], rest[31]
    wide, count = lax.axis_index("wide"), lax.axis_size("wide")
    batches, rows, width = g_in.shape
    hidden_width = prod_in.shape[2]
    outer = count // 4
    own = pl.ds(rows, rows)
    m_count, d_count = out_m.shape[0], out_d.shape[0]
    per_wide, per_narrow = hidden_width // CHUNK, width // CHUNK
    ladder_m = Ladder(m_refs + (out_m,), m_sems, outer)
    ladder_d = Ladder(d_refs + (out_d,), d_sems, outer)
    true = wide >= 0
    meet([(true, ladder_m.core_mate), (true, ladder_m.side_mate)] + [
        (true, {"wide": lax.rem(ladder_m.depth + step, outer) * 4 + ladder_m.column}) for step in range(1, outer)])

    loads = ((n2_in, n2), (att_in, att), (normed_in, normed), (prod_in, prod), (g_in, g))

    def x_copy(index):
        source, target = loads[index]
        return pltpu.make_async_copy(source, target, x_sem.at[index])

    kinds = ((dg_in, per_wide), (du_in, per_wide), (db_in, per_narrow), (dq_in, per_narrow), (dk_in, per_narrow), (dv_in, per_narrow))

    def each_load(j, act):
        slot = lax.rem(j, 2)
        base = 0
        for index, (source, parts) in enumerate(kinds):
            @pl.when((j >= base) & (j < base + parts))
            def _(source=source, base=base, index=index):
                lanes = pl.ds(pl.multiple_of((j - base) * CHUNK, CHUNK), CHUNK)
                target = dy.at[slot] if index >= 4 else dy.at[slot, :, own]
                act(pltpu.make_async_copy(source.at[:, :, lanes], target, dy_sem.at[slot]))
            base += parts
        return base

    x_copy(0).start()
    each_load(jnp.int32(0), lambda copy: copy.start())
    for index in range(1, 5):
        x_copy(index).start()

    kv_first = 2 * per_wide + 2 * per_narrow
    kv_last = kv_first + 2 * per_narrow
    narrow_first = 2 * per_wide

    def compute_m(j):
        slot, held = lax.rem(j, 2), lax.rem(j, LAG + 1)

        @pl.when(j + 1 < kv_last)
        def _():
            each_load(j + 1, lambda copy: copy.start())

        def write(left, right):
            product = dot_tn(left.reshape(-1, width), right.reshape(-1, CHUNK))
            ladder_m.dw[held] = product.reshape(ladder_m.dw.shape[1:])

        @pl.when(j < kv_last)
        def _():
            each_load(j, lambda copy: copy.wait())

        @pl.when(j < narrow_first)
        def _():
            write(n2[...], dy[slot, :, own, :])

        @pl.when((j >= narrow_first) & (j < narrow_first + per_narrow))
        def _():
            write(att[...], dy[slot, :, own, :])

        @pl.when((j >= narrow_first + per_narrow) & (j < kv_first))
        def _():
            write(normed[:, own, :], dy[slot, :, own, :])

        @pl.when((j >= kv_first) & (j < kv_last))
        def _():
            write(normed[...], dy[slot])

        @pl.when(j == kv_last)
        def _():
            first = jnp.sum(gains[0:8, :], axis=0, keepdims=True)
            second = jnp.sum(gains[8:16, :], axis=0, keepdims=True)
            row = lax.broadcasted_iota(jnp.int32, (LANES, width), 0)
            placed = jnp.where(row == 0, first, jnp.where(row == 1, second, 0.0))
            columns = placed.T
            ladder_m.dw[held] = jnp.concatenate([columns, columns], axis=1).reshape(ladder_m.dw.shape[1:])

    def compute_d(j):
        held = lax.rem(j, LAG + 1)
        lanes = pl.ds(pl.multiple_of(j * LANES, LANES), LANES)
        product = dot_tn(prod[...].reshape(-1, hidden_width), g[:, :, lanes].reshape(-1, LANES))
        ladder_d.dw[held] = product.reshape(ladder_d.dw.shape[1:])

    def on_chunk(s, act_m, act_d):
        @pl.when((s >= 0) & (s < narrow_first))
        def _():
            act_m(s)

        @pl.when((s >= narrow_first) & (s < narrow_first + d_count))
        def _():
            act_d(s - narrow_first)

        @pl.when((s >= narrow_first + d_count) & (s < m_count + d_count))
        def _():
            act_m(s - d_count)

    def both(s, name):
        on_chunk(s, getattr(ladder_m, name), getattr(ladder_d, name))

    def step(s, carry):
        for index, first_step in enumerate((0, narrow_first + d_count, narrow_first + d_count + per_narrow)):
            @pl.when(s == first_step)
            def _(index=index):
                x_copy(index).wait()

        @pl.when(s == narrow_first)
        def _():
            x_copy(3).wait()
            x_copy(4).wait()

        on_chunk(s, compute_m, compute_d)
        both(s, "stage_a")
        both(s - LAG, "stage_b")
        both(s - 2 * LAG, "stage_c")
        both(s - 3 * LAG, "stage_d")
        return carry

    lax.fori_loop(0, m_count + d_count + 3 * LAG, step, 0)
    ladder_m.drain(m_count)
    ladder_d.drain(d_count)


def run_weights(normed, att, n2, prod, g, db, dg, du, dq, dk, dv, gains, count):
    batches, rows, width = g.shape
    hidden_width = prod.shape[2]
    outer = count // 4
    m_count = 2 * (hidden_width // CHUNK) + 4 * (width // CHUNK) + 1
    d_count = width // LANES

    def ladder(chunks, block):
        refs = [
            pltpu.VMEM((LAG + 1, count) + block, F32),
            pltpu.VMEM((SENDS, count // 2) + block, BF16),
            pltpu.VMEM((chunks, count // 2) + block, BF16),
            pltpu.VMEM((SENDS, outer) + block, BF16),
            pltpu.VMEM((LAG + 1, outer) + block, F32),
            pltpu.VMEM((chunks, outer) + block, BF16),
            pltpu.VMEM((SENDS, outer) + block, BF16),
            pltpu.VMEM((LAG + 1,) + block, F32),
            pltpu.VMEM((chunks, outer) + block, BF16),
        ]
        sems = [
            pltpu.SemaphoreType.DMA((SENDS,)),
            pltpu.SemaphoreType.DMA((chunks,)),
            pltpu.SemaphoreType.DMA((SENDS,)),
            pltpu.SemaphoreType.DMA((chunks,)),
            pltpu.SemaphoreType.DMA((SENDS, outer)),
            pltpu.SemaphoreType.DMA((chunks, outer)),
        ]
        return refs, sems

    block_m, block_d = (width // count, CHUNK), (hidden_width // count, LANES)
    m_refs, m_sems = ladder(m_count, block_m)
    d_refs, d_sems = ladder(d_count, block_d)
    return pl.pallas_call(
        weight_kernel,
        out_shape=[
            jax.ShapeDtypeStruct((m_count,) + block_m, F32),
            jax.ShapeDtypeStruct((d_count,) + block_d, F32),
        ],
        in_specs=[any_spec()] * 11 + [vmem_spec()],
        out_specs=[vmem_spec()] * 2,
        scratch_shapes=[
            pltpu.VMEM(normed.shape, BF16),
            pltpu.VMEM(att.shape, BF16),
            pltpu.VMEM(n2.shape, BF16),
            pltpu.VMEM(prod.shape, BF16),
            pltpu.VMEM(g.shape, BF16),
            pltpu.VMEM((2, batches, 2 * rows, CHUNK), BF16),
        ] + m_refs + d_refs + m_sems + d_sems + [
            pltpu.SemaphoreType.DMA((5,)),
            pltpu.SemaphoreType.DMA((2,)),
        ],
        compiler_params=pltpu.CompilerParams(
            collective_id=3, has_side_effects=True, vmem_limit_bytes=VMEM_BYTES),
        name="weights",
    )(normed, att, n2, prod, g, db, dg, du, dq, dk, dv, gains)


def summed_weights(normed, att, n2, prod, g, db, dg, du, dq, dk, dv, gains):
    def outer_sum(left, right):
        total = lax.dot_general(
            left, right, (((0, 1), (0, 1)), ((), ())), preferred_element_type=F32)
        return lax.psum_scatter(total[None], "wide", scatter_dimension=1, tiled=True)

    rows = g.shape[1]
    normed_own = normed[:, rows:]
    gain_rows = gains.reshape(2, 8, -1).sum(axis=1)
    gain_parts = [
        lax.psum_scatter(gain_rows[i:i + 1], "wide", scatter_dimension=1, tiled=True) for i in range(2)]
    return (
        outer_sum(normed_own, dq), outer_sum(normed, dk), outer_sum(normed, dv), outer_sum(att, db),
        outer_sum(n2, dg), outer_sum(n2, du), outer_sum(prod, g), *gain_parts,
    )


def arrange_kernel(sizes, block, grads, chunks_m, chunks_d, block_out, grad_out, *rest):
    outs, gains, gain_sem, sem = rest[:9], rest[9], rest[10], rest[11]
    base, copies = 0, []
    for size, index in zip(sizes, (4, 5, 3, 0, 1, 2)):
        for part in range(size):
            copies.append((chunks_m.at[base + part], outs[index].at[0, :, pl.ds(part * CHUNK, CHUNK)]))
        base += size
    for part in range(chunks_d.shape[0]):
        copies.append((chunks_d.at[part], outs[6].at[0, :, pl.ds(part * LANES, LANES)]))
    copies += [(block, block_out.at[0]), (grads, grad_out.at[0])]
    started = [pltpu.make_async_copy(source, target, sem.at[index]) for index, (source, target) in enumerate(copies)]
    gain_copy = pltpu.make_async_copy(chunks_m.at[base, :, pl.ds(0, LANES)], gains, gain_sem.at[0])
    gain_copy.start()
    for copy in reversed(started):
        copy.start()
    gain_copy.wait()
    turned = gains[...].T
    outs[7][...] = turned[0:1, :]
    outs[8][...] = turned[1:2, :]
    for copy in started:
        copy.wait()


def arrange(block, grads, chunks_m, chunks_d, sizes):
    own, own_d = chunks_m.shape[1], chunks_d.shape[1]
    width, hidden_width = block.shape[2], CHUNK * sizes[0]
    shapes = [(1,) + block.shape] * 2
    narrow, broad = (1, own, width), (1, own, hidden_width)
    matrices = [narrow] * 4 + [broad] * 2 + [(1, own_d, width)]
    out_shape = [jax.ShapeDtypeStruct(shape, BF16) for shape in shapes]
    out_shape += [jax.ShapeDtypeStruct(shape, F32) for shape in matrices + [(1, own)] * 2]
    copies = sum(sizes) + chunks_d.shape[0] + 2
    return pl.pallas_call(
        functools.partial(arrange_kernel, sizes),
        out_shape=out_shape,
        in_specs=[any_spec()] * 4,
        out_specs=[any_spec()] * 9 + [vmem_spec()] * 2,
        scratch_shapes=[
            pltpu.VMEM((own, LANES), F32),
            pltpu.SemaphoreType.DMA((1,)),
            pltpu.SemaphoreType.DMA((copies,)),
        ],
        compiler_params=pltpu.CompilerParams(vmem_limit_bytes=VMEM_BYTES),
        name="arrange",
    )(block, grads, chunks_m, chunks_d)


def weight_grads(block_out, input_grads, normed, att, n2, prod, g, db, dg, du, dq, dk, dv, gains):
    count = lax.axis_size("wide")
    width, hidden_width = g.shape[2], prod.shape[2]
    if count % 4 or width % (16 * count) or hidden_width % (16 * count):
        grads = summed_weights(normed, att, n2, prod, g, db, dg, du, dq, dk, dv, gains)
        return (block_out[None], input_grads[None], *grads)
    out_m, out_d = run_weights(normed, att, n2, prod, g, db, dg, du, dq, dk, dv, gains, count)
    sizes = (hidden_width // CHUNK,) * 2 + (width // CHUNK,) * 4
    return tuple(arrange(block_out, input_grads, out_m, out_d, sizes))


def per_device(
    tokens, cotangent, seg_lengths, w_query, w_key, w_value, w_output, w_gate, w_up, w_down, gain_attn, gain_mlp,
):
    weights = (w_query, w_key, w_value, w_output, w_gate, w_up, w_down)
    lengths = seg_lengths.reshape(seg_lengths.shape[0], -1)
    (block_out, input_grads, normed, att, n2, prod, g, db, dg, du, dq, dk, dv, gains) = run_layers(
        tokens, cotangent, lengths, weights, gain_attn, gain_mlp)
    return weight_grads(block_out, input_grads, normed, att, n2, prod, g, db, dg, du, dq, dk, dv, gains)


def solution(mesh):
    in_specs = (
        P(None, "wide", None),
        P(None, "wide", None),
        P(),
        *[P("section", None, None)] * 7,
        *[P("section", None)] * 2,
    )
    out_specs = (
        *[P("section", None, "wide", None)] * 2,
        *[P("section", "wide", None)] * 7,
        *[P("section", "wide")] * 2,
    )
    return jax.shard_map(
        per_device, mesh=mesh, in_specs=in_specs, out_specs=out_specs, check_vma=False
    )
```

time: 329 us -> 396 us (1.20)
  Pallas kernels: 307 us -> 395 us
  local copies, waits for them, and re-layouts: 13.3 us -> 0 us
  other arithmetic: 8.2 us -> 0 us
    pallas_call x2, Pallas kernels: 204 us -> 291 us  [the longest x1 151 us: arrange(): pl.pallas_call(functools.partial(arrange_kernel, sizes), out_shape=out_sh...]
    mul x1 -> x0, other arithmetic: 5.51 us -> none  [per_device(): cosine, sine = (jnp.cos(angles), jnp.sin(angles) * sign)]
    reshape x6 -> x0, local copies, waits for them, and re-layouts: 4.67 us -> none  [spread(): return chunks.transpose(1, 0, 2).reshape(1, chunks.shape[1], -1)]
    unnamed x9 -> x0, local copies, waits for them, and re-layouts: 4.04 us -> none
where the time goes in v2:
time: 396 us; the launch traced here: 395 us
  Pallas kernels  395 us (100%)
    pallas_call x1, Pallas kernels, arrange(): pl.pallas_call(functools.partial(arrange_kernel, sizes), out_shape=out_sh...  151 us
    pallas_call x1, Pallas kernels, run_layers(): pl.pallas_call(layers_kernel, out_shape=[jax.ShapeDtypeStruct(shape, dtyp...  140 us
    pallas_call x1, Pallas kernels, run_weights(): pl.pallas_call(weight_kernel, out_shape=[jax.ShapeDtypeStruct((m_count,)...  103 us

profile of v2, /device:TPU:0, one launch (start us, length us, event | category | flops | bytes accessed | tf_op | source)
XLA Modules:
  0.0 395.5 jit_solution(17852609748694632713)
XLA Ops:
  0.6 140.3 %layers.1 = (bf16[4,256,768]{2,1,0:T(8,128)(2,1)}, bf16[4,256,768]{2,1,0:T(8,128)(2,1)}, bf16[4,512,768]{2,1,0:T(8,128)(2,1)}, bf16[4,256,768]{2,1,0:T(8,128)(2,...) custom-call(bf16[4,256,768]{2,1,0:T(8,128)(2,1)} %tokens.1, ...), custom_call_target="tpu_custom_call" | custom-call | tf_op jit(solution)/shard_map/layers/pallas_call | solution.py:621
  140.9 103.5 %weights.1 = (f32[29,48,256]{2,1,0:T(8,128)}, f32[6,128,128]{2,1,0:T(8,128)}) custom-call(bf16[4,512,768]{2,1,0:T(8,128)(2,1)} %get-tuple-element.29.normed_in, bf16[4,256,768]{2,1,0:T(8,128)(2,1)} %get-tuple-element.30.att_in, bf16[4,256,768]{2,1,0:T(8,128)(2,1)} %get-tuple-element.31.n2_in, bf16[4,256,2048]{2,1,0:T(8,128)(2,1)} %get-tuple-element.32.prod_in, ...), custom_call_target="tpu_custom_call" | custom-call | tf_op jit(solution)/shard_map/weights/pallas_call | solution.py:900
  244.4 150.9 %arrange.1 = (bf16[1,4,256,768]{3,2,1,0:T(8,128)(2,1)}, bf16[1,4,256,768]{3,2,1,0:T(8,128)(2,1)}, f32[1,48,768]{2,1,0:T(8,128)}, f32[1,48,768]{2,1,0:T(8,128)}, ...) custom-call(bf16[4,256,768]{2,1,0:T(8,128)(2,1)} %get-tuple-element., ...), custom_call_target="tpu_custom_call" | custom-call | tf_op jit(solution)/shard_map/arrange/pallas_call | solution.py:974

commit v3 on v2

--- a/solution.py
+++ b/solution.py
@@ -630,8 +630,10 @@
     )(tokens, cotangent, lengths, *weights, gain_attn, gain_mlp, trig)
 
 
-LAG = 2
+LAG = 3
 SENDS = 4
+LENT = 4
+MIX = 5
 CHUNK = 256
 
 
@@ -642,7 +644,8 @@
 
 
 class Ladder:
-    def __init__(self, refs, sems, outer):
+    def __init__(self, refs, sems, outer, chunks):
+        self.computed = chunks
         self.dw, self.a_out, self.a_in, self.b_out, self.b_own, self.b_in, self.c_out, self.c_own, self.c_in, self.result = refs
         self.a_send, self.a_recv, self.b_send, self.b_recv, self.c_send, self.c_recv = sems
         wide = lax.axis_index("wide")
@@ -651,6 +654,36 @@
         self.core_mate = {"wide": wide + 1 - 2 * self.core}
         self.side_mate = {"wide": wide + 2 - 4 * self.side}
         self.column = lax.rem(wide, 4)
+        self.first, self.count = 0, chunks
+        self.lent = None
+
+    def lend(self, refs, sems, section):
+        self.x_out, self.x_in, self.r_out, self.r_in = refs
+        self.x_send, self.x_recv, self.r_send, self.r_recv = sems
+        self.lender = section == 0
+        self.lent = self.x_in.shape[0]
+        self.partner = {"section": 1 - section}
+        self.first = jnp.where(self.lender, self.lent, 0)
+        self.count = jnp.where(self.lender, self.computed, self.computed + self.lent)
+
+    def x_copy(self, j):
+        return pltpu.make_async_remote_copy(
+            self.x_out.at[j], self.x_in.at[j], self.x_send.at[j], self.x_recv.at[j],
+            device_id=self.partner, device_id_type=MESH)
+
+    def r_copy(self, j):
+        return pltpu.make_async_remote_copy(
+            self.r_out.at[j], self.r_in.at[j], self.r_send.at[j], self.r_recv.at[j],
+            device_id=self.partner, device_id_type=MESH)
+
+    def stage_x(self, j):
+        held = lax.rem(j, LAG + 1)
+
+        self.a_copy(j).wait_recv()
+        for index in range(2 * self.outer):
+            self.x_out[j, index] = (
+                self.dw[held, 2 * index + self.core] + self.a_in[j, index].astype(F32)).astype(BF16)
+        self.x_copy(j).start()
 
     def a_copy(self, j):
         slot = lax.rem(j, SENDS)
@@ -686,22 +719,37 @@
     def stage_b(self, j):
         slot, held = lax.rem(j, SENDS), lax.rem(j, LAG + 1)
 
-        @pl.when(j >= SENDS)
+        @pl.when(j >= SENDS + self.first)
         def _():
             self.b_copy(j - SENDS).wait_send()
 
-        self.a_copy(j).wait_recv()
-        for index in range(self.outer):
-            far, near = 2 * index + 1 - self.side, 2 * index + self.side
-            self.b_out[slot, index] = (
-                self.dw[held, 2 * far + self.core] + self.a_in[j, far].astype(F32)).astype(BF16)
-            self.b_own[held, index] = self.dw[held, 2 * near + self.core] + self.a_in[j, near].astype(F32)
+        def split():
+            self.a_copy(j).wait_recv()
+            for index in range(self.outer):
+                far, near = 2 * index + 1 - self.side, 2 * index + self.side
+                self.b_out[slot, index] = (
+                    self.dw[held, 2 * far + self.core] + self.a_in[j, far].astype(F32)).astype(BF16)
+                self.b_own[held, index] = self.dw[held, 2 * near + self.core] + self.a_in[j, near].astype(F32)
+
+        if self.lent is None:
+            split()
+        else:
+            pl.when(j < self.computed)(split)
+
+            @pl.when(j >= self.computed)
+            def _():
+                borrowed = j - self.computed
+                self.x_copy(borrowed).wait_recv()
+                for index in range(self.outer):
+                    self.b_out[slot, index] = self.x_in[borrowed, 2 * index + 1 - self.side]
+                    self.b_own[held, index] = self.x_in[borrowed, 2 * index + self.side].astype(F32)
+
         self.b_copy(j).start()
 
     def stage_c(self, j):
         slot, held = lax.rem(j, SENDS), lax.rem(j, LAG + 1)
 
-        @pl.when(j >= SENDS)
+        @pl.when(j >= SENDS + self.first)
         def _():
             for step in range(1, self.outer):
                 self.c_copy(j - SENDS, step, False).wait_send()
@@ -720,14 +768,46 @@
             self.c_copy(j, step, True).wait_recv()
         for step in range(1, self.outer):
             total = total + self.c_in[j, lax.rem(self.depth + step, self.outer)].astype(F32)
-        self.result[j] = total
-
-    def drain(self, count):
-        for j in range(max(0, count - SENDS), count):
-            self.a_copy(j).wait_send()
-            self.b_copy(j).wait_send()
-            for step in range(1, self.outer):
-                self.c_copy(j, step, False).wait_send()
+        if self.lent is None:
+            self.result[j] = total
+            return
+
+        @pl.when(j < self.computed)
+        def _():
+            self.result[j] = total
+
+        @pl.when(j >= self.computed)
+        def _():
+            @pl.when(j == self.computed)
+            def _():
+                pl.semaphore_wait(pltpu.get_barrier_semaphore(), 1)
+
+            self.r_out[j - self.computed] = total
+            self.r_copy(j - self.computed).start()
+
+    def drain(self):
+        for back in range(1, SENDS + 1):
+            self.a_copy(self.computed - back).wait_send()
+            j = self.count - back
+
+            @pl.when(j >= self.first)
+            def _(j=j):
+                self.b_copy(j).wait_send()
+                for step in range(1, self.outer):
+                    self.c_copy(j, step, False).wait_send()
+
+        if self.lent is not None:
+            @pl.when(self.lender)
+            def _():
+                for j in range(self.lent):
+                    self.x_copy(j).wait_send()
+                    self.r_copy(j).wait_recv()
+                    self.result[j] = self.r_in[j]
+
+            @pl.when(jnp.logical_not(self.lender))
+            def _():
+                for j in range(self.lent):
+                    self.r_copy(j).wait_send()
 
 
 def weight_kernel(
@@ -735,21 +815,20 @@
     out_m, out_d,
     normed, att, n2, prod, g, dy, *rest,
 ):
-    m_refs, d_refs = rest[:9], rest[9:18]
-    m_sems, d_sems = rest[18:24], rest[24:30]
-    x_sem, dy_sem = rest[30], rest[31]
-    wide, count = lax.axis_index("wide"), lax.axis_size("wide")
+    m_refs, d_refs, lend_refs = rest[:9], rest[9:18], rest[18:22]
+    m_sems, d_sems, lend_sems = rest[22:28], rest[28:34], rest[34:38]
+    x_sem, dy_sem = rest[38], rest[39]
+    section, wide, count = lax.axis_index("section"), lax.axis_index("wide"), lax.axis_size("wide")
     batches, rows, width = g_in.shape
     hidden_width = prod_in.shape[2]
     outer = count // 4
     own = pl.ds(rows, rows)
     m_count, d_count = out_m.shape[0], out_d.shape[0]
     per_wide, per_narrow = hidden_width // CHUNK, width // CHUNK
-    ladder_m = Ladder(m_refs + (out_m,), m_sems, outer)
-    ladder_d = Ladder(d_refs + (out_d,), d_sems, outer)
+    ladder_m = Ladder(m_refs + (out_m,), m_sems, outer, m_count)
+    ladder_d = Ladder(d_refs + (out_d,), d_sems, outer, d_count)
+    ladder_d.lend(lend_refs, lend_sems, section)
     true = wide >= 0
-    meet([(true, ladder_m.core_mate), (true, ladder_m.side_mate)] + [
-        (true, {"wide": lax.rem(ladder_m.depth + step, outer) * 4 + ladder_m.column}) for step in range(1, outer)])
 
     loads = ((n2_in, n2), (att_in, att), (normed_in, normed), (prod_in, prod), (g_in, g))
 
@@ -773,8 +852,15 @@
 
     x_copy(0).start()
     each_load(jnp.int32(0), lambda copy: copy.start())
-    for index in range(1, 5):
+    for index in (3, 4, 1, 2):
         x_copy(index).start()
+    barrier = pltpu.get_barrier_semaphore()
+    peers = [ladder_m.core_mate, ladder_m.side_mate] + [
+        {"wide": lax.rem(ladder_m.depth + step, outer) * 4 + ladder_m.column} for step in range(1, outer)]
+    for peer in peers:
+        pl.semaphore_signal(barrier, inc=1, device_id=peer, device_id_type=MESH)
+    pl.semaphore_wait(barrier, len(peers) + ladder_d.lender.astype(jnp.int32))
+    pl.semaphore_signal(barrier, inc=1, device_id=ladder_d.partner, device_id_type=MESH)
 
     kv_first = 2 * per_wide + 2 * per_narrow
     kv_last = kv_first + 2 * per_narrow
@@ -794,6 +880,11 @@
         @pl.when(j < kv_last)
         def _():
             each_load(j, lambda copy: copy.wait())
+
+        for index, first in enumerate((0, narrow_first, narrow_first + per_narrow)):
+            @pl.when(j == first)
+            def _(index=index):
+                x_copy(index).wait()
 
         @pl.when(j < narrow_first)
         def _():
@@ -822,47 +913,64 @@
 
     def compute_d(j):
         held = lax.rem(j, LAG + 1)
+
+        @pl.when(j == 0)
+        def _():
+            x_copy(3).wait()
+            x_copy(4).wait()
+
         lanes = pl.ds(pl.multiple_of(j * LANES, LANES), LANES)
         product = dot_tn(prod[...].reshape(-1, hidden_width), g[:, :, lanes].reshape(-1, LANES))
         ladder_d.dw[held] = product.reshape(ladder_d.dw.shape[1:])
 
+    lent = ladder_d.lent
+    lender = ladder_d.lender
+
     def on_chunk(s, act_m, act_d):
-        @pl.when((s >= 0) & (s < narrow_first))
-        def _():
-            act_m(s)
-
-        @pl.when((s >= narrow_first) & (s < narrow_first + d_count))
-        def _():
-            act_d(s - narrow_first)
-
-        @pl.when((s >= narrow_first + d_count) & (s < m_count + d_count))
-        def _():
-            act_m(s - d_count)
-
-    def both(s, name):
-        on_chunk(s, getattr(ladder_m, name), getattr(ladder_d, name))
+        mixed = s < MIX * lent
+        turn, place = s // MIX, lax.rem(s, MIX)
+        j_lender = jnp.where(mixed, (MIX - 1) * turn + place, s - lent)
+        d_lender = jnp.where(mixed, turn, s - m_count)
+        m_turn = jnp.where(lender & mixed, place < MIX - 1, True)
+        j_m = jnp.where(lender, j_lender, s)
+        j_d = jnp.where(lender, d_lender, s - m_count)
+        last_d = ladder_d.count
+        is_m = (s >= 0) & (j_m < m_count) & m_turn
+        is_d = (s >= 0) & jnp.where(lender & mixed, place == MIX - 1, j_m >= m_count) & (j_d < last_d)
+
+        @pl.when(is_m)
+        def _():
+            act_m(j_m)
+
+        @pl.when(is_d)
+        def _():
+            act_d(j_d)
+
+    def own_d(act):
+        def guarded(j):
+            pl.when(j < d_count)(lambda: act(j))
+        return guarded
+
+    def reduced_d(act):
+        def guarded(j):
+            pl.when(j >= ladder_d.first)(lambda: act(j))
+        return guarded
+
+    def second(j):
+        pl.when(j < ladder_d.first)(lambda: ladder_d.stage_x(j))
+        pl.when(j >= ladder_d.first)(lambda: ladder_d.stage_b(j))
 
     def step(s, carry):
-        for index, first_step in enumerate((0, narrow_first + d_count, narrow_first + d_count + per_narrow)):
-            @pl.when(s == first_step)
-            def _(index=index):
-                x_copy(index).wait()
-
-        @pl.when(s == narrow_first)
-        def _():
-            x_copy(3).wait()
-            x_copy(4).wait()
-
-        on_chunk(s, compute_m, compute_d)
-        both(s, "stage_a")
-        both(s - LAG, "stage_b")
-        both(s - 2 * LAG, "stage_c")
-        both(s - 3 * LAG, "stage_d")
+        on_chunk(s, compute_m, own_d(compute_d))
+        on_chunk(s, ladder_m.stage_a, own_d(ladder_d.stage_a))
+        on_chunk(s - LAG, ladder_m.stage_b, second)
+        on_chunk(s - 2 * LAG, ladder_m.stage_c, reduced_d(ladder_d.stage_c))
+        on_chunk(s - 3 * LAG, ladder_m.stage_d, reduced_d(ladder_d.stage_d))
         return carry
 
-    lax.fori_loop(0, m_count + d_count + 3 * LAG, step, 0)
-    ladder_m.drain(m_count)
-    ladder_d.drain(d_count)
+    lax.fori_loop(0, m_count + d_count + lent + 3 * LAG, step, 0)
+    ladder_m.drain()
+    ladder_d.drain()
 
 
 def run_weights(normed, att, n2, prod, g, db, dg, du, dq, dk, dv, gains, count):
@@ -872,31 +980,39 @@
     m_count = 2 * (hidden_width // CHUNK) + 4 * (width // CHUNK) + 1
     d_count = width // LANES
 
-    def ladder(chunks, block):
+    def ladder(chunks, lent, block):
+        total = chunks + lent
         refs = [
             pltpu.VMEM((LAG + 1, count) + block, F32),
             pltpu.VMEM((SENDS, count // 2) + block, BF16),
             pltpu.VMEM((chunks, count // 2) + block, BF16),
             pltpu.VMEM((SENDS, outer) + block, BF16),
             pltpu.VMEM((LAG + 1, outer) + block, F32),
-            pltpu.VMEM((chunks, outer) + block, BF16),
+            pltpu.VMEM((total, outer) + block, BF16),
             pltpu.VMEM((SENDS, outer) + block, BF16),
             pltpu.VMEM((LAG + 1,) + block, F32),
-            pltpu.VMEM((chunks, outer) + block, BF16),
+            pltpu.VMEM((total, outer) + block, BF16),
         ]
         sems = [
             pltpu.SemaphoreType.DMA((SENDS,)),
             pltpu.SemaphoreType.DMA((chunks,)),
             pltpu.SemaphoreType.DMA((SENDS,)),
-            pltpu.SemaphoreType.DMA((chunks,)),
+            pltpu.SemaphoreType.DMA((total,)),
             pltpu.SemaphoreType.DMA((SENDS, outer)),
-            pltpu.SemaphoreType.DMA((chunks, outer)),
+            pltpu.SemaphoreType.DMA((total, outer)),
         ]
         return refs, sems
 
     block_m, block_d = (width // count, CHUNK), (hidden_width // count, LANES)
-    m_refs, m_sems = ladder(m_count, block_m)
-    d_refs, d_sems = ladder(d_count, block_d)
+    m_refs, m_sems = ladder(m_count, 0, block_m)
+    d_refs, d_sems = ladder(d_count, LENT, block_d)
+    lend_refs = [
+        pltpu.VMEM((LENT, count // 2) + block_d, BF16),
+        pltpu.VMEM((LENT, count // 2) + block_d, BF16),
+        pltpu.VMEM((LENT,) + block_d, F32),
+        pltpu.VMEM((LENT,) + block_d, F32),
+    ]
+    lend_sems = [pltpu.SemaphoreType.DMA((size,)) for size in (LENT,) * 4]
     return pl.pallas_call(
         weight_kernel,
         out_shape=[
@@ -912,7 +1028,7 @@
             pltpu.VMEM(prod.shape, BF16),
             pltpu.VMEM(g.shape, BF16),
             pltpu.VMEM((2, batches, 2 * rows, CHUNK), BF16),
-        ] + m_refs + d_refs + m_sems + d_sems + [
+        ] + m_refs + d_refs + lend_refs + m_sems + d_sems + lend_sems + [
             pltpu.SemaphoreType.DMA((5,)),
             pltpu.SemaphoreType.DMA((2,)),
         ],
@@ -940,25 +1056,36 @@
 
 
 def arrange_kernel(sizes, block, grads, chunks_m, chunks_d, block_out, grad_out, *rest):
-    outs, gains, gain_sem, sem = rest[:9], rest[9], rest[10], rest[11]
-    base, copies = 0, []
+    outs, (held_block, held_grads, held_m, held_d), (load_sem, store_sem) = rest[:9], rest[9:13], rest[13:]
+    batches = block.shape[0]
+    loads, stores = [], []
+    for mb in range(batches):
+        loads += [(block.at[mb], held_block.at[mb]), (grads.at[mb], held_grads.at[mb])]
+        stores += [(held_block.at[mb], block_out.at[0, mb]), (held_grads.at[mb], grad_out.at[0, mb])]
+    first_load = len(loads)
+    loads += [(chunks_m, held_m), (chunks_d, held_d)]
+    base = 0
     for size, index in zip(sizes, (4, 5, 3, 0, 1, 2)):
         for part in range(size):
-            copies.append((chunks_m.at[base + part], outs[index].at[0, :, pl.ds(part * CHUNK, CHUNK)]))
+            stores.append((held_m.at[base + part], outs[index].at[0, :, pl.ds(part * CHUNK, CHUNK)]))
         base += size
     for part in range(chunks_d.shape[0]):
-        copies.append((chunks_d.at[part], outs[6].at[0, :, pl.ds(part * LANES, LANES)]))
-    copies += [(block, block_out.at[0]), (grads, grad_out.at[0])]
-    started = [pltpu.make_async_copy(source, target, sem.at[index]) for index, (source, target) in enumerate(copies)]
-    gain_copy = pltpu.make_async_copy(chunks_m.at[base, :, pl.ds(0, LANES)], gains, gain_sem.at[0])
-    gain_copy.start()
-    for copy in reversed(started):
+        stores.append((held_d.at[part], outs[6].at[0, :, pl.ds(part * LANES, LANES)]))
+    loads = [pltpu.make_async_copy(*pair, load_sem.at[index]) for index, pair in enumerate(loads)]
+    stores = [pltpu.make_async_copy(*pair, store_sem.at[index]) for index, pair in enumerate(stores)]
+    for copy in loads:
         copy.start()
-    gain_copy.wait()
-    turned = gains[...].T
+    for index in range(first_load):
+        loads[index].wait()
+        stores[index].start()
+    for copy in loads[first_load:]:
+        copy.wait()
+    for copy in stores[first_load:]:
+        copy.start()
+    turned = held_m[base, :, :LANES].T
     outs[7][...] = turned[0:1, :]
     outs[8][...] = turned[1:2, :]
-    for copy in started:
+    for copy in stores:
         copy.wait()
 
 
@@ -970,17 +1097,14 @@
     matrices = [narrow] * 4 + [broad] * 2 + [(1, own_d, width)]
     out_shape = [jax.ShapeDtypeStruct(shape, BF16) for shape in shapes]
     out_shape += [jax.ShapeDtypeStruct(shape, F32) for shape in matrices + [(1, own)] * 2]
-    copies = sum(sizes) + chunks_d.shape[0] + 2
+    copies = sum(sizes) + chunks_d.shape[0] + 2 * block.shape[0]
     return pl.pallas_call(
         functools.partial(arrange_kernel, sizes),
         out_shape=out_shape,
         in_specs=[any_spec()] * 4,
         out_specs=[any_spec()] * 9 + [vmem_spec()] * 2,
-        scratch_shapes=[
-            pltpu.VMEM((own, LANES), F32),
-            pltpu.SemaphoreType.DMA((1,)),
-            pltpu.SemaphoreType.DMA((copies,)),
-        ],
+        scratch_shapes=[pltpu.VMEM(held.shape, held.dtype) for held in (block, grads, chunks_m, chunks_d)]
+        + [pltpu.SemaphoreType.DMA((2 * block.shape[0] + 2,)), pltpu.SemaphoreType.DMA((copies,))],
         compiler_params=pltpu.CompilerParams(vmem_limit_bytes=VMEM_BYTES),
         name="arrange",
     )(block, grads, chunks_m, chunks_d)

time: 396 us -> 242 us (0.61)
  Pallas kernels: 395 us -> 241 us
    pallas_call x1, Pallas kernels: 151 us -> 5.66 us  [arrange(): pl.pallas_call(functools.partial(arrange_kernel, sizes), out_shape=out_sh...]
    pallas_call x1, Pallas kernels: 103 us -> 94.7 us  [run_weights(): pl.pallas_call(weight_kernel, out_shape=[jax.ShapeDtypeStruct((m_count,)...]
where the time goes in v3:
time: 242 us; the launch traced here: 241 us
  Pallas kernels  241 us (100%)
    pallas_call x1, Pallas kernels, run_layers(): pl.pallas_call(layers_kernel, out_shape=[jax.ShapeDtypeStruct(shape, dtyp...  140 us
    pallas_call x1, Pallas kernels, run_weights(): pl.pallas_call(weight_kernel, out_shape=[jax.ShapeDtypeStruct((m_count,)...  94.7 us
    pallas_call x1, Pallas kernels, arrange(): pl.pallas_call(functools.partial(arrange_kernel, sizes), out_shape=out_sh...  5.66 us

profile of v3, /device:TPU:0, one launch (start us, length us, event | category | flops | bytes accessed | tf_op | source)
XLA Modules:
  0.0 241.5 jit_solution(868406973808298049)
XLA Ops:
  0.6 140.3 %layers.1 = (bf16[4,256,768]{2,1,0:T(8,128)(2,1)}, bf16[4,256,768]{2,1,0:T(8,128)(2,1)}, bf16[4,512,768]{2,1,0:T(8,128)(2,1)}, bf16[4,256,768]{2,1,0:T(8,128)(2,...) custom-call(bf16[4,256,768]{2,1,0:T(8,128)(2,1)} %tokens.1, ...), custom_call_target="tpu_custom_call" | custom-call | tf_op jit(solution)/shard_map/layers/pallas_call | solution.py:621
  140.9 94.7 %weights.1 = (f32[29,48,256]{2,1,0:T(8,128)}, f32[6,128,128]{2,1,0:T(8,128)}) custom-call(bf16[4,512,768]{2,1,0:T(8,128)(2,1)} %get-tuple-element.29.normed_in, bf16[4,256,768]{2,1,0:T(8,128)(2,1)} %get-tuple-element.30.att_in, bf16[4,256,768]{2,1,0:T(8,128)(2,1)} %get-tuple-element.31.n2_in, bf16[4,256,2048]{2,1,0:T(8,128)(2,1)} %get-tuple-element.32.prod_in, ...), custom_call_target="tpu_custom_call" | custom-call | tf_op jit(solution)/shard_map/weights/pallas_call | solution.py:1016
  235.6 5.7 %arrange.1 = (bf16[1,4,256,768]{3,2,1,0:T(8,128)(2,1)}, bf16[1,4,256,768]{3,2,1,0:T(8,128)(2,1)}, f32[1,48,768]{2,1,0:T(8,128)}, f32[1,48,768]{2,1,0:T(8,128)}, ...) custom-call(bf16[4,256,768]{2,1,0:T(8,128)(2,1)} %get-tuple-element., ...), custom_call_target="tpu_custom_call" | custom-call | tf_op jit(solution)/shard_map/arrange/pallas_call | solution.py:1101

commit v4 on v3

--- a/solution.py
+++ b/solution.py
@@ -18,6 +18,7 @@
 MESH = pl.DeviceIdType.MESH
 LANES = 128
 BLOCK = 64
+PIECE = 256
 VMEM_BYTES = 63 * 1024 * 1024
 
 
@@ -84,16 +85,16 @@
 
 
 def layers_kernel(
-    tokens, cotangent, lengths,
+    late, tokens, cotangent, lengths,
     w_query, w_key, w_value, w_output, w_gate, w_up, w_down,
     gain_attn, gain_mlp, trig,
     block_out, grad_out, normed_out, att_out, n2_out, prod_out,
-    g_out, db_out, dg_out, du_out, dq_out, dk_out, dv_out, gains_out,
+    g_out, db_out, dg_out, du_out, dq_out, dk_out, dv_out, own_out, halo_part_out, gains_out,
     wq, wk, wv, wo, wg, wu, wd,
     xs, qs, ks, vs, probs, slope, silu, mixed, normed, att, n2, prod, outs, gs,
     halo_in, halo_out, branch, d_att, d_norm, d_own, cosine, sine, first_key, bias, scale,
     wide_f, left_b, right_b, key_f, value_f,
-    weight_sem, trig_sem, token_sem, cot_sem, save_sem, out_sem,
+    weight_sem, trig_sem, late_sem, token_sem, cot_sem, save_sem, out_sem,
     halo_send, halo_recv, hand_send, hand_recv, back_send, back_recv, turn_send, turn_recv,
 ):
     section, wide = lax.axis_index("section"), lax.axis_index("wide")
@@ -121,25 +122,47 @@
     def cot_copy(mb):
         return pltpu.make_async_copy(cotangent.at[mb], gs.at[mb], cot_sem.at[mb])
 
-    def halo_copy(mb, source):
+    pieces = range(rows // PIECE)
+
+    def rows_of(piece, base=0):
+        return pl.ds(base + piece * PIECE, PIECE)
+
+    def halo_copy(mb, piece, source):
         return pltpu.make_async_remote_copy(
-            source, xs.at[mb, halo], halo_send.at[mb], halo_recv.at[mb],
+            source, xs.at[mb, rows_of(piece)], halo_send.at[mb, piece], halo_recv.at[mb, piece],
             device_id={"wide": wide + 1}, device_id_type=MESH)
 
-    def hand_copy(mb):
+    def own_halo_copy(mb, piece):
+        return halo_copy(mb, piece, xs.at[mb, rows_of(piece, rows)])
+
+    def token_halo_copy(mb, piece):
+        return halo_copy(mb, piece, tokens.at[mb, rows_of(piece)])
+
+    def hand_copy(mb, piece):
         return pltpu.make_async_remote_copy(
-            outs.at[mb], xs.at[mb, own], hand_send.at[mb], hand_recv.at[mb],
+            outs.at[mb, rows_of(piece)], xs.at[mb, rows_of(piece, rows)],
+            hand_send.at[mb, piece], hand_recv.at[mb, piece],
             device_id={"section": section + 1}, device_id_type=MESH)
 
-    def back_copy(mb):
+    def back_copy(mb, piece):
         return pltpu.make_async_remote_copy(
-            halo_out, halo_in.at[mb], back_send.at[mb], back_recv.at[mb],
+            halo_out.at[rows_of(piece)], halo_in.at[mb, rows_of(piece)],
+            back_send.at[mb, piece], back_recv.at[mb, piece],
             device_id={"wide": wide - 1}, device_id_type=MESH)
 
-    def turn_copy(mb):
+    def turn_copy(mb, piece):
         return pltpu.make_async_remote_copy(
-            outs.at[mb], gs.at[mb], turn_send.at[mb], turn_recv.at[mb],
+            outs.at[mb, rows_of(piece)], gs.at[mb, rows_of(piece)],
+            turn_send.at[mb, piece], turn_recv.at[mb, piece],
             device_id={"section": section - 1}, device_id_type=MESH)
+
+    def relay(mb):
+        for piece in pieces:
+            hand_copy(mb, piece).wait_recv()
+
+            @pl.when(has_right)
+            def _(piece=piece):
+                own_halo_copy(mb, piece).start()
 
     def out_copy(mb, target):
         return pltpu.make_async_copy(outs.at[mb], target.at[mb], out_sem.at[mb])
@@ -174,7 +197,8 @@
 
     @pl.when(is_first & has_right)
     def _():
-        halo_copy(0, tokens.at[0]).start()
+        for piece in pieces:
+            token_halo_copy(0, piece).start()
 
     @pl.when(is_first)
     def _():
@@ -189,6 +213,10 @@
     @pl.when(jnp.logical_not(has_left))
     def _():
         xs[:, halo, :] = jnp.zeros((batches, rows, width), BF16)
+
+    @pl.when(jnp.logical_not(has_right))
+    def _():
+        halo_in[...] = jnp.zeros(halo_in.shape, BF16)
 
     gains_out[...] = jnp.zeros(gains_out.shape, F32)
 
@@ -287,15 +315,12 @@
 
             @pl.when(has_right & (mb + 1 < batches))
             def _():
-                halo_copy(mb + 1, tokens.at[mb + 1]).start()
+                for piece in pieces:
+                    token_halo_copy(mb + 1, piece).start()
 
         @pl.when(has_before & (mb == 0))
         def _():
-            hand_copy(mb).wait_recv()
-
-            @pl.when(has_right)
-            def _():
-                halo_copy(mb, xs.at[mb, own]).start()
+            relay(mb)
 
         saved_before("normed", mb)
         normalise(mb, own)
@@ -322,7 +347,8 @@
 
         @pl.when(has_left)
         def _():
-            halo_copy(mb, xs.at[mb, own]).wait_recv()
+            for piece in pieces:
+                own_halo_copy(mb, piece).wait_recv()
 
         normalise(mb, halo)
         keys_values(mb, halo)
@@ -350,11 +376,7 @@
 
         @pl.when(has_before & (mb + 1 < batches))
         def _():
-            hand_copy(mb + 1).wait_recv()
-
-            @pl.when(has_right)
-            def _():
-                halo_copy(mb + 1, xs.at[mb + 1, own]).start()
+            relay(mb + 1)
 
         saved_before("prod", mb)
         for start in range(0, hidden_width, 256):
@@ -373,7 +395,8 @@
 
         @pl.when(has_after)
         def _():
-            hand_copy(mb).start()
+            for piece in pieces:
+                hand_copy(mb, piece).start()
 
         out_copy(mb, block_out).start()
         return carry
@@ -388,7 +411,8 @@
     @pl.when(has_after)
     def _():
         for mb in range(batches):
-            hand_copy(mb).wait_send()
+            for piece in pieces:
+                hand_copy(mb, piece).wait_send()
 
 
     def add_gain(which, product):
@@ -439,23 +463,26 @@
 
         pipelined(d_weights, d_soften, collect)
 
+    def closes(mb):
+        return has_before | (mb < batches - 1) if late else wide >= 0
+
     def finish(mb):
-        @pl.when(has_right)
-        def _():
-            back_copy(mb).wait_recv()
-            d_own[...] = d_own[...] + halo_in[mb].astype(F32)
-
-        for low in range(0, rows, BLOCK):
-            at = slice(low, low + BLOCK)
-            scaled, inverse = rms_parts(xs[mb, rows + low:rows + low + BLOCK, :].astype(F32))
-            d_normed = d_own[at, :]
-            add_gain(0, d_normed * scaled)
-            back = rms_back(d_normed * gain_attn[...], scaled, inverse)
-            outs[mb, at, :] = (branch[lax.rem(mb, 2), at, :].astype(F32) + back).astype(BF16)
-
-        @pl.when(has_before)
-        def _():
-            turn_copy(mb).start()
+        for piece in pieces:
+            @pl.when(has_right)
+            def _(piece=piece):
+                back_copy(mb, piece).wait_recv()
+
+            for low in range(piece * PIECE, (piece + 1) * PIECE, BLOCK):
+                at = pl.ds(low, BLOCK)
+                scaled, inverse = rms_parts(xs[mb, pl.ds(rows + low, BLOCK), :].astype(F32))
+                d_normed = d_own[at, :] + halo_in[mb, at, :].astype(F32)
+                add_gain(0, d_normed * scaled)
+                back = rms_back(d_normed * gain_attn[...], scaled, inverse)
+                outs[mb, at, :] = (branch[lax.rem(mb, 2), at, :].astype(F32) + back).astype(BF16)
+
+            @pl.when(has_before)
+            def _(piece=piece):
+                turn_copy(mb, piece).start()
 
         out_copy(mb, grad_out).start()
 
@@ -466,7 +493,8 @@
 
         @pl.when(has_after)
         def _():
-            turn_copy(mb).wait_recv()
+            for piece in pieces:
+                turn_copy(mb, piece).wait_recv()
 
         save("g", mb).start()
         for start in range(0, hidden_width, 256):
@@ -508,16 +536,18 @@
 
         @pl.when(has_left & (mb > 0))
         def _():
-            back_copy(mb - 1).wait_send()
+            for piece in pieces:
+                back_copy(mb - 1, piece).wait_send()
 
         for start in range(0, width, 256):
             at = slice(start, start + 256)
             halo_out[:, at] = (
                 dot_nt(ks[mb, halo, :], wk[at, :]) + dot_nt(vs[mb, halo, :], wv[at, :])).astype(BF16)
 
-        @pl.when(has_left)
-        def _():
-            back_copy(mb).start()
+        @pl.when(has_left & closes(mb))
+        def _():
+            for piece in pieces:
+                back_copy(mb, piece).start()
 
         for start in range(0, width, 256):
             at = slice(start, start + 256)
@@ -527,28 +557,49 @@
         return carry
 
     lax.fori_loop(0, batches, backward, 0)
-    finish(batches - 1)
+    closed = closes(batches - 1)
+
+    @pl.when(closed)
+    def _():
+        finish(batches - 1)
+
+    @pl.when(jnp.logical_not(closed))
+    def _():
+        copies = [pltpu.make_async_copy(d_own, own_out, late_sem.at[0]),
+                  pltpu.make_async_copy(halo_out, halo_part_out, late_sem.at[1])]
+        for copy in copies:
+            copy.start()
+        for copy in copies:
+            copy.wait()
 
     for mb in range(batches - 2, batches):
         save("branch", mb).wait()
     for mb in range(batches):
         for name in ("g", "dg", "du", "dq", "dk", "dv"):
             save(name, mb).wait()
+    for mb in range(batches - 1):
         out_copy(mb, grad_out).wait()
 
-    @pl.when(has_left)
-    def _():
-        back_copy(batches - 1).wait_send()
+    @pl.when(closed)
+    def _():
+        out_copy(batches - 1, grad_out).wait()
+
+    @pl.when(has_left & closed)
+    def _():
+        for piece in pieces:
+            back_copy(batches - 1, piece).wait_send()
 
     @pl.when(has_before)
     def _():
         for mb in range(batches):
-            turn_copy(mb).wait_send()
+            for piece in pieces:
+                turn_copy(mb, piece).wait_send()
 
     @pl.when(has_right)
     def _():
         for mb in range(batches):
-            halo_copy(mb, xs.at[mb, own]).wait_send()
+            for piece in pieces:
+                own_halo_copy(mb, piece).wait_send()
 
 
 def any_spec():
@@ -572,7 +623,7 @@
     return jnp.asarray(np.stack(parts))
 
 
-def run_layers(tokens, cotangent, lengths, weights, gain_attn, gain_mlp):
+def run_layers(tokens, cotangent, lengths, weights, gain_attn, gain_mlp, late=False):
     batches, rows, width = tokens.shape
     hidden_width = weights[4].shape[2]
     pairs = width // LANES
@@ -582,7 +633,7 @@
     wide = (batches, rows, hidden_width)
     outs = [(one, BF16), (one, BF16), (two, BF16), (one, BF16), (one, BF16), (wide, BF16),
             (one, BF16), (one, BF16), (wide, BF16), (wide, BF16), (one, BF16), (two, BF16), (two, BF16),
-            ((16, width), F32)]
+            (one[1:], F32), (one[1:], BF16), ((16, width), F32)]
     dma = pltpu.SemaphoreType.DMA
     scratch = [pltpu.VMEM(w.shape[1:], BF16) for w in weights] + [
         pltpu.VMEM(two, BF16),
@@ -615,14 +666,14 @@
         pltpu.VMEM((2, band, rows), BF16),
         pltpu.VMEM((2, band, LANES), F32),
         pltpu.VMEM((2, band, LANES), F32),
-        dma((7,)), dma((1,)), dma((batches,)), dma((batches,)), dma((11, batches)),
-    ] + [dma((batches,))] * 9
+        dma((7,)), dma((1,)), dma((2,)), dma((batches,)), dma((batches,)), dma((11, batches)),
+    ] + [dma((batches,))] + [dma((batches, rows // PIECE))] * 8
     trig = trig_table(width // HEADS, band)
     return pl.pallas_call(
-        layers_kernel,
+        functools.partial(layers_kernel, late),
         out_shape=[jax.ShapeDtypeStruct(shape, dtype) for shape, dtype in outs],
         in_specs=[any_spec()] * 2 + [pl.BlockSpec(memory_space=pltpu.SMEM)] + [any_spec()] * 7 + [vmem_spec()] * 2 + [any_spec()],
-        out_specs=[any_spec()] * 13 + [vmem_spec()],
+        out_specs=[any_spec()] * 15 + [vmem_spec()],
         scratch_shapes=scratch,
         compiler_params=pltpu.CompilerParams(
             collective_id=1, has_side_effects=True, vmem_limit_bytes=VMEM_BYTES),
@@ -632,8 +683,10 @@
 
 LAG = 3
 SENDS = 4
-LENT = 4
-MIX = 5
+LAG_PAIR = 1
+LENT = 3
+MIX = 6
+LATE = 8
 CHUNK = 256
 
 
@@ -811,9 +864,10 @@
 
 
 def weight_kernel(
-    normed_in, att_in, n2_in, prod_in, g_in, db_in, dg_in, du_in, dq_in, dk_in, dv_in, gains,
-    out_m, out_d,
-    normed, att, n2, prod, g, dy, *rest,
+    normed_in, att_in, n2_in, prod_in, g_in, db_in, dg_in, du_in, dq_in, dk_in, dv_in,
+    own_in, halo_part_in, tokens, gains, gain_attn,
+    out_m, out_d, late_grad,
+    normed, att, n2, prod, g, dy, late_own, late_part, late_halo, late_x, late_branch, late_gain, late_sem, *rest,
 ):
     m_refs, d_refs, lend_refs = rest[:9], rest[9:18], rest[18:22]
     m_sems, d_sems, lend_sems = rest[22:28], rest[28:34], rest[34:38]
@@ -828,7 +882,29 @@
     ladder_m = Ladder(m_refs + (out_m,), m_sems, outer, m_count)
     ladder_d = Ladder(d_refs + (out_d,), d_sems, outer, d_count)
     ladder_d.lend(lend_refs, lend_sems, section)
-    true = wide >= 0
+    has_left, has_right = wide > 0, wide < count - 1
+
+    late_loads = [
+        pltpu.make_async_copy(source, target, late_sem.at[index])
+        for index, (source, target) in enumerate((
+            (halo_part_in, late_part), (own_in, late_own), (tokens.at[batches - 1], late_x),
+            (db_in.at[batches - 1], late_branch)))]
+    late_copy = pltpu.make_async_remote_copy(
+        late_part, late_halo, late_sem.at[4], late_sem.at[5], device_id={"wide": wide - 1}, device_id_type=MESH)
+
+    def finish_late():
+        for copy in late_loads[1:]:
+            copy.wait()
+        pl.when(has_right)(lambda: late_copy.wait_recv())
+        for low in range(0, rows, BLOCK):
+            at = pl.ds(low, BLOCK)
+            scaled, inverse = rms_parts(late_x[at, :].astype(F32))
+            d_normed = late_own[at, :] + late_halo[at, :].astype(F32)
+            product = (d_normed * scaled).reshape(BLOCK // 8, 8, width)
+            late_gain[...] = late_gain[...] + jnp.sum(product, axis=0)
+            back = rms_back(d_normed * gain_attn[...], scaled, inverse)
+            late_grad[at, :] = (late_branch[at, :].astype(F32) + back).astype(BF16)
+
 
     loads = ((n2_in, n2), (att_in, att), (normed_in, normed), (prod_in, prod), (g_in, g))
 
@@ -852,15 +928,38 @@
 
     x_copy(0).start()
     each_load(jnp.int32(0), lambda copy: copy.start())
+
+    @pl.when(ladder_d.lender)
+    def _():
+        for copy in late_loads:
+            copy.start()
+
     for index in (3, 4, 1, 2):
         x_copy(index).start()
+    late_gain[...] = jnp.zeros(late_gain.shape, F32)
+
+    @pl.when(jnp.logical_not(has_right))
+    def _():
+        late_halo[...] = jnp.zeros(late_halo.shape, BF16)
+
     barrier = pltpu.get_barrier_semaphore()
     peers = [ladder_m.core_mate, ladder_m.side_mate] + [
         {"wide": lax.rem(ladder_m.depth + step, outer) * 4 + ladder_m.column} for step in range(1, outer)]
     for peer in peers:
         pl.semaphore_signal(barrier, inc=1, device_id=peer, device_id_type=MESH)
-    pl.semaphore_wait(barrier, len(peers) + ladder_d.lender.astype(jnp.int32))
+    for condition, step in ((has_left, -1), (has_right, 1)):
+        @pl.when(condition)
+        def _(step=step):
+            pl.semaphore_signal(barrier, inc=1, device_id={"wide": wide + step}, device_id_type=MESH)
+    greeted = len(peers) + has_left.astype(jnp.int32) + has_right.astype(jnp.int32)
+    pl.semaphore_wait(barrier, greeted + ladder_d.lender.astype(jnp.int32))
     pl.semaphore_signal(barrier, inc=1, device_id=ladder_d.partner, device_id_type=MESH)
+
+    @pl.when(ladder_d.lender)
+    def _():
+        late_loads[0].wait()
+        pl.when(has_left)(lambda: late_copy.start())
+
 
     kv_first = 2 * per_wide + 2 * per_narrow
     kv_last = kv_first + 2 * per_narrow
@@ -904,7 +1003,7 @@
 
         @pl.when(j == kv_last)
         def _():
-            first = jnp.sum(gains[0:8, :], axis=0, keepdims=True)
+            first = jnp.sum(gains[0:8, :] + late_gain[...], axis=0, keepdims=True)
             second = jnp.sum(gains[8:16, :], axis=0, keepdims=True)
             row = lax.broadcasted_iota(jnp.int32, (LANES, width), 0)
             placed = jnp.where(row == 0, first, jnp.where(row == 1, second, 0.0))
@@ -961,19 +1060,21 @@
         pl.when(j >= ladder_d.first)(lambda: ladder_d.stage_b(j))
 
     def step(s, carry):
+        pl.when(ladder_d.lender & (s == LATE))(finish_late)
         on_chunk(s, compute_m, own_d(compute_d))
         on_chunk(s, ladder_m.stage_a, own_d(ladder_d.stage_a))
-        on_chunk(s - LAG, ladder_m.stage_b, second)
-        on_chunk(s - 2 * LAG, ladder_m.stage_c, reduced_d(ladder_d.stage_c))
-        on_chunk(s - 3 * LAG, ladder_m.stage_d, reduced_d(ladder_d.stage_d))
+        on_chunk(s - LAG_PAIR, ladder_m.stage_b, second)
+        on_chunk(s - LAG_PAIR - LAG, ladder_m.stage_c, reduced_d(ladder_d.stage_c))
+        on_chunk(s - LAG_PAIR - 2 * LAG, ladder_m.stage_d, reduced_d(ladder_d.stage_d))
         return carry
 
-    lax.fori_loop(0, m_count + d_count + lent + 3 * LAG, step, 0)
+    lax.fori_loop(0, m_count + d_count + lent + LAG_PAIR + 2 * LAG, step, 0)
     ladder_m.drain()
     ladder_d.drain()
-
-
-def run_weights(normed, att, n2, prod, g, db, dg, du, dq, dk, dv, gains, count):
+    pl.when(ladder_d.lender & has_left)(lambda: late_copy.wait_send())
+
+
+def run_weights(normed, att, n2, prod, g, db, dg, du, dq, dk, dv, own, part, tokens, gains, gain_attn, count):
     batches, rows, width = g.shape
     hidden_width = prod.shape[2]
     outer = count // 4
@@ -1018,9 +1119,10 @@
         out_shape=[
             jax.ShapeDtypeStruct((m_count,) + block_m, F32),
             jax.ShapeDtypeStruct((d_count,) + block_d, F32),
+            jax.ShapeDtypeStruct(part.shape, BF16),
         ],
-        in_specs=[any_spec()] * 11 + [vmem_spec()],
-        out_specs=[vmem_spec()] * 2,
+        in_specs=[any_spec()] * 14 + [vmem_spec()] * 2,
+        out_specs=[vmem_spec()] * 3,
         scratch_shapes=[
             pltpu.VMEM(normed.shape, BF16),
             pltpu.VMEM(att.shape, BF16),
@@ -1028,6 +1130,10 @@
             pltpu.VMEM(prod.shape, BF16),
             pltpu.VMEM(g.shape, BF16),
             pltpu.VMEM((2, batches, 2 * rows, CHUNK), BF16),
+            pltpu.VMEM(own.shape, F32),
+        ] + [pltpu.VMEM(part.shape, BF16)] * 4 + [
+            pltpu.VMEM((8, width), F32),
+            pltpu.SemaphoreType.DMA((6,)),
         ] + m_refs + d_refs + lend_refs + m_sems + d_sems + lend_sems + [
             pltpu.SemaphoreType.DMA((5,)),
             pltpu.SemaphoreType.DMA((2,)),
@@ -1035,7 +1141,7 @@
         compiler_params=pltpu.CompilerParams(
             collective_id=3, has_side_effects=True, vmem_limit_bytes=VMEM_BYTES),
         name="weights",
-    )(normed, att, n2, prod, g, db, dg, du, dq, dk, dv, gains)
+    )(normed, att, n2, prod, g, db, dg, du, dq, dk, dv, own, part, tokens, gains, gain_attn)
 
 
 def summed_weights(normed, att, n2, prod, g, db, dg, du, dq, dk, dv, gains):
@@ -1055,7 +1161,7 @@
     )
 
 
-def arrange_kernel(sizes, block, grads, chunks_m, chunks_d, block_out, grad_out, *rest):
+def arrange_kernel(sizes, block, grads, late, chunks_m, chunks_d, block_out, grad_out, *rest):
     outs, (held_block, held_grads, held_m, held_d), (load_sem, store_sem) = rest[:9], rest[9:13], rest[13:]
     batches = block.shape[0]
     loads, stores = [], []
@@ -1073,8 +1179,14 @@
         stores.append((held_d.at[part], outs[6].at[0, :, pl.ds(part * LANES, LANES)]))
     loads = [pltpu.make_async_copy(*pair, load_sem.at[index]) for index, pair in enumerate(loads)]
     stores = [pltpu.make_async_copy(*pair, store_sem.at[index]) for index, pair in enumerate(stores)]
-    for copy in loads:
-        copy.start()
+    is_late = lax.axis_index("section") == 0
+    last = first_load - 1
+    late_load = pltpu.make_async_copy(late, held_grads.at[batches - 1], load_sem.at[last])
+    pl.when(is_late)(lambda: late_load.start())
+    pl.when(jnp.logical_not(is_late))(lambda: loads[last].start())
+    for index, copy in enumerate(loads):
+        if index != last:
+            copy.start()
     for index in range(first_load):
         loads[index].wait()
         stores[index].start()
@@ -1089,7 +1201,7 @@
         copy.wait()
 
 
-def arrange(block, grads, chunks_m, chunks_d, sizes):
+def arrange(block, grads, late, chunks_m, chunks_d, sizes):
     own, own_d = chunks_m.shape[1], chunks_d.shape[1]
     width, hidden_width = block.shape[2], CHUNK * sizes[0]
     shapes = [(1,) + block.shape] * 2
@@ -1101,24 +1213,13 @@
     return pl.pallas_call(
         functools.partial(arrange_kernel, sizes),
         out_shape=out_shape,
-        in_specs=[any_spec()] * 4,
+        in_specs=[any_spec()] * 5,
         out_specs=[any_spec()] * 9 + [vmem_spec()] * 2,
         scratch_shapes=[pltpu.VMEM(held.shape, held.dtype) for held in (block, grads, chunks_m, chunks_d)]
         + [pltpu.SemaphoreType.DMA((2 * block.shape[0] + 2,)), pltpu.SemaphoreType.DMA((copies,))],
         compiler_params=pltpu.CompilerParams(vmem_limit_bytes=VMEM_BYTES),
         name="arrange",
-    )(block, grads, chunks_m, chunks_d)
-
-
-def weight_grads(block_out, input_grads, normed, att, n2, prod, g, db, dg, du, dq, dk, dv, gains):
-    count = lax.axis_size("wide")
-    width, hidden_width = g.shape[2], prod.shape[2]
-    if count % 4 or width % (16 * count) or hidden_width % (16 * count):
-        grads = summed_weights(normed, att, n2, prod, g, db, dg, du, dq, dk, dv, gains)
-        return (block_out[None], input_grads[None], *grads)
-    out_m, out_d = run_weights(normed, att, n2, prod, g, db, dg, du, dq, dk, dv, gains, count)
-    sizes = (hidden_width // CHUNK,) * 2 + (width // CHUNK,) * 4
-    return tuple(arrange(block_out, input_grads, out_m, out_d, sizes))
+    )(block, grads, late, chunks_m, chunks_d)
 
 
 def per_device(
@@ -1126,9 +1227,16 @@
 ):
     weights = (w_query, w_key, w_value, w_output, w_gate, w_up, w_down)
     lengths = seg_lengths.reshape(seg_lengths.shape[0], -1)
-    (block_out, input_grads, normed, att, n2, prod, g, db, dg, du, dq, dk, dv, gains) = run_layers(
-        tokens, cotangent, lengths, weights, gain_attn, gain_mlp)
-    return weight_grads(block_out, input_grads, normed, att, n2, prod, g, db, dg, du, dq, dk, dv, gains)
+    count = lax.axis_size("wide")
+    width, hidden_width = w_gate.shape[1:]
+    whole_tiles = count % 4 == 0 and width % (16 * count) == 0 and hidden_width % (16 * count) == 0
+    block_out, input_grads, *saved, own, part, gains = run_layers(
+        tokens, cotangent, lengths, weights, gain_attn, gain_mlp, late=whole_tiles)
+    if not whole_tiles:
+        return (block_out[None], input_grads[None], *summed_weights(*saved, gains))
+    out_m, out_d, late = run_weights(*saved, own, part, tokens, gains, gain_attn, count)
+    sizes = (hidden_width // CHUNK,) * 2 + (width // CHUNK,) * 4
+    return tuple(arrange(block_out, input_grads, late, out_m, out_d, sizes))
 
 
 def solution(mesh):

time: 242 us -> 237 us (0.979)
  Pallas kernels: 241 us -> 236 us
    pallas_call x1, Pallas kernels: 94.7 us -> 92 us  [run_weights(): pl.pallas_call(weight_kernel, out_shape=[jax.ShapeDtypeStruct((m_count,)...]
where the time goes in v4:
time: 237 us
  Pallas kernels  236 us (100%)
    pallas_call x1, Pallas kernels, run_layers(): pl.pallas_call(functools.partial(layers_kernel, late), out_shape=[jax.Sha...  139 us
    pallas_call x1, Pallas kernels, run_weights(): pl.pallas_call(weight_kernel, out_shape=[jax.ShapeDtypeStruct((m_count,)...  92 us
    pallas_call x1, Pallas kernels, arrange(): pl.pallas_call(functools.partial(arrange_kernel, sizes), out_shape=out_sh...  5.44 us

profile of v4, /device:TPU:0, one launch (start us, length us, event | category | flops | bytes accessed | tf_op | source)
XLA Modules:
  0.0 236.8 jit_solution(9988793241277173596)
XLA Ops:
  0.6 138.5 %layers.1 = (bf16[4,256,768]{2,1,0:T(8,128)(2,1)}, bf16[4,256,768]{2,1,0:T(8,128)(2,1)}, bf16[4,512,768]{2,1,0:T(8,128)(2,1)}, bf16[4,256,768]{2,1,0:T(8,128)(2,...) custom-call(bf16[4,256,768]{2,1,0:T(8,128)(2,1)} %tokens.3, ...), custom_call_target="tpu_custom_call" | custom-call | tf_op jit(solution)/shard_map/layers/pallas_call | solution.py:672
  139.2 92.0 %weights.1 = (f32[29,48,256]{2,1,0:T(8,128)}, f32[6,128,128]{2,1,0:T(8,128)}, bf16[256,768]{1,0:T(8,128)(2,1)}) custom-call(bf16[4,512,768]{2,1,0:T(8,128)(2,1)} %get-tuple-element.32.normed_in, bf16[4,256,768]{2,1,0:T(8,128)(2,1)} %get-tuple-element.33.att_in, bf16[4,256,768]{2,1,0:T(8,128)(2,1)} %get-tuple-element.34.n2_in, ...), custom_call_target="tpu_custom_call" | custom-call | tf_op jit(solution)/shard_map/weights/pallas_call | solution.py:1117
  231.2 5.4 %arrange.1 = (bf16[1,4,256,768]{3,2,1,0:T(8,128)(2,1)}, bf16[1,4,256,768]{3,2,1,0:T(8,128)(2,1)}, f32[1,48,768]{2,1,0:T(8,128)}, f32[1,48,768]{2,1,0:T(8,128)}, ...) custom-call(bf16[4,256,768]{2,1,0:T(8,128)(2,1)} %get-tuple-element., ...), custom_call_target="tpu_custom_call" | custom-call | tf_op jit(solution)/shard_map/arrange/pallas_call | solution.py:1213

commit v5 on v4

--- a/solution.py
+++ b/solution.py
@@ -681,11 +681,13 @@
     )(tokens, cotangent, lengths, *weights, gain_attn, gain_mlp, trig)
 
 
-LAG = 3
-SENDS = 4
+LAG = 4
+SENDS = 6
 LAG_PAIR = 1
 LENT = 3
-MIX = 6
+MIX_LENDER = 5
+MIX_PARTNER = 4
+CROSS = 6
 LATE = 8
 CHUNK = 256
 
@@ -696,28 +698,108 @@
     )
 
 
-class Ladder:
-    def __init__(self, refs, sems, outer, chunks):
-        self.computed = chunks
-        self.dw, self.a_out, self.a_in, self.b_out, self.b_own, self.b_in, self.c_out, self.c_own, self.c_in, self.result = refs
-        self.a_send, self.a_recv, self.b_send, self.b_recv, self.c_send, self.c_recv = sems
+class Place:
+    def __init__(self, count):
         wide = lax.axis_index("wide")
-        self.outer = outer
+        self.outer = count // 4
         self.core, self.side, self.depth = lax.rem(wide, 2), lax.rem(wide // 2, 2), wide // 4
         self.core_mate = {"wide": wide + 1 - 2 * self.core}
         self.side_mate = {"wide": wide + 2 - 4 * self.side}
-        self.column = lax.rem(wide, 4)
-        self.first, self.count = 0, chunks
-        self.lent = None
-
-    def lend(self, refs, sems, section):
+        self.low, self.high = lax.rem(self.depth, 2), self.depth // 2
+        self.low_mate = {"wide": wide + 4 - 8 * self.low}
+        self.high_mate = {"wide": wide + 8 - 16 * self.high}
+
+
+class Pairs:
+    def __init__(self, place, refs, sems):
+        self.place = place
+        self.dw, self.out, self.arrived = refs
+        self.sent, self.received = sems
+
+    def copy(self, j):
+        slot = lax.rem(j, SENDS)
+        return pltpu.make_async_remote_copy(
+            self.out.at[slot], self.arrived.at[j], self.sent.at[slot], self.received.at[j],
+            device_id=self.place.core_mate, device_id_type=MESH)
+
+    def send(self, j):
+        slot, held = lax.rem(j, SENDS), lax.rem(j, LAG_PAIR + 1)
+
+        @pl.when(j >= SENDS)
+        def _():
+            self.copy(j - SENDS).wait_send()
+
+        for index in range(2 * self.place.outer):
+            self.out[slot, index] = self.dw[held, 2 * index + 1 - self.place.core].astype(BF16)
+        self.copy(j).start()
+
+    def total(self, j, index):
+        return self.dw[lax.rem(j, LAG_PAIR + 1), 2 * index + self.place.core] + self.arrived[j, index].astype(F32)
+
+    def drain(self, count):
+        for back in range(1, SENDS + 1):
+            self.copy(count - back).wait_send()
+
+
+class Halve:
+    def __init__(self, mate, bit, refs, sems, first=0):
+        self.mate, self.bit, self.first = mate, bit, first
+        self.out, self.own, self.arrived = refs
+        self.sent, self.received = sems
+
+    def copy(self, j):
+        slot = lax.rem(j, SENDS)
+        return pltpu.make_async_remote_copy(
+            self.out.at[slot], self.arrived.at[j], self.sent.at[slot], self.received.at[j],
+            device_id=self.mate, device_id_type=MESH)
+
+    def free(self, j):
+        @pl.when(j >= SENDS + self.first)
+        def _():
+            self.copy(j - SENDS).wait_send()
+
+    def split(self, j, part, place_of):
+        slot, held = lax.rem(j, SENDS), lax.rem(j, LAG + 1)
+        for k in range(self.out.shape[1]):
+            self.out[slot, k] = part(place_of(k, 1 - self.bit)).astype(BF16)
+            self.own[held, k] = part(place_of(k, self.bit)).astype(F32)
+
+    def take_from(self, j, earlier, place_of):
+        self.free(j)
+        earlier.copy(j).wait_recv()
+        self.split(j, lambda index: earlier.total(j, index), place_of)
+        self.copy(j).start()
+
+    def total(self, j, index):
+        return self.own[lax.rem(j, LAG + 1), index] + self.arrived[j, index].astype(F32)
+
+    def close(self, j):
+        self.copy(j).wait_recv()
+        return self.total(j, 0)
+
+    def drain(self, count):
+        for back in range(1, SENDS + 1):
+            j = count - back
+
+            @pl.when(j >= self.first)
+            def _(j=j):
+                self.copy(j).wait_send()
+
+
+def lowest(k, bit):
+    return 2 * k + bit
+
+
+class Lent:
+    def __init__(self, refs, sems, section, chunks):
         self.x_out, self.x_in, self.r_out, self.r_in = refs
         self.x_send, self.x_recv, self.r_send, self.r_recv = sems
         self.lender = section == 0
         self.lent = self.x_in.shape[0]
         self.partner = {"section": 1 - section}
         self.first = jnp.where(self.lender, self.lent, 0)
-        self.count = jnp.where(self.lender, self.computed, self.computed + self.lent)
+        self.computed = chunks
+        self.count = jnp.where(self.lender, chunks, chunks + self.lent)
 
     def x_copy(self, j):
         return pltpu.make_async_remote_copy(
@@ -729,138 +811,31 @@
             self.r_out.at[j], self.r_in.at[j], self.r_send.at[j], self.r_recv.at[j],
             device_id=self.partner, device_id_type=MESH)
 
-    def stage_x(self, j):
-        held = lax.rem(j, LAG + 1)
-
-        self.a_copy(j).wait_recv()
-        for index in range(2 * self.outer):
-            self.x_out[j, index] = (
-                self.dw[held, 2 * index + self.core] + self.a_in[j, index].astype(F32)).astype(BF16)
+    def give(self, j, pairs):
+        pairs.copy(j).wait_recv()
+        for index in range(self.x_out.shape[1]):
+            self.x_out[j, index] = pairs.total(j, index).astype(BF16)
         self.x_copy(j).start()
 
-    def a_copy(self, j):
-        slot = lax.rem(j, SENDS)
-        return pltpu.make_async_remote_copy(
-            self.a_out.at[slot], self.a_in.at[j], self.a_send.at[slot], self.a_recv.at[j],
-            device_id=self.core_mate, device_id_type=MESH)
-
-    def b_copy(self, j):
-        slot = lax.rem(j, SENDS)
-        return pltpu.make_async_remote_copy(
-            self.b_out.at[slot], self.b_in.at[j], self.b_send.at[slot], self.b_recv.at[j],
-            device_id=self.side_mate, device_id_type=MESH)
-
-    def c_copy(self, j, step, arriving):
-        slot = lax.rem(j, SENDS)
-        peer = lax.rem(self.depth + step, self.outer)
-        sender = peer if arriving else self.depth
-        return pltpu.make_async_remote_copy(
-            self.c_out.at[slot, peer], self.c_in.at[j, sender], self.c_send.at[slot, step], self.c_recv.at[j, sender],
-            device_id={"wide": peer * 4 + self.column}, device_id_type=MESH)
-
-    def stage_a(self, j):
-        slot, held = lax.rem(j, SENDS), lax.rem(j, LAG + 1)
-
-        @pl.when(j >= SENDS)
-        def _():
-            self.a_copy(j - SENDS).wait_send()
-
-        for index in range(2 * self.outer):
-            self.a_out[slot, index] = self.dw[held, 2 * index + 1 - self.core].astype(BF16)
-        self.a_copy(j).start()
-
-    def stage_b(self, j):
-        slot, held = lax.rem(j, SENDS), lax.rem(j, LAG + 1)
-
-        @pl.when(j >= SENDS + self.first)
-        def _():
-            self.b_copy(j - SENDS).wait_send()
-
-        def split():
-            self.a_copy(j).wait_recv()
-            for index in range(self.outer):
-                far, near = 2 * index + 1 - self.side, 2 * index + self.side
-                self.b_out[slot, index] = (
-                    self.dw[held, 2 * far + self.core] + self.a_in[j, far].astype(F32)).astype(BF16)
-                self.b_own[held, index] = self.dw[held, 2 * near + self.core] + self.a_in[j, near].astype(F32)
-
-        if self.lent is None:
-            split()
-        else:
-            pl.when(j < self.computed)(split)
-
-            @pl.when(j >= self.computed)
-            def _():
-                borrowed = j - self.computed
-                self.x_copy(borrowed).wait_recv()
-                for index in range(self.outer):
-                    self.b_out[slot, index] = self.x_in[borrowed, 2 * index + 1 - self.side]
-                    self.b_own[held, index] = self.x_in[borrowed, 2 * index + self.side].astype(F32)
-
-        self.b_copy(j).start()
-
-    def stage_c(self, j):
-        slot, held = lax.rem(j, SENDS), lax.rem(j, LAG + 1)
-
-        @pl.when(j >= SENDS + self.first)
-        def _():
-            for step in range(1, self.outer):
-                self.c_copy(j - SENDS, step, False).wait_send()
-
-        self.b_copy(j).wait_recv()
-        for index in range(self.outer):
-            self.c_out[slot, index] = (self.b_own[held, index] + self.b_in[j, index].astype(F32)).astype(BF16)
-        for step in range(1, self.outer):
-            self.c_copy(j, step, False).start()
-        self.c_own[held] = self.b_own[held, self.depth] + self.b_in[j, self.depth].astype(F32)
-
-    def stage_d(self, j):
-        held = lax.rem(j, LAG + 1)
-        total = self.c_own[held]
-        for step in range(1, self.outer):
-            self.c_copy(j, step, True).wait_recv()
-        for step in range(1, self.outer):
-            total = total + self.c_in[j, lax.rem(self.depth + step, self.outer)].astype(F32)
-        if self.lent is None:
-            self.result[j] = total
-            return
-
-        @pl.when(j < self.computed)
-        def _():
-            self.result[j] = total
-
-        @pl.when(j >= self.computed)
-        def _():
-            @pl.when(j == self.computed)
-            def _():
-                pl.semaphore_wait(pltpu.get_barrier_semaphore(), 1)
-
-            self.r_out[j - self.computed] = total
-            self.r_copy(j - self.computed).start()
-
-    def drain(self):
-        for back in range(1, SENDS + 1):
-            self.a_copy(self.computed - back).wait_send()
-            j = self.count - back
-
-            @pl.when(j >= self.first)
-            def _(j=j):
-                self.b_copy(j).wait_send()
-                for step in range(1, self.outer):
-                    self.c_copy(j, step, False).wait_send()
-
-        if self.lent is not None:
-            @pl.when(self.lender)
-            def _():
-                for j in range(self.lent):
-                    self.x_copy(j).wait_send()
-                    self.r_copy(j).wait_recv()
-                    self.result[j] = self.r_in[j]
-
-            @pl.when(jnp.logical_not(self.lender))
-            def _():
-                for j in range(self.lent):
-                    self.r_copy(j).wait_send()
+    def give_back(self, j):
+        @pl.when(j == self.computed)
+        def _():
+            pl.semaphore_wait(pltpu.get_barrier_semaphore(), 1)
+
+        self.r_copy(j - self.computed).start()
+
+    def drain(self, result):
+        @pl.when(self.lender)
+        def _():
+            for j in range(self.lent):
+                self.x_copy(j).wait_send()
+                self.r_copy(j).wait_recv()
+                result[j] = self.r_in[j]
+
+        @pl.when(jnp.logical_not(self.lender))
+        def _():
+            for j in range(self.lent):
+                self.r_copy(j).wait_send()
 
 
 def weight_kernel(
@@ -869,19 +844,28 @@
     out_m, out_d, late_grad,
     normed, att, n2, prod, g, dy, late_own, late_part, late_halo, late_x, late_branch, late_gain, late_sem, *rest,
 ):
-    m_refs, d_refs, lend_refs = rest[:9], rest[9:18], rest[18:22]
-    m_sems, d_sems, lend_sems = rest[22:28], rest[28:34], rest[34:38]
-    x_sem, dy_sem = rest[38], rest[39]
+    rest = list(rest)
+
+    def take(number):
+        taken, rest[:number] = rest[:number], []
+        return taken
+
     section, wide, count = lax.axis_index("section"), lax.axis_index("wide"), lax.axis_size("wide")
     batches, rows, width = g_in.shape
     hidden_width = prod_in.shape[2]
-    outer = count // 4
     own = pl.ds(rows, rows)
     m_count, d_count = out_m.shape[0], out_d.shape[0]
     per_wide, per_narrow = hidden_width // CHUNK, width // CHUNK
-    ladder_m = Ladder(m_refs + (out_m,), m_sems, outer, m_count)
-    ladder_d = Ladder(d_refs + (out_d,), d_sems, outer, d_count)
-    ladder_d.lend(lend_refs, lend_sems, section)
+    place = Place(count)
+    lent = Lent(take(4), take(4), section, d_count)
+    pairs_m, pairs_d = Pairs(place, take(3), take(2)), Pairs(place, take(3), take(2))
+    mates = ((place.side_mate, place.side), (place.low_mate, place.low), (place.high_mate, place.high))
+    side_m, low_m, high_m = [Halve(*mate, take(3), take(2)) for mate in mates]
+    side_d, low_d, high_d = [Halve(*mate, take(3), take(2), lent.first) for mate in mates]
+    low_z, high_z, side_z = [Halve(*mates[index], take(3), take(2)) for index in (1, 2, 0)]
+    x_sem, dy_sem = take(2)
+    z_count = m_count // CROSS
+    y_count = m_count - z_count
     has_left, has_right = wide > 0, wide < count - 1
 
     late_loads = [
@@ -929,7 +913,7 @@
     x_copy(0).start()
     each_load(jnp.int32(0), lambda copy: copy.start())
 
-    @pl.when(ladder_d.lender)
+    @pl.when(lent.lender)
     def _():
         for copy in late_loads:
             copy.start()
@@ -943,8 +927,7 @@
         late_halo[...] = jnp.zeros(late_halo.shape, BF16)
 
     barrier = pltpu.get_barrier_semaphore()
-    peers = [ladder_m.core_mate, ladder_m.side_mate] + [
-        {"wide": lax.rem(ladder_m.depth + step, outer) * 4 + ladder_m.column} for step in range(1, outer)]
+    peers = [place.core_mate, place.side_mate, place.low_mate, place.high_mate]
     for peer in peers:
         pl.semaphore_signal(barrier, inc=1, device_id=peer, device_id_type=MESH)
     for condition, step in ((has_left, -1), (has_right, 1)):
@@ -952,10 +935,10 @@
         def _(step=step):
             pl.semaphore_signal(barrier, inc=1, device_id={"wide": wide + step}, device_id_type=MESH)
     greeted = len(peers) + has_left.astype(jnp.int32) + has_right.astype(jnp.int32)
-    pl.semaphore_wait(barrier, greeted + ladder_d.lender.astype(jnp.int32))
-    pl.semaphore_signal(barrier, inc=1, device_id=ladder_d.partner, device_id_type=MESH)
-
-    @pl.when(ladder_d.lender)
+    pl.semaphore_wait(barrier, greeted + lent.lender.astype(jnp.int32))
+    pl.semaphore_signal(barrier, inc=1, device_id=lent.partner, device_id_type=MESH)
+
+    @pl.when(lent.lender)
     def _():
         late_loads[0].wait()
         pl.when(has_left)(lambda: late_copy.start())
@@ -966,7 +949,7 @@
     narrow_first = 2 * per_wide
 
     def compute_m(j):
-        slot, held = lax.rem(j, 2), lax.rem(j, LAG + 1)
+        slot, held = lax.rem(j, 2), lax.rem(j, LAG_PAIR + 1)
 
         @pl.when(j + 1 < kv_last)
         def _():
@@ -974,7 +957,7 @@
 
         def write(left, right):
             product = dot_tn(left.reshape(-1, width), right.reshape(-1, CHUNK))
-            ladder_m.dw[held] = product.reshape(ladder_m.dw.shape[1:])
+            pairs_m.dw[held] = product.reshape(pairs_m.dw.shape[1:])
 
         @pl.when(j < kv_last)
         def _():
@@ -1008,10 +991,10 @@
             row = lax.broadcasted_iota(jnp.int32, (LANES, width), 0)
             placed = jnp.where(row == 0, first, jnp.where(row == 1, second, 0.0))
             columns = placed.T
-            ladder_m.dw[held] = jnp.concatenate([columns, columns], axis=1).reshape(ladder_m.dw.shape[1:])
+            pairs_m.dw[held] = jnp.concatenate([columns, columns], axis=1).reshape(pairs_m.dw.shape[1:])
 
     def compute_d(j):
-        held = lax.rem(j, LAG + 1)
+        held = lax.rem(j, LAG_PAIR + 1)
 
         @pl.when(j == 0)
         def _():
@@ -1020,22 +1003,17 @@
 
         lanes = pl.ds(pl.multiple_of(j * LANES, LANES), LANES)
         product = dot_tn(prod[...].reshape(-1, hidden_width), g[:, :, lanes].reshape(-1, LANES))
-        ladder_d.dw[held] = product.reshape(ladder_d.dw.shape[1:])
-
-    lent = ladder_d.lent
-    lender = ladder_d.lender
+        pairs_d.dw[held] = product.reshape(pairs_d.dw.shape[1:])
 
     def on_chunk(s, act_m, act_d):
-        mixed = s < MIX * lent
-        turn, place = s // MIX, lax.rem(s, MIX)
-        j_lender = jnp.where(mixed, (MIX - 1) * turn + place, s - lent)
-        d_lender = jnp.where(mixed, turn, s - m_count)
-        m_turn = jnp.where(lender & mixed, place < MIX - 1, True)
-        j_m = jnp.where(lender, j_lender, s)
-        j_d = jnp.where(lender, d_lender, s - m_count)
-        last_d = ladder_d.count
-        is_m = (s >= 0) & (j_m < m_count) & m_turn
-        is_d = (s >= 0) & jnp.where(lender & mixed, place == MIX - 1, j_m >= m_count) & (j_d < last_d)
+        period = jnp.where(lent.lender, MIX_LENDER, MIX_PARTNER)
+        turn = jnp.where(lent.lender, s // MIX_LENDER, s // MIX_PARTNER)
+        spot = s - period * turn
+        mixed = turn < lent.count
+        j_m = jnp.where(mixed, (period - 1) * turn + spot, s - lent.count)
+        j_d = turn
+        is_d = (s >= 0) & mixed & (spot == period - 1)
+        is_m = (s >= 0) & (j_m < m_count) & jnp.logical_not(is_d)
 
         @pl.when(is_m)
         def _():
@@ -1045,75 +1023,142 @@
         def _():
             act_d(j_d)
 
-    def own_d(act):
-        def guarded(j):
-            pl.when(j < d_count)(lambda: act(j))
-        return guarded
-
-    def reduced_d(act):
-        def guarded(j):
-            pl.when(j >= ladder_d.first)(lambda: act(j))
-        return guarded
-
-    def second(j):
-        pl.when(j < ladder_d.first)(lambda: ladder_d.stage_x(j))
-        pl.when(j >= ladder_d.first)(lambda: ladder_d.stage_b(j))
+    def either(act_y, act_z):
+        def act(j):
+            crossing = lax.rem(j, CROSS) == CROSS - 1
+            pl.when(jnp.logical_not(crossing))(lambda: act_y(j, j - j // CROSS))
+            pl.when(crossing)(lambda: act_z(j, j // CROSS))
+        return act
+
+    def nothing(*_):
+        pass
+
+    def below(limit, act):
+        return lambda j: pl.when(j < limit)(lambda: act(j))
+
+    def reduced(act):
+        return lambda j: pl.when(j >= lent.first)(lambda: act(j))
+
+    def open_y(j, c):
+        side_m.free(c)
+        pairs_m.copy(j).wait_recv()
+        side_m.split(c, lambda index: pairs_m.total(j, index), lowest)
+        side_m.copy(c).start()
+
+    def open_z(j, z):
+        low_z.free(z)
+        pairs_m.copy(j).wait_recv()
+        low_z.split(z, lambda index: pairs_m.total(j, index), lambda k, bit: ((k // 2) * 2 + bit) * 2 + k % 2)
+        low_z.copy(z).start()
+
+    def open_d(j):
+        pl.when(j < lent.first)(lambda: lent.give(j, pairs_d))
+
+        @pl.when(j >= lent.first)
+        def _():
+            side_d.free(j)
+
+            @pl.when(j < d_count)
+            def _():
+                pairs_d.copy(j).wait_recv()
+                side_d.split(j, lambda index: pairs_d.total(j, index), lowest)
+
+            @pl.when(j >= d_count)
+            def _():
+                lent.x_copy(j - d_count).wait_recv()
+                side_d.split(j, lambda index: lent.x_in[j - d_count, index], lowest)
+
+            side_d.copy(j).start()
+
+    def close_y(j, c):
+        out_m[j] = high_m.close(c)
+
+    def close_z(j, z):
+        out_m[j] = side_z.close(z)
+
+    def close_d(j):
+        total = high_d.close(j)
+
+        @pl.when(j < d_count)
+        def _():
+            out_d[j] = total
+
+        @pl.when(j >= d_count)
+        def _():
+            lent.r_out[j - d_count] = total
+            lent.give_back(j)
 
     def step(s, carry):
-        pl.when(ladder_d.lender & (s == LATE))(finish_late)
-        on_chunk(s, compute_m, own_d(compute_d))
-        on_chunk(s, ladder_m.stage_a, own_d(ladder_d.stage_a))
-        on_chunk(s - LAG_PAIR, ladder_m.stage_b, second)
-        on_chunk(s - LAG_PAIR - LAG, ladder_m.stage_c, reduced_d(ladder_d.stage_c))
-        on_chunk(s - LAG_PAIR - 2 * LAG, ladder_m.stage_d, reduced_d(ladder_d.stage_d))
+        pl.when(lent.lender & (s == LATE))(finish_late)
+        on_chunk(s, compute_m, below(d_count, compute_d))
+        on_chunk(s, pairs_m.send, below(d_count, pairs_d.send))
+        on_chunk(s - LAG_PAIR, either(open_y, open_z), open_d)
+        on_chunk(
+            s - LAG_PAIR - LAG,
+            either(lambda j, c: low_m.take_from(c, side_m, lowest),
+                   lambda j, z: high_z.take_from(z, low_z, lambda k, bit: 2 * bit + k)),
+            reduced(lambda j: low_d.take_from(j, side_d, lowest)))
+        on_chunk(
+            s - LAG_PAIR - 2 * LAG,
+            either(lambda j, c: high_m.take_from(c, low_m, lowest),
+                   lambda j, z: side_z.take_from(z, high_z, lowest)),
+            reduced(lambda j: high_d.take_from(j, low_d, lowest)))
+        on_chunk(s - LAG_PAIR - 3 * LAG, either(close_y, close_z), reduced(close_d))
         return carry
 
-    lax.fori_loop(0, m_count + d_count + lent + LAG_PAIR + 2 * LAG, step, 0)
-    ladder_m.drain()
-    ladder_d.drain()
-    pl.when(ladder_d.lender & has_left)(lambda: late_copy.wait_send())
+    total = d_count + lent.lent
+    steps = max(m_count + total, MIX_PARTNER * total, MIX_LENDER * d_count)
+    lax.fori_loop(0, steps + LAG_PAIR + 3 * LAG, step, 0)
+    pairs_m.drain(m_count)
+    pairs_d.drain(d_count)
+    for stage in (side_m, low_m, high_m):
+        stage.drain(y_count)
+    for stage in (side_d, low_d, high_d):
+        stage.drain(lent.count)
+    for stage in (low_z, high_z, side_z):
+        stage.drain(z_count)
+    lent.drain(out_d)
+    pl.when(lent.lender & has_left)(lambda: late_copy.wait_send())
 
 
 def run_weights(normed, att, n2, prod, g, db, dg, du, dq, dk, dv, own, part, tokens, gains, gain_attn, count):
     batches, rows, width = g.shape
     hidden_width = prod.shape[2]
-    outer = count // 4
     m_count = 2 * (hidden_width // CHUNK) + 4 * (width // CHUNK) + 1
     d_count = width // LANES
 
-    def ladder(chunks, lent, block):
-        total = chunks + lent
-        refs = [
-            pltpu.VMEM((LAG + 1, count) + block, F32),
+    dma = pltpu.SemaphoreType.DMA
+    block_m, block_d = (width // count, CHUNK), (hidden_width // count, LANES)
+    z_count = m_count // CROSS
+    y_count = m_count - z_count
+
+    def pairs(chunks, block):
+        return [
+            pltpu.VMEM((LAG_PAIR + 1, count) + block, F32),
             pltpu.VMEM((SENDS, count // 2) + block, BF16),
             pltpu.VMEM((chunks, count // 2) + block, BF16),
-            pltpu.VMEM((SENDS, outer) + block, BF16),
-            pltpu.VMEM((LAG + 1, outer) + block, F32),
-            pltpu.VMEM((total, outer) + block, BF16),
-            pltpu.VMEM((SENDS, outer) + block, BF16),
-            pltpu.VMEM((LAG + 1,) + block, F32),
-            pltpu.VMEM((total, outer) + block, BF16),
+            dma((SENDS,)), dma((chunks,)),
         ]
-        sems = [
-            pltpu.SemaphoreType.DMA((SENDS,)),
-            pltpu.SemaphoreType.DMA((chunks,)),
-            pltpu.SemaphoreType.DMA((SENDS,)),
-            pltpu.SemaphoreType.DMA((total,)),
-            pltpu.SemaphoreType.DMA((SENDS, outer)),
-            pltpu.SemaphoreType.DMA((total, outer)),
-        ]
-        return refs, sems
-
-    block_m, block_d = (width // count, CHUNK), (hidden_width // count, LANES)
-    m_refs, m_sems = ladder(m_count, 0, block_m)
-    d_refs, d_sems = ladder(d_count, LENT, block_d)
-    lend_refs = [
+
+    def halves(chunks, block):
+        refs = []
+        for blocks in (count // 4, count // 8, count // 16):
+            refs += [
+                pltpu.VMEM((SENDS, blocks) + block, BF16),
+                pltpu.VMEM((LAG + 1, blocks) + block, F32),
+                pltpu.VMEM((chunks, blocks) + block, BF16),
+                dma((SENDS,)), dma((chunks,)),
+            ]
+        return refs
+
+    ladders = [
         pltpu.VMEM((LENT, count // 2) + block_d, BF16),
         pltpu.VMEM((LENT, count // 2) + block_d, BF16),
         pltpu.VMEM((LENT,) + block_d, F32),
         pltpu.VMEM((LENT,) + block_d, F32),
-    ]
-    lend_sems = [pltpu.SemaphoreType.DMA((size,)) for size in (LENT,) * 4]
+    ] + [dma((LENT,))] * 4
+    ladders += pairs(m_count, block_m) + pairs(d_count, block_d)
+    ladders += halves(y_count, block_m) + halves(d_count + LENT, block_d) + halves(z_count, block_m)
     return pl.pallas_call(
         weight_kernel,
         out_shape=[
@@ -1134,7 +1179,7 @@
         ] + [pltpu.VMEM(part.shape, BF16)] * 4 + [
             pltpu.VMEM((8, width), F32),
             pltpu.SemaphoreType.DMA((6,)),
-        ] + m_refs + d_refs + lend_refs + m_sems + d_sems + lend_sems + [
+        ] + ladders + [
             pltpu.SemaphoreType.DMA((5,)),
             pltpu.SemaphoreType.DMA((2,)),
         ],
@@ -1229,7 +1274,7 @@
     lengths = seg_lengths.reshape(seg_lengths.shape[0], -1)
     count = lax.axis_size("wide")
     width, hidden_width = w_gate.shape[1:]
-    whole_tiles = count % 4 == 0 and width % (16 * count) == 0 and hidden_width % (16 * count) == 0
+    whole_tiles = count == 16 and width % (16 * count) == 0 and hidden_width % (16 * count) == 0
     block_out, input_grads, *saved, own, part, gains = run_layers(
         tokens, cotangent, lengths, weights, gain_attn, gain_mlp, late=whole_tiles)
     if not whole_tiles:

time: 237 us -> 233 us (0.983)
  Pallas kernels: 236 us -> 232 us
    pallas_call x1, Pallas kernels: 92 us -> 87.9 us  [run_weights(): pl.pallas_call(weight_kernel, out_shape=[jax.ShapeDtypeStruct((m_count,)...]
where the time goes in v5:
time: 233 us
  Pallas kernels  232 us (100%)
    pallas_call x1, Pallas kernels, run_layers(): pl.pallas_call(functools.partial(layers_kernel, late), out_shape=[jax.Sha...  139 us
    pallas_call x1, Pallas kernels, run_weights(): pl.pallas_call(weight_kernel, out_shape=[jax.ShapeDtypeStruct((m_count,)...  87.9 us
    pallas_call x1, Pallas kernels, arrange(): pl.pallas_call(functools.partial(arrange_kernel, sizes), out_shape=out_sh...  5.44 us

profile of v5, /device:TPU:0, one launch (start us, length us, event | category | flops | bytes accessed | tf_op | source)
XLA Modules:
  0.0 232.7 jit_solution(9220241546456740783)
XLA Ops:
  0.6 138.5 %layers.1 = (bf16[4,256,768]{2,1,0:T(8,128)(2,1)}, bf16[4,256,768]{2,1,0:T(8,128)(2,1)}, bf16[4,512,768]{2,1,0:T(8,128)(2,1)}, bf16[4,256,768]{2,1,0:T(8,128)(2,...) custom-call(bf16[4,256,768]{2,1,0:T(8,128)(2,1)} %tokens.3, ...), custom_call_target="tpu_custom_call" | custom-call | tf_op jit(solution)/shard_map/layers/pallas_call | solution.py:672
  139.2 87.9 %weights.1 = (f32[29,48,256]{2,1,0:T(8,128)}, f32[6,128,128]{2,1,0:T(8,128)}, bf16[256,768]{1,0:T(8,128)(2,1)}) custom-call(bf16[4,512,768]{2,1,0:T(8,128)(2,1)} %get-tuple-element.32.normed_in, bf16[4,256,768]{2,1,0:T(8,128)(2,1)} %get-tuple-element.33.att_in, bf16[4,256,768]{2,1,0:T(8,128)(2,1)} %get-tuple-element.34.n2_in, ...), custom_call_target="tpu_custom_call" | custom-call | tf_op jit(solution)/shard_map/weights/pallas_call | solution.py:1162
  227.1 5.4 %arrange.1 = (bf16[1,4,256,768]{3,2,1,0:T(8,128)(2,1)}, bf16[1,4,256,768]{3,2,1,0:T(8,128)(2,1)}, f32[1,48,768]{2,1,0:T(8,128)}, f32[1,48,768]{2,1,0:T(8,128)}, ...) custom-call(bf16[4,256,768]{2,1,0:T(8,128)(2,1)} %get-tuple-element., ...), custom_call_target="tpu_custom_call" | custom-call | tf_op jit(solution)/shard_map/arrange/pallas_call | solution.py:1258

commit v6 on v5

--- a/solution.py
+++ b/solution.py
@@ -934,15 +934,6 @@
         @pl.when(condition)
         def _(step=step):
             pl.semaphore_signal(barrier, inc=1, device_id={"wide": wide + step}, device_id_type=MESH)
-    greeted = len(peers) + has_left.astype(jnp.int32) + has_right.astype(jnp.int32)
-    pl.semaphore_wait(barrier, greeted + lent.lender.astype(jnp.int32))
-    pl.semaphore_signal(barrier, inc=1, device_id=lent.partner, device_id_type=MESH)
-
-    @pl.when(lent.lender)
-    def _():
-        late_loads[0].wait()
-        pl.when(has_left)(lambda: late_copy.start())
-
 
     kv_first = 2 * per_wide + 2 * per_narrow
     kv_last = kv_first + 2 * per_narrow
@@ -1004,6 +995,17 @@
         lanes = pl.ds(pl.multiple_of(j * LANES, LANES), LANES)
         product = dot_tn(prod[...].reshape(-1, hidden_width), g[:, :, lanes].reshape(-1, LANES))
         pairs_d.dw[held] = product.reshape(pairs_d.dw.shape[1:])
+
+    compute_m(jnp.int32(0))
+    greeted = len(peers) + has_left.astype(jnp.int32) + has_right.astype(jnp.int32)
+    pl.semaphore_wait(barrier, greeted + lent.lender.astype(jnp.int32))
+    pl.semaphore_signal(barrier, inc=1, device_id=lent.partner, device_id_type=MESH)
+
+    @pl.when(lent.lender)
+    def _():
+        late_loads[0].wait()
+        pl.when(has_left)(lambda: late_copy.start())
+
 
     def on_chunk(s, act_m, act_d):
         period = jnp.where(lent.lender, MIX_LENDER, MIX_PARTNER)
@@ -1090,7 +1092,7 @@
 
     def step(s, carry):
         pl.when(lent.lender & (s == LATE))(finish_late)
-        on_chunk(s, compute_m, below(d_count, compute_d))
+        on_chunk(jnp.where(s == 0, -1, s), compute_m, below(d_count, compute_d))
         on_chunk(s, pairs_m.send, below(d_count, pairs_d.send))
         on_chunk(s - LAG_PAIR, either(open_y, open_z), open_d)
         on_chunk(
@@ -1214,7 +1216,8 @@
         loads += [(block.at[mb], held_block.at[mb]), (grads.at[mb], held_grads.at[mb])]
         stores += [(held_block.at[mb], block_out.at[0, mb]), (held_grads.at[mb], grad_out.at[0, mb])]
     first_load = len(loads)
-    loads += [(chunks_m, held_m), (chunks_d, held_d)]
+    groups = [pl.ds(base, min(8, chunks_m.shape[0] - base)) for base in range(0, chunks_m.shape[0], 8)]
+    loads += [(chunks_m.at[group], held_m.at[group]) for group in groups] + [(chunks_d, held_d)]
     base = 0
     for size, index in zip(sizes, (4, 5, 3, 0, 1, 2)):
         for part in range(size):
@@ -1229,16 +1232,16 @@
     late_load = pltpu.make_async_copy(late, held_grads.at[batches - 1], load_sem.at[last])
     pl.when(is_late)(lambda: late_load.start())
     pl.when(jnp.logical_not(is_late))(lambda: loads[last].start())
-    for index, copy in enumerate(loads):
+    for index, copy in reversed(list(enumerate(loads))):
         if index != last:
             copy.start()
-    for index in range(first_load):
-        loads[index].wait()
-        stores[index].start()
     for copy in loads[first_load:]:
         copy.wait()
     for copy in stores[first_load:]:
         copy.start()
+    for index in range(first_load):
+        loads[index].wait()
+        stores[index].start()
     turned = held_m[base, :, :LANES].T
     outs[7][...] = turned[0:1, :]
     outs[8][...] = turned[1:2, :]
@@ -1261,7 +1264,7 @@
         in_specs=[any_spec()] * 5,
         out_specs=[any_spec()] * 9 + [vmem_spec()] * 2,
         scratch_shapes=[pltpu.VMEM(held.shape, held.dtype) for held in (block, grads, chunks_m, chunks_d)]
-        + [pltpu.SemaphoreType.DMA((2 * block.shape[0] + 2,)), pltpu.SemaphoreType.DMA((copies,))],
+        + [pltpu.SemaphoreType.DMA((2 * block.shape[0] + pl.cdiv(chunks_m.shape[0], 8) + 1,)), pltpu.SemaphoreType.DMA((copies,))],
         compiler_params=pltpu.CompilerParams(vmem_limit_bytes=VMEM_BYTES),
         name="arrange",
     )(block, grads, late, chunks_m, chunks_d)

time: 233 us -> 233 us (level)
  no operation moved by 1% of the time
where the time goes in v6:
time: 233 us; the launch traced here: 232 us
  Pallas kernels  231 us (99%)
    pallas_call x1, Pallas kernels, run_layers(): pl.pallas_call(functools.partial(layers_kernel, late), out_shape=[jax.Sha...  139 us
    pallas_call x1, Pallas kernels, run_weights(): pl.pallas_call(weight_kernel, out_shape=[jax.ShapeDtypeStruct((m_count,)...  87.9 us
    pallas_call x1, Pallas kernels, arrange(): pl.pallas_call(functools.partial(arrange_kernel, sizes), out_shape=out_sh...  5.09 us

profile of v6, /device:TPU:0, one launch (start us, length us, event | category | flops | bytes accessed | tf_op | source)
XLA Modules:
  0.0 232.3 jit_solution(14183413923862892224)
XLA Ops:
  0.6 138.5 %layers.1 = (bf16[4,256,768]{2,1,0:T(8,128)(2,1)}, bf16[4,256,768]{2,1,0:T(8,128)(2,1)}, bf16[4,512,768]{2,1,0:T(8,128)(2,1)}, bf16[4,256,768]{2,1,0:T(8,128)(2,...) custom-call(bf16[4,256,768]{2,1,0:T(8,128)(2,1)} %tokens.3, ...), custom_call_target="tpu_custom_call" | custom-call | tf_op jit(solution)/shard_map/layers/pallas_call | solution.py:672
  139.2 87.9 %weights.1 = (f32[29,48,256]{2,1,0:T(8,128)}, f32[6,128,128]{2,1,0:T(8,128)}, bf16[256,768]{1,0:T(8,128)(2,1)}) custom-call(bf16[4,512,768]{2,1,0:T(8,128)(2,1)} %get-tuple-element.32.normed_in, bf16[4,256,768]{2,1,0:T(8,128)(2,1)} %get-tuple-element.33.att_in, bf16[4,256,768]{2,1,0:T(8,128)(2,1)} %get-tuple-element.34.n2_in, ...), custom_call_target="tpu_custom_call" | custom-call | tf_op jit(solution)/shard_map/weights/pallas_call | solution.py:1164
  227.1 5.1 %arrange.1 = (bf16[1,4,256,768]{3,2,1,0:T(8,128)(2,1)}, bf16[1,4,256,768]{3,2,1,0:T(8,128)(2,1)}, f32[1,48,768]{2,1,0:T(8,128)}, f32[1,48,768]{2,1,0:T(8,128)}, ...) custom-call(bf16[4,256,768]{2,1,0:T(8,128)(2,1)} %get-tuple-element., ...), custom_call_target="tpu_custom_call" | custom-call | tf_op jit(solution)/shard_map/arrange/pallas_call | solution.py:1261
